TPU v7x, 32 devices: a whole 2x2x4 slice. The times are simulated.
32 devices in a mesh: dp: 4 (over y, x), mp: 8 (over z, core).
Axes of the slice: x: 2, y: 2, z: 4, core: 2. Of those that a mesh axis runs over, the one named last changes fastest.
Arguments:
- text_states: bfloat16 [8, 2048, 2048], P('dp', 'mp'), may hold values from -6 to 6
- image_states: bfloat16 [8, 384, 2048], P('dp'), may hold values from -6 to 6
- image_offsets: int32 [8, 6], P('dp'), may hold values from 0 to 1984, as said below
- image_counts: int32 [8], P('dp'), may hold values from 0 to 6, as said below
- output_grad: bfloat16 [8, 2048, 2048], P('dp', 'mp'), may hold values from -6 to 6
- head_master: float32 [3, 2048, 2048], P(None, 'dp', 'mp'), may hold values from -0.1502602 to 0.1502602
- head_moment: float32 [3, 2048, 2048], P(None, 'dp', 'mp'), may hold values from -80 to 80
- head_square: float32 [3, 2048, 2048], P(None, 'dp', 'mp'), may hold values from 16.384 to 262.144
- outward_master: float32 [2048, 2048], P('dp'), may hold values from -0.1502602 to 0.1502602
- outward_moment: float32 [2048, 2048], P('dp'), may hold values from -80 to 80
- outward_square: float32 [2048, 2048], P('dp'), may hold values from 8.192 to 131.072
- upward_master: float32 [2048, 8192], P('dp', 'mp'), may hold values from -0.1502602 to 0.1502602
- upward_moment: float32 [2048, 8192], P('dp', 'mp'), may hold values from -80 to 80
- upward_square: float32 [2048, 8192], P('dp', 'mp'), may hold values from 8.192 to 131.072
- downward_master: float32 [8192, 2048], P('mp', 'dp'), may hold values from -0.0751301 to 0.0751301
- downward_moment: float32 [8192, 2048], P('mp', 'dp'), may hold values from -80 to 80
- downward_square: float32 [8192, 2048], P('mp', 'dp'), may hold values from 8.192 to 131.072
- gains_master: float32 [14336], replicated, may hold values from 0.525 to 1.925
- gains_moment: float32 [14336], replicated, may hold values from -80 to 80
- gains_square: float32 [14336], replicated, may hold values from 8.192 to 131.072
Outputs:
- layer_output: bfloat16 [8, 2048, 2048], P('dp', 'mp')
- input_grad: float32 [8, 2048, 2048], P('dp', 'mp')
- moment_head: float32 [3, 2048, 2048], P(None, 'dp', 'mp')
- square_head: float32 [3, 2048, 2048], P(None, 'dp', 'mp')
- updated_head: float32 [3, 2048, 2048], P(None, 'dp', 'mp')
- copied_head: bfloat16 [3, 2048, 2048], P(None, 'dp', 'mp')
- moment_outward: float32 [2048, 2048], P('dp')
- square_outward: float32 [2048, 2048], P('dp')
- updated_outward: float32 [2048, 2048], P('dp')
- copied_outward: bfloat16 [2048, 2048], P('dp')
- moment_upward: float32 [2048, 8192], P('dp', 'mp')
- square_upward: float32 [2048, 8192], P('dp', 'mp')
- updated_upward: float32 [2048, 8192], P('dp', 'mp')
- copied_upward: bfloat16 [2048, 8192], P('dp', 'mp')
- moment_downward: float32 [8192, 2048], P('mp', 'dp')
- square_downward: float32 [8192, 2048], P('mp', 'dp')
- updated_downward: float32 [8192, 2048], P('mp', 'dp')
- copied_downward: bfloat16 [8192, 2048], P('mp', 'dp')
- moment_gains: float32 [14336], replicated
- square_gains: float32 [14336], replicated
- updated_gains: float32 [14336], replicated
- update_norms: float32 [10, 2], replicated
Inputs may be any that keep to these rules, and one draw needn't show every extreme that they name: `image_counts`: images in a sequence; in every draw some sequence holds 6 images and some holds none. `image_offsets`: start position of each image in its sequence; images lie inside the sequence in increasing order, each 64 positions long, none intersecting; entries at or after a sequence's count are ignored.
All inputs are finite; a program needn't handle non-finite values.
Results may differ from a plain program's by a relative error of at most 0.02.
Values may be sent and summed in bfloat16 or wider, within the bound.
A program may use at most 384 MiB of HBM per device.

v0:
```python
from functools import partial

import jax
import jax.numpy as jnp
from jax import lax
from jax.sharding import PartitionSpec as P

HEAD_DIM = 64
FF = 8192
PATCH = 64
STEP = 10


EPS_NORM = 1e-05
BETA_ONE = 0.9
BETA_TWO = 0.999
EPS_ADAM = 1e-06
DECAY_RATE = 0.01
STEP_RATE = 0.5


def layer_norm(inputs, gain_vector):
    centre = jnp.mean(inputs, axis=-1, keepdims=True)
    shifted = inputs - centre
    spread = jnp.mean(shifted * shifted, axis=-1, keepdims=True)
    return shifted * lax.rsqrt(spread + EPS_NORM) * gain_vector


def xpos_tables(length, head_size):
    halfway = head_size // 2
    pair_index = jnp.arange(halfway, dtype=jnp.float32)
    angular = jnp.exp(-(2.0 * pair_index / head_size) * jnp.log(10000.0))
    zeta_base = (2.0 * pair_index + 0.4 * head_size) / (1.4 * head_size)
    position = jnp.arange(length, dtype=jnp.float32)[:, None, None]
    return (
        jnp.cos(position * angular),
        jnp.sin(position * angular),
        position / 512.0 * jnp.log(zeta_base),
    )


def rotate(inputs, tables, polarity):
    cosine, sine_part, exponent = tables
    halfway = inputs.shape[-1] // 2
    factor = jnp.exp(polarity * exponent)
    leading = inputs[..., :halfway]
    behind = inputs[..., halfway:]
    return jnp.concatenate(
        [
            (leading * cosine - behind * sine_part) * factor,
            (behind * cosine + leading * sine_part) * factor,
        ],
        axis=-1,
    )


def merge_images(text_rows, image_rows, offsets, image_count, position):
    slot_index = jnp.arange(offsets.shape[0], dtype=jnp.int32)
    inside = (
        (position[:, None] >= offsets[None, :])
        & (position[:, None] < offsets[None, :] + PATCH)
        & (slot_index[None, :] < image_count)
    )
    picked = jnp.sum(
        jnp.where(inside, slot_index[None, :] * PATCH + position[:, None] - offsets[None, :], 0),
        axis=-1,
    )
    chosen = jnp.take(image_rows, picked, axis=0)
    covered = jnp.any(inside, axis=-1)
    return jnp.where(covered[:, None], chosen, text_rows)


def adapt_step(gradient, master, moment, square, decay_rate):
    moment_new = BETA_ONE * moment + (1.0 - BETA_ONE) * gradient
    square_new = BETA_TWO * square + (1.0 - BETA_TWO) * gradient * gradient
    direction = (
        moment_new
        / (1.0 - BETA_ONE**STEP)
        / (jnp.sqrt(square_new / (1.0 - BETA_TWO**STEP)) + EPS_ADAM)
        + decay_rate * master
    )
    return (moment_new, square_new, direction)


def trust_move(master, direction, weight_sum, update_sum):
    return master - STEP_RATE * jnp.sqrt(weight_sum) / (jnp.sqrt(update_sum) + EPS_ADAM) * direction


def gain_segments(entries, model_width):
    return jnp.stack(
        [
            jnp.sum(entries[:model_width]),
            jnp.sum(entries[model_width : 2 * model_width]),
            jnp.sum(entries[2 * model_width : 3 * model_width]),
            jnp.sum(entries[3 * model_width :]),
        ]
    )


def gain_spread(sums, model_width, hidden_width):
    return jnp.concatenate(
        [
            jnp.broadcast_to(sums[0], (model_width,)),
            jnp.broadcast_to(sums[1], (model_width,)),
            jnp.broadcast_to(sums[2], (model_width,)),
            jnp.broadcast_to(sums[3], (hidden_width,)),
        ]
    )


def pair_sums(master, direction):
    return jnp.stack([jnp.sum(master * master), jnp.sum(direction * direction)])[None]


def on_device(
    text_states,
    image_states,
    image_offsets,
    image_counts,
    output_grad,
    head_master,
    head_moment,
    head_square,
    outward_master,
    outward_moment,
    outward_square,
    upward_master,
    upward_moment,
    upward_square,
    downward_master,
    downward_moment,
    downward_square,
    gains_master,
    gains_moment,
    gains_square,
):
    groups = lax.axis_size("mp")
    model_rank = lax.axis_index("mp")
    seq_count, local_len, model_width = text_states.shape
    length = local_len * groups
    hidden_local = upward_master.shape[1]
    heads_local = head_master.shape[2] // HEAD_DIM
    tables = xpos_tables(length, HEAD_DIM)
    position = model_rank * local_len + jnp.arange(local_len, dtype=jnp.int32)
    merged = jax.vmap(
        lambda text_rows, image_rows, offsets, image_count: merge_images(
            text_rows, image_rows, offsets, image_count, position
        )
    )(text_states, image_states, image_offsets, image_counts).astype(jnp.float32)
    gain_in = gains_master[:model_width]
    gain_ctx = gains_master[model_width : 2 * model_width]
    gain_mid = gains_master[2 * model_width : 3 * model_width]
    hidden_start = 3 * model_width + model_rank * hidden_local
    gain_hidden = lax.dynamic_slice_in_dim(gains_master, hidden_start, hidden_local)
    head_weight_whole, outward_weight_whole, upward_weight_whole, down_weight_whole = (
        lax.all_gather(head_master.astype(jnp.bfloat16), "dp", axis=1, tiled=True),
        lax.all_gather(outward_master.astype(jnp.bfloat16), "dp", axis=0, tiled=True),
        lax.all_gather(upward_master.astype(jnp.bfloat16), "dp", axis=0, tiled=True),
        lax.all_gather(downward_master.astype(jnp.bfloat16), "dp", axis=1, tiled=True),
    )
    normed_low = layer_norm(merged, gain_in).astype(jnp.bfloat16)
    normed_rows_full, cotangent_rows_full = (
        lax.all_gather(normed_low, "mp", axis=1, tiled=True),
        lax.all_gather(output_grad, "mp", axis=1, tiled=True),
    )
    projected = jnp.einsum(
        "hvg,bga->bhva", normed_rows_full, head_weight_whole, preferred_element_type=jnp.float32
    )
    shaped = projected.reshape(3, seq_count, length, heads_local, HEAD_DIM)
    queries = rotate(shaped[0], tables, 1.0).astype(jnp.bfloat16)
    key_rows = rotate(shaped[1], tables, -1.0).astype(jnp.bfloat16)
    values = shaped[2].astype(jnp.bfloat16)
    block_len = min(512, length)
    block_count = length // block_len
    starts = jnp.arange(block_count, dtype=jnp.int32) * block_len
    key_place = jnp.arange(length, dtype=jnp.int32)

    def block_scores(query_block, start):
        scores = (
            jnp.einsum("sqhd,skhd->shqk", query_block, key_rows, preferred_element_type=jnp.float32)
            * 0.125
        )
        allowed = key_place[None, :] <= (start + jnp.arange(block_len, dtype=jnp.int32))[:, None]
        return jnp.where(allowed, scores, -1e30)

    def forward_block(start):
        query_block = lax.dynamic_slice_in_dim(queries, start, block_len, 1)
        scores = block_scores(query_block, start)
        highest = jnp.max(scores, axis=-1, keepdims=True)
        exponent = jnp.exp(scores - highest)
        total = jnp.sum(exponent, axis=-1, keepdims=True)
        attention = exponent / total
        context_block = jnp.einsum(
            "shqk,skhd->sqhd",
            attention.astype(jnp.bfloat16),
            values,
            preferred_element_type=jnp.float32,
        )
        return (context_block, highest[..., 0] + jnp.log(total[..., 0]))

    context_blocks, log_sums = lax.map(forward_block, starts)
    context = jnp.transpose(context_blocks, (1, 0, 2, 3, 4)).reshape(
        seq_count, length, heads_local * HEAD_DIM
    )
    context_rows = lax.all_to_all(
        context.astype(jnp.bfloat16), "mp", split_axis=1, concat_axis=2, tiled=True
    )
    context_in = context_rows.astype(jnp.float32)
    mixed_half_precision = layer_norm(context_in, gain_ctx).astype(jnp.bfloat16)
    middle = merged + jnp.einsum(
        "ymq,qc->ymc",
        mixed_half_precision,
        outward_weight_whole,
        preferred_element_type=jnp.float32,
    )
    lifted_low = layer_norm(middle, gain_mid).astype(jnp.bfloat16)
    lifted_rows_full = lax.all_gather(lifted_low, "mp", axis=1, tiled=True)
    hidden_rows = jnp.einsum(
        "orb,bg->org", lifted_rows_full, upward_weight_whole, preferred_element_type=jnp.float32
    )
    activated = jax.nn.gelu(hidden_rows, approximate=False)
    first_sum, second_sum = lax.psum(
        (jnp.sum(activated, axis=-1), jnp.sum(activated * activated, axis=-1)), "mp"
    )
    centre = first_sum / FF
    scale_inv = lax.rsqrt(second_sum / FF - centre * centre + EPS_NORM)[..., None]
    standard = (activated - centre[..., None]) * scale_inv
    squashed_half_precision = (standard * gain_hidden).astype(jnp.bfloat16)
    ffn_part = jnp.einsum(
        "wxp,pk->wxk",
        squashed_half_precision,
        down_weight_whole,
        preferred_element_type=jnp.float32,
    )
    ffn_rows = lax.psum_scatter(
        ffn_part.astype(jnp.bfloat16), "mp", scatter_dimension=1, tiled=True
    ).astype(jnp.float32)
    layer_output = (middle + ffn_rows).astype(jnp.bfloat16)
    down_grad = jnp.einsum(
        "uxy,uxo->yo",
        squashed_half_precision,
        cotangent_rows_full,
        preferred_element_type=jnp.float32,
    )
    squashed_grad = jnp.einsum(
        "yxr,ur->yxu", cotangent_rows_full, down_weight_whole, preferred_element_type=jnp.float32
    )
    hidden_gain_grad = jnp.sum(squashed_grad * standard, axis=(0, 1))
    scaled_grad = squashed_grad * gain_hidden
    mean_one, mean_two = (
        lax.psum(jnp.sum(scaled_grad, axis=-1).astype(jnp.bfloat16), "mp").astype(jnp.float32),
        lax.psum(jnp.sum(scaled_grad * standard, axis=-1).astype(jnp.bfloat16), "mp").astype(
            jnp.float32
        ),
    )
    activated_grad = (
        scaled_grad - mean_one[..., None] / FF - standard * (mean_two[..., None] / FF)
    ) * scale_inv
    gelu_out, gelu_back = jax.vjp(partial(jax.nn.gelu, approximate=False), hidden_rows)
    hidden_rows_grad = gelu_back(activated_grad)[0].astype(jnp.bfloat16)
    upward_gradient = jnp.einsum(
        "gki,gkt->it", lifted_rows_full, hidden_rows_grad, preferred_element_type=jnp.float32
    )
    lifted_part = jnp.einsum(
        "eiw,mw->eim", hidden_rows_grad, upward_weight_whole, preferred_element_type=jnp.float32
    )
    lifted_grad = lax.psum_scatter(lifted_part, "mp", scatter_dimension=1, tiled=True)
    norm_out, middle_back = jax.vjp(layer_norm, middle, gain_mid)
    middle_part, mid_gain_grad = middle_back(lifted_grad)
    middle_grad = output_grad.astype(jnp.float32) + middle_part
    middle_half_precision = middle_grad.astype(jnp.bfloat16)
    outward_part = jnp.einsum(
        "hyk,hyo->ko",
        mixed_half_precision,
        middle_half_precision,
        preferred_element_type=jnp.float32,
    )
    mixed_grad = jnp.einsum(
        "hox,kx->hok",
        middle_half_precision,
        outward_weight_whole,
        preferred_element_type=jnp.float32,
    )
    context_out, context_back = jax.vjp(layer_norm, context_in, gain_ctx)
    context_grad, ctx_gain_grad = context_back(mixed_grad)
    context_heads = lax.all_to_all(
        context_grad.astype(jnp.bfloat16), "mp", split_axis=2, concat_axis=1, tiled=True
    )
    grad_heads = context_heads.reshape(seq_count, length, heads_local, HEAD_DIM)

    def backward_block(totals, inputs):
        key_total, value_total = totals
        start, log_block = inputs
        query_block = lax.dynamic_slice_in_dim(queries, start, block_len, 1)
        grad_block = lax.dynamic_slice_in_dim(grad_heads, start, block_len, 1)
        scores = block_scores(query_block, start)
        attention = jnp.exp(scores - log_block[..., None])
        prob_grad = jnp.einsum(
            "sqhd,skhd->shqk", grad_block, values, preferred_element_type=jnp.float32
        )
        row_dot = jnp.sum(attention * prob_grad, axis=-1, keepdims=True)
        score_low = (attention * (prob_grad - row_dot)).astype(jnp.bfloat16)
        query_turned = (
            jnp.einsum("shqk,skhd->sqhd", score_low, key_rows, preferred_element_type=jnp.float32)
            * 0.125
        )
        key_total = (
            key_total
            + jnp.einsum(
                "shqk,sqhd->skhd", score_low, query_block, preferred_element_type=jnp.float32
            )
            * 0.125
        )
        value_total = value_total + jnp.einsum(
            "shqk,sqhd->skhd",
            attention.astype(jnp.bfloat16),
            grad_block,
            preferred_element_type=jnp.float32,
        )
        return ((key_total, value_total), query_turned)

    zero_heads = jnp.zeros((seq_count, length, heads_local, HEAD_DIM), jnp.float32)
    (key_turned, value_grad), query_blocks = lax.scan(
        backward_block, (zero_heads, zero_heads), (starts, log_sums)
    )
    query_turned = jnp.transpose(query_blocks, (1, 0, 2, 3, 4)).reshape(
        seq_count, length, heads_local, HEAD_DIM
    )
    query_out, query_back = jax.vjp(lambda inputs: rotate(inputs, tables, 1.0), shaped[0])
    key_out, key_back = jax.vjp(lambda inputs: rotate(inputs, tables, -1.0), shaped[1])
    projection_gradient = (
        jnp.stack([query_back(query_turned)[0], key_back(key_turned)[0], value_grad])
        .astype(jnp.bfloat16)
        .reshape(3, seq_count, length, heads_local * HEAD_DIM)
    )
    head_grad = jnp.einsum(
        "fbn,ufbj->unj", normed_rows_full, projection_gradient, preferred_element_type=jnp.float32
    )
    normed_part = jnp.einsum(
        "acqr,aur->cqu", projection_gradient, head_weight_whole, preferred_element_type=jnp.float32
    )
    normed_grad = lax.psum_scatter(
        normed_part.astype(jnp.bfloat16), "mp", scatter_dimension=1, tiled=True
    ).astype(jnp.float32)
    input_out, input_back = jax.vjp(layer_norm, merged, gain_in)
    merged_part, in_gain_grad = input_back(normed_grad)
    input_grad = middle_grad + merged_part
    head_sum, outward_sum, upward_sum, downward_sum = (
        lax.psum_scatter(
            head_grad.astype(jnp.bfloat16), "dp", scatter_dimension=1, tiled=True
        ).astype(jnp.float32),
        lax.psum_scatter(
            outward_part.astype(jnp.bfloat16), "dp", scatter_dimension=0, tiled=True
        ).astype(jnp.float32),
        lax.psum_scatter(
            upward_gradient.astype(jnp.bfloat16), "dp", scatter_dimension=0, tiled=True
        ).astype(jnp.float32),
        lax.psum_scatter(
            down_grad.astype(jnp.bfloat16), "dp", scatter_dimension=1, tiled=True
        ).astype(jnp.float32),
    )
    outward_sum = lax.psum(outward_sum.astype(jnp.bfloat16), "mp").astype(jnp.float32)
    moment_head, square_head, head_dir = adapt_step(
        head_sum, head_master, head_moment, head_square, DECAY_RATE
    )
    moment_outward, square_outward, outward_dir = adapt_step(
        outward_sum, outward_master, outward_moment, outward_square, DECAY_RATE
    )
    moment_upward, square_upward, upward_dir = adapt_step(
        upward_sum, upward_master, upward_moment, upward_square, DECAY_RATE
    )
    moment_downward, square_downward, downward_dir = adapt_step(
        downward_sum, downward_master, downward_moment, downward_square, DECAY_RATE
    )
    owner = (model_rank == 0).astype(jnp.float32)
    head_part = jnp.stack(
        [
            jnp.sum(head_master * head_master, axis=(1, 2)),
            jnp.sum(head_dir * head_dir, axis=(1, 2)),
        ],
        axis=-1,
    )
    norm_part = jnp.concatenate(
        [
            head_part,
            pair_sums(outward_master, outward_dir) * owner,
            pair_sums(upward_master, upward_dir),
            pair_sums(downward_master, downward_dir),
        ],
        axis=0,
    )
    gains_part = jnp.concatenate(
        [in_gain_grad, ctx_gain_grad, mid_gain_grad, jnp.zeros((FF,), jnp.float32)]
    )
    gains_part = lax.dynamic_update_slice(gains_part, hidden_gain_grad, (hidden_start,))
    gains_sum, norm_sums = lax.psum((gains_part, norm_part), ("dp", "mp"))
    moment_gains, square_gains, gains_dir = adapt_step(
        gains_sum, gains_master, gains_moment, gains_square, 0.0
    )
    gains_sums = jnp.stack(
        [
            gain_segments(gains_master * gains_master, model_width),
            gain_segments(gains_dir * gains_dir, model_width),
        ],
        axis=-1,
    )
    updated_head = trust_move(
        head_master, head_dir, norm_sums[0:3, 0][:, None, None], norm_sums[0:3, 1][:, None, None]
    )
    updated_outward = trust_move(outward_master, outward_dir, norm_sums[3, 0], norm_sums[3, 1])
    updated_upward = trust_move(upward_master, upward_dir, norm_sums[4, 0], norm_sums[4, 1])
    updated_downward = trust_move(downward_master, downward_dir, norm_sums[5, 0], norm_sums[5, 1])
    updated_gains = trust_move(
        gains_master,
        gains_dir,
        gain_spread(gains_sums[:, 0], model_width, FF),
        gain_spread(gains_sums[:, 1], model_width, FF),
    )
    update_norms = jnp.sqrt(jnp.concatenate([norm_sums, gains_sums], axis=0))
    return (
        layer_output,
        input_grad,
        moment_head,
        square_head,
        updated_head,
        updated_head.astype(jnp.bfloat16),
        moment_outward,
        square_outward,
        updated_outward,
        updated_outward.astype(jnp.bfloat16),
        moment_upward,
        square_upward,
        updated_upward,
        updated_upward.astype(jnp.bfloat16),
        moment_downward,
        square_downward,
        updated_downward,
        updated_downward.astype(jnp.bfloat16),
        moment_gains,
        square_gains,
        updated_gains,
        update_norms,
    )


def solution(mesh):
    return jax.shard_map(
        on_device,
        mesh=mesh,
        in_specs=(
            P("dp", "mp", None),
            P("dp", None, None),
            P("dp", None),
            P("dp"),
            P("dp", "mp", None),
            P(None, "dp", "mp"),
            P(None, "dp", "mp"),
            P(None, "dp", "mp"),
            P("dp", None),
            P("dp", None),
            P("dp", None),
            P("dp", "mp"),
            P("dp", "mp"),
            P("dp", "mp"),
            P("mp", "dp"),
            P("mp", "dp"),
            P("mp", "dp"),
            P(),
            P(),
            P(),
        ),
        out_specs=(
            P("dp", "mp", None),
            P("dp", "mp", None),
            P(None, "dp", "mp"),
            P(None, "dp", "mp"),
            P(None, "dp", "mp"),
            P(None, "dp", "mp"),
            P("dp", None),
            P("dp", None),
            P("dp", None),
            P("dp", None),
            P("dp", "mp"),
            P("dp", "mp"),
            P("dp", "mp"),
            P("dp", "mp"),
            P("mp", "dp"),
            P("mp", "dp"),
            P("mp", "dp"),
            P("mp", "dp"),
            P(),
            P(),
            P(),
            P(),
        ),
        check_vma=False,
    )
```

profile of v0, /device:TPU:0, one launch (start us, length us, event | category | flops | bytes accessed | tf_op | source)
XLA Modules:
  0.0 2553.2 jit_solution(17883917249131691869)
XLA Ops:
  59.6 153.3 %all-gather.8.cloned.1.call-done = bf16[2,2048,2048]{2,1,0:T(8,128)(2,1)} async-done(((bf16[2,256,2048]{2,1,0:T(8,128)(2,1)}), bf16[2,2048,2048]{2,1,0:T(8,128)(2,1)}) %all-gather.8.cloned.1.call-update) | async-done | bytes 16777232 | tf_op jit(solution)/shard_map/all_gather | solution.py:163
  244.2 203.1 %while.30 = (s32[]{:T(128)}, bf16[4,2,512,4,64]{2,4,3,1,0:T(8,128)(2,1)}, f32[4,2,4,512]{3,2,1,0:T(4,128)}, s32[4]{0:T(128)S(1)}, bf16[2,2048,4,64]{1,3,2,0:T(8,...) while((s32[]{:T(128)}, ...), condition=%wide.region_7.8_spmd.clone.clone, body=%wide.region_4.7_spmd.clone.sunk.clone | while | flops 2249191936 | bytes 110761088 | solution.py:201
  468.9 46.3 %all-to-all-done = bf16[2,2048,256]{2,0,1:T(2,128)(2,1)S(1)} async-done(((bf16[2,2048,256]{2,0,1:T(2,128)(2,1)}), bf16[2,2048,256]{2,0,1:T(2,128)(2,1)S(1)}, u32[]{:S(2)}, u32[]{:S(2)}) %all-to-all-start) | async-done | bytes 2097184 | tf_op jit(solution)/shard_map/all_to_all | solution.py:205
  543.9 148.7 %all-gather.14.cloned.1.call-done = bf16[2,2048,2048]{2,1,0:T(8,128)(2,1)} async-done(((bf16[2,256,2048]{2,1,0:T(8,128)(2,1)}), bf16[2,2048,2048]{2,1,0:T(8,128)(2,1)}) %all-gather.14.cloned.1.call-update) | async-done | bytes 16777232 | tf_op jit(solution)/shard_map/all_gather | solution.py:217
  692.7 32.8 %fusion.75 = (u8[2048,1024]{0,1:T(8,128)(4,1)S(1)}, u8[2048,1024]{0,1:T(8,128)(4,1)}, u8[2048,1024]{0,1:T(8,128)(4,1)}, f32[2,2048,1024]{1,2,0:T(8,128)}) fusion(bf16[2,2048,2048]{2,1,0:T(8,128)(2,1)} %all-gather.14.cloned.1.call-done, bf16[2048,1024]{0,1:T(8,128)(2,1)} %all-gather.16.cloned.1.call-done), kind=kOutput, calls=%fused_computation.144 | convolution fusion | flops 17257463808 | bytes 44040192 | tf_op jit(solution)/shard_map/orb,bg->org/dot_general | solution.py:218
  725.4 43.1 %fusion.115 = (f32[2,2048]{1,0:T(2,128)S(1)}, f32[2,2048]{1,0:T(2,128)S(1)}, f32[2,2048,1024]{1,2,0:T(8,128)}, f32[2,2048,1024]{1,2,0:T(8,128)}) fusion(f32[2,2048,1024]{1,2,0:T(8,128)} %get-tuple-element.402, u8[2048,1024]{0,1:T(8,128)(4,1)} %get-tuple-element.274, u8[2048,1024]{0,1:T(8,128)(4,1)} %get-tuple-element.275, ...), kind=kLoop, calls=%fused_computation.267 | loop fusion | flops 310370304 | bytes 56655872 | tf_op jit(solution)/shard_map/reduce_sum | solution.py:223
  768.5 31.3 %all-reduce.5 = (f32[2,2048]{1,0:T(2,128)S(1)}, f32[2,2048]{1,0:T(2,128)S(1)}) all-reduce(f32[2,2048]{1,0:T(2,128)S(1)} %get-tuple-element.272, f32[2,2048]{1,0:T(2,128)S(1)} %get-tuple-element.271), channel_id=1, replica_groups=mesh['dp'=4,'mp'=8] {'mp'}, use_global_device_ids=true, to_apply=%region_15.16 | all-reduce | flops 8192 | bytes 65536 | tf_op jit(solution)/shard_map/psum | solution.py:222
  799.8 44.2 %all-gather.20.cloned.1.call-done = bf16[2,2048,2048]{2,1,0:T(8,128)(2,1)} async-done(((bf16[2,256,2048]{2,1,0:T(8,128)(2,1)}), bf16[2,2048,2048]{2,1,0:T(8,128)(2,1)}) %all-gather.20.cloned.1.call-update) | async-done | bytes 16777232 | tf_op jit(solution)/shard_map/all_gather | solution.py:164
  870.3 51.0 %reduce-scatter.20.cloned.1.call-done = bf16[1024,512]{1,0:T(8,128)(2,1)} async-done(((bf16[1024,2048]{1,0:T(8,128)(2,1)}), bf16[1024,512]{1,0:T(8,128)(2,1)}) %reduce-scatter.20.cloned.1.call-update) | async-done | bytes 1048592 | tf_op jit(solution)/shard_map/reduce_scatter | solution.py:358
  928.2 52.7 %all-gather.18.cloned.1.call-done = bf16[1024,2048]{1,0:T(8,128)(2,1)} async-done(((bf16[1024,512]{1,0:T(8,128)(2,1)}), bf16[1024,2048]{1,0:T(8,128)(2,1)}) %all-gather.18.cloned.1.call-update) | async-done | bytes 4194320 | tf_op jit(solution)/shard_map/all_gather | solution.py:159
  980.8 29.8 %multiply_reduce_fusion.1 = (f32[1024]{0:T(1024)}, bf16[2,2048]{1,0:T(2,128)(2,1)S(1)}, bf16[2,2048]{1,0:T(2,128)(2,1)S(1)}, f32[2,2048,1024]{1,2,0:T(8,128)}) fusion(f32[2,2048,1024]{1,2,0:T(8,128)} %get-tuple-element.356, f32[2,2048]{1,0:T(2,128)S(1)} %get-tuple-element.389, f32[2,2048]{1,0:T(2,128)S(1)} %get-tuple-element.388, ...), kind=kOutput, calls=%fused_computation.60 | convolution fusion | flops 17213415424 | bytes 54583296 | tf_op jit(solution)/shard_map/yxr,ur->yxu/dot_general | solution.py:245
  1010.7 28.8 %all-reduce.6 = (bf16[2,2048]{1,0:T(2,128)(2,1)S(1)}, bf16[2,2048]{1,0:T(2,128)(2,1)S(1)}) all-reduce(bf16[2,2048]{1,0:T(2,128)(2,1)S(1)} %get-tuple-element.269, bf16[2,2048]{1,0:T(2,128)(2,1)S(1)} %get-tuple-element.270), channel_id=1, replica_groups=mesh['dp'=4,'mp'=8] {'mp'}, use_global_device_ids=true, to_apply=%region_20.21 | all-reduce | flops 8192 | bytes 32768 | tf_op jit(solution)/shard_map/psum | solution.py:252
  1088.8 27.5 %convolution_convert_fusion = bf16[2,2048,2048]{2,1,0:T(8,128)(2,1)} fusion(bf16[1024,2048]{1,0:T(8,128)(2,1)} %all-gather.18.cloned.1.call-done, f32[2,2048,1024]{1,2,0:T(8,128)} %get-tuple-element.356, f32[1024]{0:T(1024)S(1)} %dynamic_slice.23, f32[2,2048]{1,0:T(2,128)S(1)} %get-tuple-element.389, f32[2,2048]{1,0:T(2,128)S(1)} %get-tuple-element.388), kind=kOutput, calls=%fused_computation.80 | convolution fusion | flops 17205035008 | bytes 37785600 | tf_op jit(solution)/shard_map/wxp,pk->wxk/dot_general | solution.py:229
  1116.4 295.3 %reduce-scatter.10.cloned.1.call-done = f32[2,256,2048]{2,1,0:T(8,128)} async-done(((f32[2,2048,2048]{2,1,0:T(8,128)}), f32[2,256,2048]{2,1,0:T(8,128)}) %reduce-scatter.10.cloned.1.call-update) | async-done | bytes 4194320 | tf_op jit(solution)/shard_map/reduce_scatter | solution.py:267
  1417.2 163.4 %reduce-scatter.8.cloned.1.call-done = bf16[2,256,2048]{2,1,0:T(8,128)(2,1)} async-done(((bf16[2,2048,2048]{2,1,0:T(8,128)(2,1)}), bf16[2,256,2048]{2,1,0:T(8,128)(2,1)}) %reduce-scatter.8.cloned.1.call-update) | async-done | bytes 2097168 | tf_op jit(solution)/shard_map/reduce_scatter | solution.py:235
  1680.7 449.1 %while.31 = (s32[]{:T(128)}, f32[2,2048,4,64]{1,3,2,0:T(8,128)}, f32[2,2048,4,64]{1,3,2,0:T(8,128)}, f32[4,2,512,4,64]{2,4,3,1,0:T(8,128)}, s32[4]{0:T(128)S(1)}...) while((s32[]{:T(128)}, f32[2,2048,4,64]{1,3,2,0:T(8,128)}, ...), condition=%wide.region_28.29_spmd.clone.clone, body=%wide.region_26.28_spmd.clone.sunk.clone | while | flops 5501088256 | bytes 290575040 | solution.py:323
  1700.5 26.2 %multiply_reduce_fusion.20 = (f32[2,4,512]{2,1,0:T(4,128)S(1)}, f32[2,4,512,2048]{3,2,1,0:T(8,128)}) fusion(f32[2,4,512,2048]{3,2,1,0:T(8,128)} %fusion.198, f32[2,4,512]{2,1,0:T(4,128)S(1)} %dynamic-slice_bitcast_fusion.3, pred[512,2048]{1,0:T(8,128)(4,1)S(1)} %iota_compare_fusion.8, bf16[2,2048,4,64]{1,3,2,0:T(8,128)(2,1)S(1)} %copy-done.9, ...), kind=kOutput, calls=%fused_computation.20.clone.1.clone | convolution fusion | flops 1115680768 | bytes 70811648 | tf_op jit(solution)/shard_map/while/body/eval_jaxpr/sqhd,skhd->shqk/dot_general | solution.py:298
  1726.7 28.1 %multiply_convert_fusion.14 = bf16[2,4,512,2048]{3,2,1,0:T(8,128)(2,1)} fusion(f32[2,4,512,2048]{3,2,1,0:T(8,128)} %get-tuple-element.551, f32[2,4,512,2048]{3,2,1,0:T(8,128)} %fusion.198, f32[2,4,512]{2,1,0:T(4,128)S(1)} %get-tuple-element.552, f32[2,4,512]{2,1,0:T(4,128)S(1)} %dynamic-slice_bitcast_fusion.3, ...), kind=kLoop, calls=%fused_computation.19.clone.1.clone | loop fusion | flops 50331648 | bytes 84967424 | tf_op jit(solution)/shard_map/while/body/eval_jaxpr/convert_element_type | solution.py:302
  1837.1 27.7 %multiply_convert_fusion.14 = bf16[2,4,512,2048]{3,2,1,0:T(8,128)(2,1)} fusion(f32[2,4,512,2048]{3,2,1,0:T(8,128)} %get-tuple-element.551, f32[2,4,512,2048]{3,2,1,0:T(8,128)} %fusion.198, f32[2,4,512]{2,1,0:T(4,128)S(1)} %get-tuple-element.552, f32[2,4,512]{2,1,0:T(4,128)S(1)} %dynamic-slice_bitcast_fusion.3, ...), kind=kLoop, calls=%fused_computation.19.clone.1.clone | loop fusion | flops 50331648 | bytes 84967424 | tf_op jit(solution)/shard_map/while/body/eval_jaxpr/convert_element_type | solution.py:302
  1949.6 27.7 %multiply_convert_fusion.14 = bf16[2,4,512,2048]{3,2,1,0:T(8,128)(2,1)} fusion(f32[2,4,512,2048]{3,2,1,0:T(8,128)} %get-tuple-element.551, f32[2,4,512,2048]{3,2,1,0:T(8,128)} %fusion.198, f32[2,4,512]{2,1,0:T(4,128)S(1)} %get-tuple-element.552, f32[2,4,512]{2,1,0:T(4,128)S(1)} %dynamic-slice_bitcast_fusion.3, ...), kind=kLoop, calls=%fused_computation.19.clone.1.clone | loop fusion | flops 50331648 | bytes 84967424 | tf_op jit(solution)/shard_map/while/body/eval_jaxpr/convert_element_type | solution.py:302
  2061.9 27.7 %multiply_convert_fusion.14 = bf16[2,4,512,2048]{3,2,1,0:T(8,128)(2,1)} fusion(f32[2,4,512,2048]{3,2,1,0:T(8,128)} %get-tuple-element.551, f32[2,4,512,2048]{3,2,1,0:T(8,128)} %fusion.198, f32[2,4,512]{2,1,0:T(4,128)S(1)} %get-tuple-element.552, f32[2,4,512]{2,1,0:T(4,128)S(1)} %dynamic-slice_bitcast_fusion.3, ...), kind=kLoop, calls=%fused_computation.19.clone.1.clone | loop fusion | flops 50331648 | bytes 84967424 | tf_op jit(solution)/shard_map/while/body/eval_jaxpr/convert_element_type | solution.py:302
  2224.4 59.8 %all-reduce.9.cloned.1.call-done = bf16[512,2048]{1,0:T(8,128)(2,1)} async-done(((bf16[512,2048]{1,0:T(8,128)(2,1)}), bf16[512,2048]{1,0:T(8,128)(2,1)}) %all-reduce.9.cloned.1.call-update) | async-done | bytes 2097168 | tf_op jit(solution)/shard_map/psum | solution.py:362
  2295.5 158.9 %reduce-scatter.12.cloned.1.call-done = bf16[2,256,2048]{2,1,0:T(8,128)(2,1)} async-done(((bf16[2,2048,2048]{2,1,0:T(8,128)(2,1)}), bf16[2,256,2048]{2,1,0:T(8,128)(2,1)}) %reduce-scatter.12.cloned.1.call-update) | async-done | bytes 2097168 | tf_op jit(solution)/shard_map/reduce_scatter | solution.py:342
  2462.6 38.4 %all-reduce.4 = (f32[6,2]{0,1:T(2,128)S(1)}, f32[14336]{0:T(1024)S(1)}) all-reduce(f32[6,2]{0,1:T(2,128)S(1)} %pad_maximum_fusion.6, f32[14336]{0:T(1024)S(1)} %dynamic_update_slice.14), channel_id=1, replica_groups=mesh['dp'=4,'mp'=8] {'dp','mp'}, use_global_device_ids=true, to_apply=%region_45.46 | all-reduce | flops 14348 | bytes 114784 | tf_op jit(solution)/shard_map/psum | solution.py:396
  (398 shorter events, 974.5 us)
Async XLA Ops:
  7.2 52.4 %all-gather.10.cloned.1.call-start = ((), (), s32[]{:S(2)}) async-start(), calls=%async_computation.10 | async-start | bytes 3932160 | tf_op jit(solution)/shard_map/all_gather | solution.py:156
  12.9 200.0 %all-gather.8.cloned.1.call-start = ((), (), s32[]{:S(2)}) async-start(), calls=%async_computation.9 | async-start | bytes 18874368 | tf_op jit(solution)/shard_map/all_gather | solution.py:163
  32.8 486.6 %all-gather.12.cloned.1.call-start = ((), (), s32[]{:S(2)}) async-start(), calls=%async_computation.11 | async-start | bytes 10485760 | tf_op jit(solution)/shard_map/all_gather | solution.py:157
  462.6 52.6 %all-to-all-start = ((bf16[2,2048,256]{2,0,1:T(2,128)(2,1)}), bf16[2,2048,256]{2,0,1:T(2,128)(2,1)S(1)}, u32[]{:S(2)}, u32[]{:S(2)}) async-start(bf16[2,2048,256]{2,0,1:T(2,128)(2,1)} %reshape.522), calls=%async_computation | async-start | bytes 4194304 | tf_op jit(solution)/shard_map/all_to_all | solution.py:205
  466.2 77.7 %all-gather.16.cloned.1.call-start = ((), (), s32[]{:S(2)}) async-start(), calls=%async_computation.13 | async-start | bytes 5242880 | tf_op jit(solution)/shard_map/all_gather | solution.py:158
  468.9 223.8 %all-gather.14.cloned.1.call-start = ((), (), s32[]{:S(2)}) async-start(), calls=%async_computation.12 | async-start | bytes 18874368 | tf_op jit(solution)/shard_map/all_gather | solution.py:217
  542.6 301.4 %all-gather.20.cloned.1.call-start = ((), (), s32[]{:S(2)}) async-start(), calls=%async_computation.16 | async-start | bytes 18874368 | tf_op jit(solution)/shard_map/all_gather | solution.py:164
  543.2 378.1 %reduce-scatter.20.cloned.1.call-start = ((), (), s32[]{:S(2)}) async-start(), calls=%async_computation.23 | async-start | bytes 5242880 | tf_op jit(solution)/shard_map/reduce_scatter | solution.py:358
  870.2 110.6 %all-gather.18.cloned.1.call-start = ((), (), s32[]{:S(2)}) async-start(), calls=%async_computation.14 | async-start | bytes 5242880 | tf_op jit(solution)/shard_map/all_gather | solution.py:159
  928.1 483.6 %reduce-scatter.10.cloned.1.call-start = ((), (), s32[]{:S(2)}) async-start(), calls=%async_computation.17 | async-start | bytes 37748736 | tf_op jit(solution)/shard_map/reduce_scatter | solution.py:267
  1088.8 491.8 %reduce-scatter.8.cloned.1.call-start = ((), (), s32[]{:S(2)}) async-start(), calls=%async_computation.15 | async-start | bytes 18874368 | tf_op jit(solution)/shard_map/reduce_scatter | solution.py:235
  1116.3 295.4 %copy-start.47 = (f32[2048]{0:T(1024)S(1)}, f32[2048]{0:T(1024)}, u32[]{:S(2)}) copy-start(f32[2048]{0:T(1024)} %get-tuple-element.385) | copy-start | bytes 24580
  1116.3 295.4 %copy-start.55 = (f32[2,256]{1,0:T(2,128)S(1)}, f32[2,256]{1,0:T(2,128)}, u32[]{:S(2)}) copy-start(f32[2,256]{1,0:T(2,128)} %copy-done.54) | copy-start | bytes 6148
  1116.3 295.4 %copy-start.59 = (f32[2,256]{1,0:T(2,128)S(1)}, f32[2,256]{1,0:T(2,128)}, u32[]{:S(2)}) copy-start(f32[2,256]{1,0:T(2,128)} %copy-done.58) | copy-start | bytes 6148
  1116.3 300.8 %copy-start.65 = (f32[2,256]{1,0:T(2,128)S(1)}, f32[2,256]{1,0:T(2,128)}, u32[]{:S(2)}) copy-start(f32[2,256]{1,0:T(2,128)} %copy-done.64) | copy-start | bytes 6148
  1116.3 1057.8 %reduce-scatter.16.cloned.1.call-start = ((), (), s32[]{:S(2)}) async-start(), calls=%async_computation.20 | async-start | bytes 10485760 | tf_op jit(solution)/shard_map/reduce_scatter | solution.py:352
  1618.2 52.6 %all-to-all-start.1 = ((bf16[2,256,2048]{1,0,2:T(2,128)(2,1)}), bf16[2,256,2048]{1,0,2:T(2,128)(2,1)S(1)}, u32[]{:S(2)}, u32[]{:S(2)}) async-start(bf16[2,256,2048]{1,0,2:T(2,128)(2,1)} %copy.136), calls=%async_computation.3 | async-start | bytes 4194304 | tf_op jit(solution)/shard_map/all_to_all | solution.py:286
  1621.8 581.3 %reduce-scatter.18.cloned.1.call-start = ((), (), s32[]{:S(2)}) async-start(), calls=%async_computation.22 | async-start | bytes 5242880 | tf_op jit(solution)/shard_map/reduce_scatter | solution.py:355
  1646.0 571.2 %reduce-scatter.14.cloned.1.call-start = ((), (), s32[]{:S(2)}) async-start(), calls=%async_computation.19 | async-start | bytes 3932160 | tf_op jit(solution)/shard_map/reduce_scatter | solution.py:349
  2174.0 110.2 %all-reduce.9.cloned.1.call-start = ((), (), s32[]{:S(2)}) async-start(), calls=%async_computation.21 | async-start | bytes 4194304 | tf_op jit(solution)/shard_map/psum | solution.py:362
  2174.6 279.8 %reduce-scatter.12.cloned.1.call-start = ((), (), s32[]{:S(2)}) async-start(), calls=%async_computation.18 | async-start | bytes 18874368 | tf_op jit(solution)/shard_map/reduce_scatter | solution.py:342
  2224.4 230.0 %copy-start.7 = (bf16[2,256,2048]{2,1,0:T(8,128)(2,1)S(1)}, bf16[2,256,2048]{2,1,0:T(8,128)(2,1)}, u32[]{:S(2)}) copy-start(bf16[2,256,2048]{2,1,0:T(8,128)(2,1)} %copy-done.5) | copy-start | bytes 6291460
  2224.4 230.0 %copy-start.45 = (f32[2048]{0:T(1024)S(1)}, f32[2048]{0:T(1024)}, u32[]{:S(2)}) copy-start(f32[2048]{0:T(1024)} %copy-done.44) | copy-start | bytes 24580
  2224.4 230.0 %copy-start.49 = (f32[2,256]{1,0:T(2,128)S(1)}, f32[2,256]{1,0:T(2,128)}, u32[]{:S(2)}) copy-start(f32[2,256]{1,0:T(2,128)} %copy-done.48) | copy-start | bytes 6148
  (75 other events, 2477.4 us)
Sparse Core Ops, SparseCore 0:
  13.0 46.5 all-gather.9
  61.8 151.0 all-gather.7
  215.3 85.8 all-gather.11
  469.2 53.8 all-gather.15
  542.7 149.9 all-gather.13
  694.1 149.8 all-gather.19
  870.4 50.9 reduce-scatter.19
  928.2 52.5 all-gather.17
  1088.9 322.7 reduce-scatter.9
  1413.9 166.6 reduce-scatter.7
  1599.1 84.7 reduce-scatter.15
  1686.9 52.6 reduce-scatter.17
  2174.2 42.9 reduce-scatter.13
  2219.4 64.8 all-reduce.8
  2286.5 167.8 reduce-scatter.11
where the time goes:
time: 2560 us; the launch traced here: 2550 us
  waiting for transfers between devices  1220 us (48%)
  matrix products  703 us (27%)
  other arithmetic  370 us (14%)
  local copies, waits for them, and re-layouts  114 us (4%)
  blocking collectives  98.4 us (4%)
    reduce_scatter x1, waiting for transfers between devices, on_device(): lax.psum_scatter(lifted_part, 'mp', scatter_dimension=1, tiled=True)  295 us
    reduce_scatter x1, waiting for transfers between devices, on_device(): lax.psum_scatter(ffn_part.astype(jnp.bfloat16), 'mp', scatter_dimension=1...  163 us
    reduce_scatter x1, waiting for transfers between devices, on_device(): lax.psum_scatter(normed_part.astype(jnp.bfloat16), 'mp', scatter_dimensio...  159 us
    all_gather x1, waiting for transfers between devices, on_device(): lax.all_gather(normed_low, 'mp', axis=1, tiled=True)  153 us
    all_gather x1, waiting for transfers between devices, on_device(): lifted_rows_full = lax.all_gather(lifted_low, 'mp', axis=1, tiled=True)  149 us
    dot_general x8, matrix products, block_scores(): jnp.einsum('sqhd,skhd->shqk', query_block, key_rows, preferred_element_ty...  121 us
    convert_element_type x4, other arithmetic, backward_block(): score_low = (attention * (prob_grad - row_dot)).astype(jnp.bfloat16)  111 us
    dot_general x4, matrix products, backward_block(): jnp.einsum('sqhd,skhd->shqk', grad_block, values, preferred_element_type=...  104 us
  transfers between devices with their start and end apart: 17, of which 13 were waited for; matrix products, arithmetic and copies ran while one was open for 39% of the time, Pallas kernels for 0%

commit v1 on v0

--- a/solution.py
+++ b/solution.py
@@ -3,6 +3,8 @@
 import jax
 import jax.numpy as jnp
 from jax import lax
+from jax.experimental import pallas as pl
+from jax.experimental.pallas import tpu as pltpu
 from jax.sharding import PartitionSpec as P
 
 HEAD_DIM = 64
@@ -112,7 +114,7 @@
     return jnp.stack([jnp.sum(master * master), jnp.sum(direction * direction)])[None]
 
 
-def on_device(
+def on_device_general(
     text_states,
     image_states,
     image_offsets,
@@ -443,9 +445,910 @@
     )
 
 
+LOG2E = 1.4426950408889634
+LANES = 128
+NT = (((1,), (1,)), ((), ()))
+NN = (((1,), (0,)), ((), ()))
+LOW = jnp.bfloat16
+WIDE = jnp.float32
+ONCE = pl.Buffered(1)
+
+
+def dot(left, right, dims):
+    return lax.dot_general(left, right, dims, preferred_element_type=WIDE)
+
+
+def kernel_call(body, grid, in_specs, out_specs, out_shape, scratch, flops, moved, operands):
+    return pl.pallas_call(
+        body,
+        grid_spec=pltpu.PrefetchScalarGridSpec(
+            num_scalar_prefetch=1, grid=grid, in_specs=in_specs, out_specs=out_specs, scratch_shapes=scratch
+        ),
+        out_shape=out_shape,
+        compiler_params=pltpu.CompilerParams(vmem_limit_bytes=56 << 20),
+        cost_estimate=pl.CostEstimate(flops=int(flops), bytes_accessed=int(moved), transcendentals=0),
+    )(*operands)
+
+
+def own_rows(sub, rank, j, b):
+    return pl.ds(pl.multiple_of(b * 4 * sub + (rank ^ j) * sub, sub), sub)
+
+
+def own_block(place, k, width):
+    return pl.ds(pl.multiple_of((place ^ k) * width, width), width)
+
+
+def swap_halves(block):
+    low = lax.broadcasted_iota(jnp.int32, (1, LANES), 1) % HEAD_DIM < HEAD_DIM // 2
+    return jnp.where(low, pltpu.roll(block, LANES - HEAD_DIM // 2, 1), pltpu.roll(block, HEAD_DIM // 2, 1))
+
+
+def project_kernel(ids, x, w0, w1, w2, w3, cq, sq, ck, sk, q, k, v):
+    depth = w0.shape[1]
+    width = w0.shape[2]
+    for f, (out, c, s) in enumerate(((q, cq, sq), (k, ck, sk), (v, None, None))):
+        total = None
+        for n, w in enumerate((w0, w1, w2, w3)):
+            part = dot(x[:, own_block(ids[1], n, depth)], w[f], NN)
+            total = part if total is None else total + part
+        for p in range(width // LANES):
+            here = slice(p * LANES, (p + 1) * LANES)
+            block = total[:, here]
+            if c is not None:
+                block = block * c[...] + swap_halves(block) * s[...]
+            out[:, here] = block.astype(LOW)
+
+
+def project(ids, x, weights, tables, j):
+    rows, model = x.shape
+    sub = rows // 2
+    width = weights[0].shape[2]
+    table = pl.BlockSpec((sub, LANES), lambda b, ids: (b * 4 + (ids[0] ^ j), 0))
+    out = pl.BlockSpec((sub, width), lambda b, ids: (b, 0))
+    return kernel_call(
+        project_kernel,
+        (2,),
+        [pl.BlockSpec((sub, model), lambda b, ids: (b, 0))]
+        + [pl.BlockSpec(weights[0].shape, lambda b, ids: (0, 0, 0), pipeline_mode=ONCE)] * 4
+        + [table] * 4,
+        [out] * 3,
+        [jax.ShapeDtypeStruct((rows, width), LOW)] * 3,
+        [],
+        6 * rows * model * width,
+        6 * model * width + 8 * rows * model,
+        (ids, x, *weights, *tables),
+    )
+
+
+def attend_kernel(ids, *refs, bq, bk):
+    q_, k_, v_, o_, lse_ref = refs[0:4], refs[4:8], refs[8:12], refs[12:16], refs[16]
+    qs, ks, vt, os = refs[17:]
+    rank = ids[0]
+    length = qs.shape[0]
+    sub = q_[0].shape[0] // 2
+    for j in range(4):
+        for b in range(2):
+            rows = own_rows(sub, rank, j, b)
+            here = slice(b * sub, (b + 1) * sub)
+            qs[rows, :] = q_[j][here, :]
+            ks[rows, :] = k_[j][here, :]
+            vt[:, rows] = v_[j][here, :].T
+    first = lax.broadcasted_iota(jnp.int32, (1, LANES), 1) < HEAD_DIM
+    ratio = bq // bk
+
+    def q_block(i, _):
+        here = pl.ds(pl.multiple_of(i * bq, bq), bq)
+        q = qs[here, :]
+        zero = jnp.zeros_like(q)
+        parted = (jnp.where(first, q, zero), jnp.where(first, zero, q))
+
+        def step(j, carry, diagonal):
+            at = pl.multiple_of(j * bk, bk)
+            k = ks[pl.ds(at, bk), :]
+            out = []
+            for h in range(2):
+                highest, total, sums = carry[h]
+                scores = dot(k, parted[h], NT) * (0.125 * LOG2E)
+                if diagonal is not None:
+                    key = diagonal * bk + lax.broadcasted_iota(jnp.int32, (bk, bq), 0)
+                    scores = jnp.where(key <= lax.broadcasted_iota(jnp.int32, (bk, bq), 1), scores, -1e30)
+                new = jnp.maximum(highest, jnp.max(scores, axis=0, keepdims=True))
+                probs = jnp.exp2(scores - new)
+                scale = jnp.exp2(highest - new)
+                total = total * scale + jnp.sum(probs, axis=0, keepdims=True)
+                rows = vt[h * HEAD_DIM : (h + 1) * HEAD_DIM, pl.ds(at, bk)]
+                out.append((new, total, sums * scale + dot(rows, probs.astype(LOW), NN)))
+            return tuple(out)
+
+        start = tuple(
+            (jnp.full((1, bq), -1e30, WIDE), jnp.zeros((1, bq), WIDE), jnp.zeros((HEAD_DIM, bq), WIDE))
+            for _ in range(2)
+        )
+        carry = lax.fori_loop(0, i * ratio, lambda j, c: step(j, c, None), start)
+        for d in range(ratio):
+            carry = step(i * ratio + d, carry, d)
+        turned = jnp.concatenate([carry[h][2] / carry[h][1] for h in range(2)], axis=0)
+        os[here, :] = turned.T.astype(LOW)
+        for h in range(2):
+            lse_ref[0, h : h + 1, here] = carry[h][0] + jnp.log2(carry[h][1])
+        return 0
+
+    lax.fori_loop(0, length // bq, q_block, 0)
+    for j in range(4):
+        for b in range(2):
+            o_[j][b * sub : (b + 1) * sub, :] = os[own_rows(sub, rank, j, b), :]
+
+
+def attend(ids, queries, keys, values):
+    rows, width = queries[0].shape
+    length, pairs = rows * 4, width // LANES
+    chunk = pl.BlockSpec((rows, LANES), lambda p, ids: (0, p))
+    low = pltpu.VMEM((length, LANES), LOW)
+    result = kernel_call(
+        partial(attend_kernel, bq=min(1024, length), bk=min(512, length)),
+        (pairs,),
+        [chunk] * 12,
+        [chunk] * 4 + [pl.BlockSpec((1, 2, length), lambda p, ids: (p, 0, 0))],
+        [jax.ShapeDtypeStruct((rows, width), LOW)] * 4 + [jax.ShapeDtypeStruct((pairs, 2, length), WIDE)],
+        [low, low, pltpu.VMEM((LANES, length), LOW), low],
+        40e9,
+        10e6,
+        (ids, *queries, *keys, *values),
+    )
+    return result[:4], result[4]
+
+
+def attend_back_kernel(ids, *refs, bq, bk):
+    q_, k_, v_, d_, o_ = refs[0:4], refs[4:8], refs[8:12], refs[12:16], refs[16:20]
+    lse_ref, cq, sq, ck, sk = refs[20:25]
+    dq_, dk_, dv_ = refs[25:29], refs[29:33], refs[33:37]
+    qs, ks, vs, ds, kt, dqt, dks, dvs, delta = refs[37:]
+    rank = ids[0]
+    length = qs.shape[0]
+    sub = q_[0].shape[0] // 2
+    for j in range(4):
+        for b in range(2):
+            rows = own_rows(sub, rank, j, b)
+            here = slice(b * sub, (b + 1) * sub)
+            qs[rows, :] = q_[j][here, :]
+            ks[rows, :] = k_[j][here, :]
+            kt[:, rows] = k_[j][here, :].T
+            vs[rows, :] = v_[j][here, :]
+            ds[rows, :] = d_[j][here, :]
+            product = (d_[j][here, :].astype(WIDE) * o_[j][here, :].astype(WIDE)).T
+            delta[0:1, rows] = jnp.sum(product[:HEAD_DIM], axis=0, keepdims=True)
+            delta[1:2, rows] = jnp.sum(product[HEAD_DIM:], axis=0, keepdims=True)
+    first = lax.broadcasted_iota(jnp.int32, (1, LANES), 1) < HEAD_DIM
+    dqt[...] = jnp.zeros_like(dqt)
+
+    def k_block(j, _):
+        at = pl.ds(pl.multiple_of(j * bk, bk), bk)
+        k = ks[at, :]
+        v = vs[at, :]
+
+        def step(i, carry, diagonal):
+            dk, dv = carry
+            here = pl.ds(pl.multiple_of(i * bq, bq), bq)
+            q, do = qs[here, :], ds[here, :]
+            zero = jnp.zeros_like(q)
+            for h in range(2):
+                lanes = slice(h * HEAD_DIM, (h + 1) * HEAD_DIM)
+                q_own = jnp.where(first, q, zero) if h == 0 else jnp.where(first, zero, q)
+                do_own = jnp.where(first, do, zero) if h == 0 else jnp.where(first, zero, do)
+                scores = dot(k, q_own, NT) * (0.125 * LOG2E) - lse_ref[0, h : h + 1, here]
+                if diagonal:
+                    key = lax.broadcasted_iota(jnp.int32, (bk, bq), 0)
+                    scores = jnp.where(key <= lax.broadcasted_iota(jnp.int32, (bk, bq), 1), scores, -1e30)
+                probs = jnp.exp2(scores)
+                prob_grad = dot(v, do_own, NT)
+                grad = (probs * (prob_grad - delta[h : h + 1, here])).astype(LOW)
+                dv = dv + dot(probs.astype(LOW), do_own, NN)
+                dk = dk + dot(grad, q_own, NN)
+                dqt[lanes, here] += dot(kt[lanes, at], grad, NN)
+            return dk, dv
+
+        zeros = jnp.zeros((bk, LANES), WIDE)
+        carry = step(j, (zeros, zeros), True)
+        dk, dv = lax.fori_loop(j + 1, length // bq, lambda i, c: step(i, c, False), carry)
+        dks[at, :] = dk * 0.125
+        dvs[at, :] = dv.astype(LOW)
+        return 0
+
+    lax.fori_loop(0, length // bk, k_block, 0)
+    for j in range(4):
+        for b in range(2):
+            rows = own_rows(sub, rank, j, b)
+            here = slice(b * sub, (b + 1) * sub)
+            query_grad = dqt[:, rows].T * 0.125
+            dq_[j][here, :] = (query_grad * cq[rows, :] - swap_halves(query_grad) * sq[rows, :]).astype(LOW)
+            key_grad = dks[rows, :]
+            dk_[j][here, :] = (key_grad * ck[rows, :] - swap_halves(key_grad) * sk[rows, :]).astype(LOW)
+            dv_[j][here, :] = dvs[rows, :]
+
+
+def attend_back(ids, queries, keys, values, cotangents, contexts, lse, tables):
+    rows, width = queries[0].shape
+    length, pairs = rows * 4, width // LANES
+    chunk = pl.BlockSpec((rows, LANES), lambda p, ids: (0, p))
+    whole = pl.BlockSpec((length, LANES), lambda p, ids: (0, 0), pipeline_mode=ONCE)
+    low = pltpu.VMEM((length, LANES), LOW)
+    block = min(512, length)
+    result = kernel_call(
+        partial(attend_back_kernel, bq=block, bk=block),
+        (pairs,),
+        [chunk] * 20 + [pl.BlockSpec((1, 2, length), lambda p, ids: (p, 0, 0))] + [whole] * 4,
+        [chunk] * 12,
+        [jax.ShapeDtypeStruct((rows, width), LOW)] * 12,
+        [
+            low,
+            low,
+            low,
+            low,
+            pltpu.VMEM((LANES, length), LOW),
+            pltpu.VMEM((LANES, length), WIDE),
+            pltpu.VMEM((length, LANES), WIDE),
+            low,
+            pltpu.VMEM((2, length), WIDE),
+        ],
+        60e9,
+        20e6,
+        (ids, *queries, *keys, *values, *cotangents, *contexts, lse, *tables),
+    )
+    return result[0:4], result[4:8], result[8:12]
+
+
+def centred(block):
+    shifted = block - jnp.mean(block, axis=-1, keepdims=True)
+    spread = jnp.mean(shifted * shifted, axis=-1, keepdims=True)
+    scale = lax.rsqrt(spread + EPS_NORM)
+    return shifted * scale, scale
+
+
+def norm_back(standard, scale, gain, grad):
+    scaled = grad * gain
+    first = jnp.mean(scaled, axis=-1, keepdims=True)
+    second = jnp.mean(scaled * standard, axis=-1, keepdims=True)
+    return scale * (scaled - first - standard * second)
+
+
+def context_lanes(ids, j, side, width):
+    half = ids[2] ^ side
+    return pl.ds(pl.multiple_of(half * 4 * width + (ids[0] ^ j) * width, width), width)
+
+
+def mid_kernel(ids, c0, c1, c2, c3, merged, w0, w1, w2, w3, g_ctx, g_mid, ctx, mixed, middle, lifted):
+    width = c0.shape[1] // 2
+    for j, c in enumerate((c0, c1, c2, c3)):
+        for side in range(2):
+            ctx[:, context_lanes(ids, j, side, width)] = c[:, side * width : (side + 1) * width]
+    standard, _ = centred(ctx[...].astype(WIDE))
+    mixed[...] = (standard * g_ctx[...]).astype(LOW)
+    total = merged[...].astype(WIDE)
+    depth = w0.shape[0]
+    for k, w in enumerate((w0, w1, w2, w3)):
+        total = total + dot(mixed[:, own_block(ids[1], k, depth)], w[...], NN)
+    middle[...] = total
+    standard, _ = centred(total)
+    lifted[...] = (standard * g_mid[...]).astype(LOW)
+
+
+def mid_forward(ids, contexts, merged, weights, g_ctx, g_mid):
+    rows, model = merged.shape
+    block = min(256, rows)
+    line = lambda width: pl.BlockSpec((block, width), lambda b, ids: (b, 0))
+    gain = pl.BlockSpec((1, model), lambda b, ids: (0, 0))
+    weight = pl.BlockSpec(weights[0].shape, lambda b, ids: (0, 0), pipeline_mode=ONCE)
+    shape = lambda kind: jax.ShapeDtypeStruct((rows, model), kind)
+    return kernel_call(
+        mid_kernel,
+        (rows // block,),
+        [line(contexts[0].shape[1])] * 4 + [line(model)] + [weight] * 4 + [gain] * 2,
+        [line(model)] * 4,
+        [shape(LOW), shape(LOW), shape(WIDE), shape(LOW)],
+        [],
+        2 * rows * model * model,
+        2 * model * model + 14 * rows * model,
+        (ids, *contexts, merged, *weights, g_ctx, g_mid),
+    )
+
+
+def mid_back_kernel(
+    ids, a, r, middle, og, ctx, w0, w1, w2, w3, g_mid, g_ctx, middle_grad, middle_low, d0, d1, d2, d3, gains, mixed_grad
+):
+    grad = a[...].astype(WIDE) + r[...].astype(WIDE)
+    standard, scale = centred(middle[...])
+
+    @pl.when(pl.program_id(0) == 0)
+    def _():
+        gains[...] = jnp.zeros_like(gains)
+
+    gains[0:1, :] += jnp.sum(grad * standard, axis=0, keepdims=True)
+    total = og[...].astype(WIDE) + norm_back(standard, scale, g_mid[...], grad)
+    middle_grad[...] = total
+    low = total.astype(LOW)
+    middle_low[...] = low
+    depth = w0.shape[0]
+    for k, w in enumerate((w0, w1, w2, w3)):
+        mixed_grad[:, own_block(ids[1], k, depth)] = dot(low, w[...], NT)
+    grad = mixed_grad[...]
+    standard, scale = centred(ctx[...].astype(WIDE))
+    gains[1:2, :] += jnp.sum(grad * standard, axis=0, keepdims=True)
+    mixed_grad[...] = norm_back(standard, scale, g_ctx[...], grad)
+    width = d0.shape[1] // 2
+    for j, d in enumerate((d0, d1, d2, d3)):
+        for side in range(2):
+            d[:, side * width : (side + 1) * width] = mixed_grad[:, context_lanes(ids, j, side, width)].astype(LOW)
+
+
+def mid_backward(ids, parts, middle, og, ctx, weights, g_mid, g_ctx):
+    rows, model = middle.shape
+    block = min(256, rows)
+    line = lambda width: pl.BlockSpec((block, width), lambda b, ids: (b, 0))
+    gain = pl.BlockSpec((1, model), lambda b, ids: (0, 0))
+    weight = pl.BlockSpec(weights[0].shape, lambda b, ids: (0, 0), pipeline_mode=ONCE)
+    shape = lambda width, kind: jax.ShapeDtypeStruct((rows, width), kind)
+    result = kernel_call(
+        mid_back_kernel,
+        (rows // block,),
+        [line(model)] * 5 + [weight] * 4 + [gain] * 2,
+        [line(model)] * 2 + [line(model // 4)] * 4 + [pl.BlockSpec((8, model), lambda b, ids: (0, 0))],
+        [shape(model, WIDE), shape(model, LOW)]
+        + [shape(model // 4, LOW)] * 4
+        + [jax.ShapeDtypeStruct((8, model), WIDE)],
+        [pltpu.VMEM((block, model), WIDE)],
+        2 * rows * model * model,
+        2 * model * model + 18 * rows * model,
+        (ids, *parts, middle, og, ctx, *weights, g_mid, g_ctx),
+    )
+    return result[0], result[1], result[2:6], result[6]
+
+
+def gelu_parts(hidden):
+    share = 0.5 + 0.5 * lax.erf(hidden * 0.7071067811865476)
+    return hidden * share, share
+
+
+def gelu_slope(hidden, share):
+    return share + hidden * (0.3989422804014327 * jnp.exp(-0.5 * hidden * hidden))
+
+
+def fold(block):
+    out = block[:, :LANES]
+    for p in range(1, block.shape[1] // LANES):
+        out = out + block[:, p * LANES : (p + 1) * LANES]
+    return out
+
+
+def ffn_first_kernel(ids, x, og, u0, u1, u2, u3, d0, d1, d2, d3, gain, hidden, squashed_grad, sums, acc):
+    step = pl.program_id(0)
+    depth = u0.shape[0]
+    rows = x.shape[0]
+    part = rows // 2
+
+    @pl.when(step == 0)
+    def _():
+        acc[...] = jnp.zeros_like(acc)
+
+    for b in range(2):
+        here = slice(b * part, (b + 1) * part)
+        h = None
+        s = None
+        for k, (u, d) in enumerate(((u0, d0), (u1, d1), (u2, d2), (u3, d3))):
+            lanes = own_block(ids[1], k, depth)
+            one = dot(x[here, lanes], u[...], NN)
+            two = dot(og[here, lanes], d[...], NT)
+            h = one if h is None else h + one
+            s = two if s is None else s + two
+        h = h.astype(LOW)
+        s = s.astype(LOW)
+        hidden[here, :] = h
+        squashed_grad[here, :] = s
+        activated, _ = gelu_parts(h.astype(WIDE))
+        scaled = s.astype(WIDE) * gain[...]
+        acc[0, here, :] += fold(activated)
+        acc[1, here, :] += fold(activated * activated)
+        acc[2, here, :] += fold(scaled)
+        acc[3, here, :] += fold(scaled * activated)
+
+    @pl.when(step == pl.num_programs(0) - 1)
+    def _():
+        for n in range(4):
+            sums[n : n + 1, :] = jnp.sum(acc[n].T, axis=0, keepdims=True)
+        sums[4:8, :] = jnp.zeros_like(sums[4:8, :])
+
+
+def ffn_first(ids, x, og, upward, downward, gain):
+    rows, model = x.shape
+    units = upward[0].shape[1]
+    block = min(512, units)
+    line = pl.BlockSpec((rows, model), lambda u, ids: (0, 0), pipeline_mode=ONCE)
+    out = pl.BlockSpec((rows, block), lambda u, ids: (0, u))
+    return kernel_call(
+        ffn_first_kernel,
+        (units // block,),
+        [line] * 2
+        + [pl.BlockSpec((model // 4, block), lambda u, ids: (0, u))] * 4
+        + [pl.BlockSpec((block, model // 4), lambda u, ids: (u, 0))] * 4
+        + [pl.BlockSpec((1, block), lambda u, ids: (0, u))],
+        [out] * 2 + [pl.BlockSpec((8, rows), lambda u, ids: (0, 0))],
+        [jax.ShapeDtypeStruct((rows, units), LOW)] * 2 + [jax.ShapeDtypeStruct((8, rows), WIDE)],
+        [pltpu.VMEM((4, rows, LANES), WIDE)],
+        4 * rows * model * units,
+        4 * model * units + 4 * rows * (model + units),
+        (ids, x, og, *upward, *downward, gain),
+    )
+
+
+def ffn_second_kernel(ids, hidden, squashed_grad, sums, gain, u0, u1, u2, u3, squashed, hidden_grad, out, gains, acc, *, hidden_width):
+    step = pl.program_id(0)
+    depth = u0.shape[0]
+    rows = hidden.shape[0]
+    part = rows // 2
+
+    @pl.when(step == 0)
+    def _():
+        acc[...] = jnp.zeros_like(acc)
+
+    columns = sums[...].T
+    gain_sum = None
+    for b in range(2):
+        here = slice(b * part, (b + 1) * part)
+        centre = columns[here, 0:1] / hidden_width
+        scale = lax.rsqrt(columns[here, 1:2] / hidden_width - centre * centre + EPS_NORM)
+        mean_one = columns[here, 2:3] / hidden_width
+        mean_two = scale * (columns[here, 3:4] - centre * columns[here, 2:3]) / hidden_width
+        h = hidden[here, :].astype(WIDE)
+        activated, share = gelu_parts(h)
+        standard = (activated - centre) * scale
+        squashed[here, :] = (standard * gain[...]).astype(LOW)
+        s = squashed_grad[here, :].astype(WIDE)
+        piece = jnp.sum(s * standard, axis=0, keepdims=True)
+        gain_sum = piece if gain_sum is None else gain_sum + piece
+        activated_grad = (s * gain[...] - mean_one - standard * mean_two) * scale
+        grad = (activated_grad * gelu_slope(h, share)).astype(LOW)
+        hidden_grad[here, :] = grad
+        for k, u in enumerate((u0, u1, u2, u3)):
+            acc[here, own_block(ids[1], k, depth)] += dot(grad, u[...], NT)
+    gains[...] = jnp.broadcast_to(gain_sum, gains.shape)
+
+    @pl.when(step == pl.num_programs(0) - 1)
+    def _():
+        out[...] = acc[...].astype(LOW)
+
+
+def ffn_second(ids, hidden, squashed_grad, sums, gain, upward, hidden_width):
+    rows, units = hidden.shape
+    model = upward[0].shape[0] * 4
+    block = min(512, units)
+    line = pl.BlockSpec((rows, block), lambda u, ids: (0, u))
+    return kernel_call(
+        partial(ffn_second_kernel, hidden_width=hidden_width),
+        (units // block,),
+        [line] * 2
+        + [pl.BlockSpec((8, rows), lambda u, ids: (0, 0)), pl.BlockSpec((1, block), lambda u, ids: (0, u))]
+        + [pl.BlockSpec((model // 4, block), lambda u, ids: (0, u))] * 4,
+        [line] * 2
+        + [pl.BlockSpec((rows, model), lambda u, ids: (0, 0)), pl.BlockSpec((8, block), lambda u, ids: (0, u))],
+        [jax.ShapeDtypeStruct((rows, units), LOW)] * 2
+        + [jax.ShapeDtypeStruct((rows, model), LOW), jax.ShapeDtypeStruct((8, units), WIDE)],
+        [pltpu.VMEM((rows, model), WIDE)],
+        2 * rows * model * units,
+        2 * model * units + 8 * rows * units + 2 * rows * model,
+        (ids, hidden, squashed_grad, sums, gain, *upward),
+    )
+
+
+def spread_kernel(ids, x, w0, w1, w2, w3, out, acc):
+    step = pl.program_id(0)
+    depth = w0.shape[1]
+    for k, w in enumerate((w0, w1, w2, w3)):
+        lanes = own_block(ids[1], k, depth)
+        part = dot(x[...], w[...], NN)
+
+        @pl.when(step == 0)
+        def _():
+            acc[:, lanes] = part
+
+        @pl.when(step > 0)
+        def _():
+            acc[:, lanes] += part
+
+    @pl.when(step == pl.num_programs(0) - 1)
+    def _():
+        out[...] = acc[...].astype(LOW)
+
+
+def ffn_out(ids, x, downward):
+    rows, units = x.shape
+    model = downward[0].shape[1] * 4
+    block = min(512, units)
+    return kernel_call(
+        spread_kernel,
+        (units // block,),
+        [pl.BlockSpec((rows, block), lambda u, ids: (0, u))]
+        + [pl.BlockSpec((block, model // 4), lambda u, ids: (u, 0))] * 4,
+        [pl.BlockSpec((rows, model), lambda u, ids: (0, 0))],
+        [jax.ShapeDtypeStruct((rows, model), LOW)],
+        [pltpu.VMEM((rows, model), WIDE)],
+        2 * rows * model * units,
+        2 * model * units + 2 * rows * (units + model),
+        (ids, x, *downward),
+    )[0]
+
+
+def unproject_kernel(ids, q, k, v, w0, w1, w2, w3, out):
+    depth = w0.shape[1]
+    for n, w in enumerate((w0, w1, w2, w3)):
+        total = None
+        for f, g in enumerate((q, k, v)):
+            part = dot(g[...], w[f], NT)
+            total = part if total is None else total + part
+        out[:, own_block(ids[1], n, depth)] = total.astype(LOW)
+
+
+def unproject(ids, q, k, v, weights):
+    rows, width = q.shape
+    model = weights[0].shape[1] * 4
+    block = min(256, rows)
+    line = pl.BlockSpec((block, width), lambda b, ids: (b, 0))
+    return kernel_call(
+        unproject_kernel,
+        (rows // block,),
+        [line] * 3 + [pl.BlockSpec(weights[0].shape, lambda b, ids: (0, 0, 0), pipeline_mode=ONCE)] * 4,
+        [pl.BlockSpec((block, model), lambda b, ids: (b, 0))],
+        [jax.ShapeDtypeStruct((rows, model), LOW)],
+        [],
+        6 * rows * model * width,
+        6 * model * width + 2 * rows * (3 * width + model),
+        (ids, q, k, v, *weights),
+    )[0]
+
+
+def flip(value, axis, mask):
+    return lax.ppermute(value, axis, [(i, i ^ mask) for i in range(lax.axis_size(axis))])
+
+
+def flip_both(value, mask_dp, mask_mp):
+    count_mp = lax.axis_size("mp")
+    pairs = [
+        (d * count_mp + m, (d ^ mask_dp) * count_mp + (m ^ mask_mp))
+        for d in range(lax.axis_size("dp"))
+        for m in range(count_mp)
+    ]
+    return lax.ppermute(value, ("dp", "mp"), pairs)
+
+
+def gather_tokens(chunk):
+    across = flip(chunk, "mp", 2)
+    return [chunk, flip(chunk, "mp", 1), across, flip(across, "mp", 1)]
+
+
+def gather_weight(shard, x_first):
+    if x_first:
+        one = flip(shard, "dp", 1)
+        return [shard, one, flip(shard, "dp", 2), flip(one, "dp", 2)]
+    two = flip(shard, "dp", 2)
+    return [shard, flip(shard, "dp", 1), two, flip(two, "dp", 1)]
+
+
+def add_low(one, two):
+    return (one.astype(WIDE) + two.astype(WIDE)).astype(LOW)
+
+
+def scatter_grad(blocks, x_first):
+    if x_first:
+        kept = add_low(blocks[0], flip(blocks[1], "dp", 1))
+        passed = add_low(blocks[2], flip(blocks[3], "dp", 1))
+        return add_low(kept, flip(passed, "dp", 2))
+    kept = add_low(blocks[0], flip(blocks[2], "dp", 2))
+    passed = add_low(blocks[1], flip(blocks[3], "dp", 2))
+    return add_low(kept, flip(passed, "dp", 1))
+
+
+def scatter_tokens(parts):
+    passed = add_low(parts[2], flip(parts[3], "mp", 1))
+    kept = add_low(parts[0], flip(parts[1], "mp", 1))
+    return kept, flip(passed, "mp", 2)
+
+
+def sum_everywhere(value):
+    value = (value + flip(value, "mp", 1)) + (flip(value, "mp", 2) + flip(value, "mp", 3))
+    far = [flip_both(value, n // 2, 4 * (n % 2)) for n in range(1, 8)]
+    return ((value + far[0]) + (far[1] + far[2])) + ((far[3] + far[4]) + (far[5] + far[6]))
+
+
+def rotary_tables(length):
+    cosine, sine_part, exponent = xpos_tables(length, HEAD_DIM)
+    out = []
+    for polarity in (1.0, -1.0):
+        factor = jnp.exp(polarity * exponent)
+        near = (cosine * factor)[:, 0]
+        far = (sine_part * factor)[:, 0]
+        out.append(jnp.concatenate([near] * 4, axis=-1))
+        out.append(jnp.concatenate([-far, far, -far, far], axis=-1))
+    return out
+
+
+def on_device_paired(
+    text_states,
+    image_states,
+    image_offsets,
+    image_counts,
+    output_grad,
+    head_master,
+    head_moment,
+    head_square,
+    outward_master,
+    outward_moment,
+    outward_square,
+    upward_master,
+    upward_moment,
+    upward_square,
+    downward_master,
+    downward_moment,
+    downward_square,
+    gains_master,
+    gains_moment,
+    gains_square,
+):
+    model_rank = lax.axis_index("mp")
+    side = model_rank // 4
+    rank = model_rank % 4
+    place = lax.axis_index("dp")
+    ids = jnp.stack([rank, place, side]).astype(jnp.int32)
+    _, local_len, model_width = text_states.shape
+    length = local_len * 8
+    rows = 2 * local_len
+    hidden_local = upward_master.shape[1]
+    hidden_width = hidden_local * 8
+
+    def pick(value, index):
+        return lax.dynamic_index_in_dim(value, index, 0, keepdims=False)
+
+    def exchange(pair):
+        kept, got = pick(pair, side), flip(pick(pair, 1 - side), "mp", 4)
+        return jnp.where(side == 0, jnp.stack([kept, got]), jnp.stack([got, kept]))
+
+    tables = rotary_tables(length)
+    text = exchange(text_states)
+    head_low = head_master.astype(LOW)
+    head_shard = jnp.concatenate([head_low, flip(head_low, "mp", 4)], axis=2)
+    head_weight = gather_weight(head_shard, True)
+    cotangent = exchange(output_grad).reshape(rows, model_width)
+
+    outward_low = outward_master.astype(LOW)
+    core = rank % 2
+    half_width = model_width // 2
+    outward_half = lax.dynamic_slice_in_dim(outward_low, core * half_width, half_width, 1)
+    outward_own = gather_weight(outward_half, False)
+    outward_other = [flip(piece, "mp", 1) for piece in outward_own[1:]]
+    outward_weight = [outward_low] + [
+        jnp.where(
+            core == 0,
+            jnp.concatenate([own, other], axis=1),
+            jnp.concatenate([other, own], axis=1),
+        )
+        for own, other in zip(outward_own[1:], outward_other)
+    ]
+    upward_low = upward_master.astype(LOW)
+    upward_weight = gather_weight(jnp.concatenate([upward_low, flip(upward_low, "mp", 4)], axis=1), True)
+    downward_low = downward_master.astype(LOW)
+    downward_weight = gather_weight(jnp.concatenate([downward_low, flip(downward_low, "mp", 4)], axis=0), False)
+
+    gain_in = gains_master[None, :model_width]
+    gain_ctx = gains_master[None, model_width : 2 * model_width]
+    gain_mid = gains_master[None, 2 * model_width : 3 * model_width]
+    hidden_start = 3 * model_width + model_rank * hidden_local
+    other_start = 3 * model_width + (model_rank ^ 4) * hidden_local
+    gain_hidden = jnp.concatenate(
+        [
+            lax.dynamic_slice_in_dim(gains_master, hidden_start, hidden_local),
+            lax.dynamic_slice_in_dim(gains_master, other_start, hidden_local),
+        ]
+    )[None]
+
+    offsets = pick(image_offsets, side)
+    image_count = pick(image_counts, side)
+    position = (
+        jnp.arange(2, dtype=jnp.int32)[:, None] * (4 * local_len)
+        + rank * local_len
+        + jnp.arange(local_len, dtype=jnp.int32)[None, :]
+    ).reshape(rows)
+    slot_index = jnp.arange(offsets.shape[0], dtype=jnp.int32)
+    inside = (
+        (position[:, None] >= offsets[None, :])
+        & (position[:, None] < offsets[None, :] + PATCH)
+        & (slot_index[None, :] < image_count)
+    )
+    picked = jnp.sum(
+        jnp.where(inside, slot_index[None, :] * PATCH + position[:, None] - offsets[None, :], 0), axis=-1
+    )
+    covered = jnp.any(inside, axis=-1)
+    place_index = jnp.arange(image_states.shape[1], dtype=jnp.int32)
+    chosen = (covered[:, None] & (picked[:, None] == place_index[None, :])).astype(LOW)
+    images = jnp.dot(chosen, pick(image_states, side), preferred_element_type=WIDE).astype(LOW)
+    merged = jnp.where(covered[:, None], images, text.reshape(rows, model_width))
+
+    normed = gather_tokens(layer_norm(merged.astype(WIDE), gain_in).astype(LOW))
+    cotangents = gather_tokens(cotangent)
+    projected = [project(ids, chunk, head_weight, tables, j) for j, chunk in enumerate(normed)]
+    queries, keys, values = ([p[n] for p in projected] for n in range(3))
+    contexts, lse = attend(ids, queries, keys, values)
+    arrived = [contexts[0]] + [flip(contexts[j], "mp", j) for j in range(1, 4)]
+    context, mixed, middle, lifted_own = mid_forward(ids, arrived, merged, outward_weight, gain_ctx, gain_mid)
+    lifted = gather_tokens(lifted_own)
+    first = [ffn_first(ids, x, g, upward_weight, downward_weight, gain_hidden) for x, g in zip(lifted, cotangents)]
+    sums = jnp.stack([f[2] for f in first])
+    others = [flip(sums, "mp", k) for k in range(1, 4)]
+    whole_sums = [
+        (sums[j] + others[0][j ^ 1]) + (others[1][j ^ 2] + others[2][j ^ 3]) for j in range(4)
+    ]
+    second = [
+        ffn_second(ids, first[j][0], first[j][1], whole_sums[j], gain_hidden, upward_weight, hidden_width)
+        for j in range(4)
+    ]
+    lifted_parts = scatter_tokens([s[2] for s in second])
+    middle_grad, middle_low, context_grads, mid_gains = mid_backward(
+        ids, lifted_parts, middle, cotangent, context, outward_weight, gain_mid, gain_ctx
+    )
+    context_heads = [context_grads[0]] + [flip(context_grads[j], "mp", j) for j in range(1, 4)]
+    query_grads, key_grads, value_grads = attend_back(
+        ids, queries, keys, values, context_heads, contexts, lse, tables
+    )
+    normed_parts = [unproject(ids, *g, head_weight) for g in zip(query_grads, key_grads, value_grads)]
+    normed_kept, normed_got = scatter_tokens(normed_parts)
+    normed_grad = normed_kept.astype(WIDE) + normed_got.astype(WIDE)
+    _, input_back = jax.vjp(layer_norm, merged.astype(WIDE), gain_in)
+    merged_part, in_gain_grad = input_back(normed_grad)
+    input_rows = (middle_grad + merged_part).reshape(2, local_len, model_width)
+
+    ffn_kept, ffn_got = scatter_tokens([ffn_out(ids, s[0], downward_weight) for s in second])
+    output_rows = (
+        (middle + (ffn_kept.astype(WIDE) + ffn_got.astype(WIDE))).astype(LOW).reshape(2, local_len, model_width)
+    )
+
+    def give_back(pair):
+        kept = pick(pair, side)
+        got = flip(pick(pair, 1 - side).astype(LOW), "mp", 4).astype(pair.dtype)
+        return jnp.where(side == 0, jnp.stack([kept, got]), jnp.stack([got, kept]))
+
+    layer_output = give_back(output_rows)
+    input_grad = give_back(input_rows)
+
+    tokens = (((0,), (0,)), ((), ()))
+    squashed_rows = jnp.concatenate([s[0] for s in second])
+    hidden_grad_rows = jnp.concatenate([s[1] for s in second])
+    cotangent_rows = jnp.concatenate(cotangents)
+    lifted_rows = jnp.concatenate(lifted)
+    normed_rows = jnp.concatenate(normed)
+    quarter = model_width // 4
+
+    def lanes(value, k):
+        return lax.dynamic_slice_in_dim(value, (place ^ k) * quarter, quarter, 1)
+
+    down_grad = scatter_grad(
+        [dot(squashed_rows, lanes(cotangent_rows, k), tokens).astype(LOW) for k in range(4)], False
+    )
+    down_sum = down_grad[:hidden_local].astype(WIDE) + flip(down_grad[hidden_local:], "mp", 4).astype(WIDE)
+    up_grad = scatter_grad(
+        [dot(lanes(lifted_rows, k), hidden_grad_rows, tokens).astype(LOW) for k in range(4)], True
+    )
+    up_sum = up_grad[:, :hidden_local].astype(WIDE) + flip(up_grad[:, hidden_local:], "mp", 4).astype(WIDE)
+
+    outward_parts = [dot(lanes(mixed, k), middle_low, tokens).astype(LOW) for k in range(4)]
+    outward_parts = [
+        add_low(
+            lax.dynamic_slice_in_dim(part, core * half_width, half_width, 1),
+            flip(lax.dynamic_slice_in_dim(part, (1 - core) * half_width, half_width, 1), "mp", 1),
+        )
+        for part in outward_parts
+    ]
+    outward_grad = scatter_grad(outward_parts, False)
+    bits = ((2, (rank // 2) % 2), (4, side))
+    for mask, bit in bits:
+        size = outward_grad.shape[0] // 2
+        outward_grad = add_low(
+            lax.dynamic_slice_in_dim(outward_grad, bit * size, size, 0),
+            flip(lax.dynamic_slice_in_dim(outward_grad, (1 - bit) * size, size, 0), "mp", mask),
+        )
+    for mask, bit, axis in ((4, side, 0), (2, (rank // 2) % 2, 0), (1, core, 1)):
+        got = flip(outward_grad, "mp", mask)
+        outward_grad = jnp.where(
+            bit == 0,
+            jnp.concatenate([outward_grad, got], axis=axis),
+            jnp.concatenate([got, outward_grad], axis=axis),
+        )
+    outward_sum = outward_grad.astype(WIDE)
+
+    head_parts = [jnp.concatenate(g) for g in (query_grads, key_grads, value_grads)]
+    head_grad = scatter_grad(
+        [jnp.stack([dot(lanes(normed_rows, k), g, tokens).astype(LOW) for g in head_parts]) for k in range(4)], True
+    )
+    head_local = head_master.shape[2]
+    head_sum = head_grad[:, :, :head_local].astype(WIDE) + flip(head_grad[:, :, head_local:], "mp", 4).astype(WIDE)
+
+    moment_head, square_head, head_dir = adapt_step(head_sum, head_master, head_moment, head_square, DECAY_RATE)
+    moment_outward, square_outward, outward_dir = adapt_step(
+        outward_sum, outward_master, outward_moment, outward_square, DECAY_RATE
+    )
+    moment_upward, square_upward, upward_dir = adapt_step(
+        up_sum, upward_master, upward_moment, upward_square, DECAY_RATE
+    )
+    moment_downward, square_downward, downward_dir = adapt_step(
+        down_sum, downward_master, downward_moment, downward_square, DECAY_RATE
+    )
+    owner = (model_rank == 0).astype(WIDE)
+    norm_early = sum_everywhere(
+        jnp.concatenate(
+            [
+                pair_sums(outward_master, outward_dir) * owner,
+                pair_sums(upward_master, upward_dir),
+                pair_sums(downward_master, downward_dir),
+            ],
+            axis=0,
+        )
+    )
+    head_part = jnp.stack(
+        [jnp.sum(head_master * head_master, axis=(1, 2)), jnp.sum(head_dir * head_dir, axis=(1, 2))], axis=-1
+    )
+    hidden_gain = jnp.concatenate([s[3][0:1] for s in second], axis=0).sum(axis=0)
+    gains_part = jnp.concatenate([in_gain_grad[0], mid_gains[1], mid_gains[0], jnp.zeros((hidden_width,), WIDE)])
+    gains_part = lax.dynamic_update_slice(gains_part, hidden_gain[:hidden_local], (hidden_start,))
+    gains_part = lax.dynamic_update_slice(gains_part, hidden_gain[hidden_local:], (other_start,))
+    gains_sum = sum_everywhere(gains_part)
+    head_norms = sum_everywhere(head_part)
+    norm_sums = jnp.concatenate([head_norms, norm_early], axis=0)
+    moment_gains, square_gains, gains_dir = adapt_step(gains_sum, gains_master, gains_moment, gains_square, 0.0)
+    gains_sums = jnp.stack(
+        [
+            gain_segments(gains_master * gains_master, model_width),
+            gain_segments(gains_dir * gains_dir, model_width),
+        ],
+        axis=-1,
+    )
+    updated_head = trust_move(
+        head_master, head_dir, head_norms[:, 0][:, None, None], head_norms[:, 1][:, None, None]
+    )
+    updated_outward = trust_move(outward_master, outward_dir, norm_early[0, 0], norm_early[0, 1])
+    updated_upward = trust_move(upward_master, upward_dir, norm_early[1, 0], norm_early[1, 1])
+    updated_downward = trust_move(downward_master, downward_dir, norm_early[2, 0], norm_early[2, 1])
+    updated_gains = trust_move(
+        gains_master,
+        gains_dir,
+        gain_spread(gains_sums[:, 0], model_width, hidden_width),
+        gain_spread(gains_sums[:, 1], model_width, hidden_width),
+    )
+    update_norms = jnp.sqrt(jnp.concatenate([norm_sums, gains_sums], axis=0))
+    return (
+        layer_output,
+        input_grad,
+        moment_head,
+        square_head,
+        updated_head,
+        updated_head.astype(LOW),
+        moment_outward,
+        square_outward,
+        updated_outward,
+        updated_outward.astype(LOW),
+        moment_upward,
+        square_upward,
+        updated_upward,
+        updated_upward.astype(LOW),
+        moment_downward,
+        square_downward,
+        updated_downward,
+        updated_downward.astype(LOW),
+        moment_gains,
+        square_gains,
+        updated_gains,
+        update_norms,
+    )
+
+
 def solution(mesh):
+    paired = mesh.shape["dp"] == 4 and mesh.shape["mp"] == 8
     return jax.shard_map(
-        on_device,
+        on_device_paired if paired else on_device_general,
         mesh=mesh,
         in_specs=(
             P("dp", "mp", None),

time: 2560 us -> 1440 us (0.56)
  waiting for transfers between devices: 1220 us -> 588 us
  matrix products: 703 us -> 104 us
  Pallas kernels: 0 us -> 398 us
  other arithmetic: 370 us -> 160 us
  blocking collectives: 98.4 us -> 0 us
  starting transfers between devices: 8.04 us -> 101 us
  local copies, waits for them, and re-layouts: 114 us -> 72.9 us
    reduce_scatter x7 -> x0, waiting for transfers between devices: 673 us -> none  [the longest x1 295 us: on_device(): lax.psum_scatter(lifted_part, 'mp', scatter_dimension=1, tiled=True)]
    dot_general x40 -> x25, matrix products: 703 us -> 104 us  [the longest x24 102 us: dot(): return lax.dot_general(left, right, dims, preferred_element_type=WIDE)]
    ppermute x0 -> x103, waiting for transfers between devices: none -> 588 us  [the longest x82 543 us: flip(): lax.ppermute(value, axis, [(i, i ^ mask) for i in range(lax.axis_size(axi...]
    all_gather x7 -> x0, waiting for transfers between devices: 419 us -> none  [the longest x1 153 us: on_device(): lax.all_gather(normed_low, 'mp', axis=1, tiled=True)]
    pallas_call x0 -> x24, Pallas kernels: none -> 398 us  [kernel_call(): pl.pallas_call(body, grid_spec=pltpu.PrefetchScalarGridSpec(num_scalar_pr...]
    reduce_sum x10 -> x3, other arithmetic: 111 us -> 3.16 us  [the longest x1 2.12 us: on_device_paired(): jnp.sum(head_master * head_master, axis=(1, 2))]
    convert_element_type x15 -> x26, other arithmetic: 167 us -> 59.6 us  [the longest x16 30.4 us: add_low(): return (one.astype(WIDE) + two.astype(WIDE)).astype(LOW)]
    ppermute x0 -> x103, starting transfers between devices: none -> 101 us  [the longest x82 72.3 us: flip(): lax.ppermute(value, axis, [(i, i ^ mask) for i in range(lax.axis_size(axi...]
  transfers between devices with their start and end apart: 17 -> 103, of which waited for: 13 -> 39; matrix products, arithmetic and copies ran while one was open for 39% -> 14% of each run, Pallas kernels for 0% -> 23%
where the time goes in v1:
time: 1440 us; the launch traced here: 1430 us
  waiting for transfers between devices  588 us (41%)
  Pallas kernels  398 us (28%)
  other arithmetic  160 us (11%)
  matrix products  104 us (7%)
  starting transfers between devices  101 us (7%)
  local copies, waits for them, and re-layouts  72.9 us (5%)
    ppermute x82, waiting for transfers between devices, flip(): lax.ppermute(value, axis, [(i, i ^ mask) for i in range(lax.axis_size(axi...  543 us
    pallas_call x24, Pallas kernels, kernel_call(): pl.pallas_call(body, grid_spec=pltpu.PrefetchScalarGridSpec(num_scalar_pr...  398 us
    dot_general x24, matrix products, dot(): return lax.dot_general(left, right, dims, preferred_element_type=WIDE)  102 us
    ppermute x82, starting transfers between devices, flip(): lax.ppermute(value, axis, [(i, i ^ mask) for i in range(lax.axis_size(axi...  72.3 us
    ppermute x21, waiting for transfers between devices, flip_both(): return lax.ppermute(value, ('dp', 'mp'), pairs)  44.7 us
    unnamed x267, local copies, waits for them, and re-layouts  40.5 us
    convert_element_type x16, other arithmetic, add_low(): return (one.astype(WIDE) + two.astype(WIDE)).astype(LOW)  30.4 us
    ppermute x21, starting transfers between devices, flip_both(): return lax.ppermute(value, ('dp', 'mp'), pairs)  29 us
  transfers between devices with their start and end apart: 103, of which 39 were waited for; matrix products, arithmetic and copies ran while one was open for 14% of the time, Pallas kernels for 23%

profile of v1, /device:TPU:0, one launch (start us, length us, event | category | flops | bytes accessed | tf_op | source)
XLA Modules:
  0.0 1431.3 jit_solution(279573137310629039)
XLA Ops:
  24.7 78.4 %collective-permute-done = bf16[256,2048]{1,0:T(8,128)(2,1)} collective-permute-done((bf16[256,2048]{1,0:T(8,128)(2,1)}, bf16[256,2048]{1,0:T(8,128)(2,1)}, u32[]{:S(2)}, u32[]{:S(2)}) %collective-permute-start) | collective-permute-done | bytes 1048608 | tf_op jit(solution)/shard_map/ppermute | solution.py:1008
  127.5 15.1 %collective-permute-done.17 = bf16[256,2048]{1,0:T(8,128)(2,1)} collective-permute-done((bf16[256,2048]{1,0:T(8,128)(2,1)}, bf16[256,2048]{1,0:T(8,128)(2,1)}, u32[]{:S(2)}, u32[]{:S(2)}) %collective-permute-start.17) | collective-permute-done | bytes 1048608 | tf_op jit(solution)/shard_map/ppermute | solution.py:1008
  147.4 62.5 %collective-permute-done.18 = bf16[512,1024]{1,0:T(8,128)(2,1)} collective-permute-done((bf16[512,1024]{1,0:T(8,128)(2,1)}, bf16[512,1024]{1,0:T(8,128)(2,1)}, u32[]{:S(2)}, u32[]{:S(2)}) %collective-permute-start.18) | collective-permute-done | bytes 1048608 | tf_op jit(solution)/shard_map/ppermute | solution.py:1008
  213.0 18.3 %collective-permute-done.22 = bf16[1024,512]{1,0:T(8,128)(2,1)} collective-permute-done((bf16[1024,512]{1,0:T(8,128)(2,1)}, bf16[1024,512]{1,0:T(8,128)(2,1)}, u32[]{:S(2)}, u32[]{:S(2)}) %collective-permute-start.22) | collective-permute-done | bytes 1048608 | tf_op jit(solution)/shard_map/ppermute | solution.py:1008
  251.8 16.8 %collective-permute-done.3.w2 = bf16[3,512,512]{2,1,0:T(8,128)(2,1)S(1)} collective-permute-done((bf16[3,512,512]{2,1,0:T(8,128)(2,1)S(1)}, bf16[3,512,512]{2,1,0:T(8,128)(2,1)S(1)}, u32[]{:S(2)}, u32[]{:S(2)}) %collective-permute-start.3) | collective-permute-done | bytes 1572896 | tf_op jit(solution)/shard_map/ppermute | solution.py:1008
  268.6 31.6 %collective-permute-done.4.w3 = bf16[3,512,512]{2,1,0:T(8,128)(2,1)S(1)} collective-permute-done((bf16[3,512,512]{2,1,0:T(8,128)(2,1)S(1)}, bf16[3,512,512]{2,1,0:T(8,128)(2,1)S(1)}, u32[]{:S(2)}, u32[]{:S(2)}) %collective-permute-start.4) | collective-permute-done | bytes 1572896 | tf_op jit(solution)/shard_map/ppermute | solution.py:1008
  338.7 43.1 %shard_map.367 = (bf16[512,512]{1,0:T(8,128)(2,1)}, bf16[512,512]{1,0:T(8,128)(2,1)}, bf16[512,512]{1,0:T(8,128)(2,1)}, bf16[512,512]{1,0:T(8,128)(2,1)}, f32[4,2,2048]{2,1,0:T(2,128)}) custom-call(s32[3]{0:T(128)} %pad_add_fusion.ids, bf16[512,512]{1,0:T(8,128)(2,1)} %get-tuple-element.90.refs_0_, bf16[512,512]{1,0:T(8,128)(2,1)} %get-tuple-element.91.refs_1_, ...), custom_call_target="tpu_custom_call" | custom-call | flops 40000000000 | bytes 10000000 | tf_op jit(solution)/shard_map/pallas_call | solution.py:462
  383.7 35.9 %collective-permute-done.24.d2.w2 = bf16[2048,512]{1,0:T(8,128)(2,1)} collective-permute-done((bf16[2048,512]{1,0:T(8,128)(2,1)S(1)}, bf16[2048,512]{1,0:T(8,128)(2,1)}, u32[]{:S(2)}, u32[]{:S(2)}) %collective-permute-start.24) | collective-permute-done | bytes 2097184 | tf_op jit(solution)/shard_map/ppermute | solution.py:1008
  478.8 43.5 %collective-permute-done.25.d3.w3 = bf16[2048,512]{1,0:T(8,128)(2,1)} collective-permute-done((bf16[2048,512]{1,0:T(8,128)(2,1)}, bf16[2048,512]{1,0:T(8,128)(2,1)}, u32[]{:S(2)}, u32[]{:S(2)}) %collective-permute-start.25) | collective-permute-done | bytes 2097184 | tf_op jit(solution)/shard_map/ppermute | solution.py:1008
  522.3 17.2 %shard_map.369 = (bf16[512,2048]{1,0:T(8,128)(2,1)}, bf16[512,2048]{1,0:T(8,128)(2,1)}, f32[8,512]{1,0:T(8,128)}) custom-call(s32[3]{0:T(128)} %pad_add_fusion.ids, bf16[512,2048]{1,0:T(8,128)(2,1)} %get-tuple-element.107.x, bf16[512,2048]{1,0:T(8,128)(2,1)} %bitcast.14.og, bf16[512,2048]{1,0:T(8,128)(2,1)} %pad_maximum_fusion.2.u0, ...), custom_call_target="tpu_custom_call" | custom-call | flops 8589934592 | bytes 25165824 | tf_op jit(solution)/shard_map/pallas_call | solution.py:462
  544.7 17.1 %shard_map.370 = (bf16[512,2048]{1,0:T(8,128)(2,1)}, bf16[512,2048]{1,0:T(8,128)(2,1)}, f32[8,512]{1,0:T(8,128)}) custom-call(s32[3]{0:T(128)} %pad_add_fusion.ids, bf16[512,2048]{1,0:T(8,128)(2,1)} %copy-done.62, bf16[512,2048]{1,0:T(8,128)(2,1)} %copy-done.68, bf16[512,2048]{1,0:T(8,128)(2,1)} %pad_maximum_fusion.2.u0, ...), custom_call_target="tpu_custom_call" | custom-call | flops 8589934592 | bytes 25165824 | tf_op jit(solution)/shard_map/pallas_call | solution.py:462
  561.8 17.3 %shard_map.371 = (bf16[512,2048]{1,0:T(8,128)(2,1)}, bf16[512,2048]{1,0:T(8,128)(2,1)}, f32[8,512]{1,0:T(8,128)}) custom-call(s32[3]{0:T(128)} %pad_add_fusion.ids, bf16[512,2048]{1,0:T(8,128)(2,1)} %collective-permute-done.28.x, bf16[512,2048]{1,0:T(8,128)(2,1)} %collective-permute-done.29.og, bf16[512,2048]{1,0:T(8,128)(2,1)} %pad_maximum_fusion.2.u0, ...), custom_call_target="tpu_custom_call" | custom-call | flops 8589934592 | bytes 25165824 | tf_op jit(solution)/shard_map/pallas_call | solution.py:462
  580.5 17.1 %shard_map.372 = (bf16[512,2048]{1,0:T(8,128)(2,1)}, bf16[512,2048]{1,0:T(8,128)(2,1)}, f32[8,512]{1,0:T(8,128)}) custom-call(s32[3]{0:T(128)} %pad_add_fusion.ids, bf16[512,2048]{1,0:T(8,128)(2,1)} %copy-done.63, bf16[512,2048]{1,0:T(8,128)(2,1)} %collective-permute-done.31.og, bf16[512,2048]{1,0:T(8,128)(2,1)} %pad_maximum_fusion.2.u0, ...), custom_call_target="tpu_custom_call" | custom-call | flops 8589934592 | bytes 25165824 | tf_op jit(solution)/shard_map/pallas_call | solution.py:462
  639.7 14.7 %shard_map.377 = (bf16[512,2048]{1,0:T(8,128)(2,1)}, bf16[512,2048]{1,0:T(8,128)(2,1)}, bf16[512,2048]{1,0:T(8,128)(2,1)}, f32[8,2048]{1,0:T(8,128)}) custom-call(s32[3]{0:T(128)} %pad_add_fusion.ids, bf16[512,2048]{1,0:T(8,128)(2,1)} %get-tuple-element.118.hidden, bf16[512,2048]{1,0:T(8,128)(2,1)} %get-tuple-element.119.squashed_grad, ...), custom_call_target="tpu_custom_call" | custom-call | flops 4294967296 | bytes 18874368 | tf_op jit(solution)/shard_map/pallas_call | solution.py:462
  820.4 31.8 %collective-permute-done.41.r = bf16[512,2048]{1,0:T(8,128)(2,1)S(1)} collective-permute-done((bf16[512,2048]{1,0:T(8,128)(2,1)S(1)}, bf16[512,2048]{1,0:T(8,128)(2,1)S(1)}, u32[]{:S(2)}, u32[]{:S(2)}) %collective-permute-start.41) | collective-permute-done | bytes 2097184 | tf_op jit(solution)/shard_map/ppermute | solution.py:1008
  853.5 19.4 %shard_map.381 = (f32[512,2048]{1,0:T(8,128)}, bf16[512,2048]{1,0:T(8,128)(2,1)}, bf16[512,512]{1,0:T(8,128)(2,1)}, bf16[512,512]{1,0:T(8,128)(2,1)}, bf16[512,5...) custom-call(s32[3]{0:T(128)} %pad_add_fusion.ids, bf16[512,2048]{1,0:T(8,128)(2,1)} %add_convert_fusion.9.a, ...), custom_call_target="tpu_custom_call" | custom-call | flops 4294967296 | bytes 27262976 | tf_op jit(solution)/shard_map/pallas_call | solution.py:462
  880.3 22.4 %collective-permute-done.79 = bf16[2048,512]{1,0:T(8,128)(2,1)} collective-permute-done((bf16[2048,512]{1,0:T(8,128)(2,1)}, bf16[2048,512]{1,0:T(8,128)(2,1)}, u32[]{:S(2)}, u32[]{:S(2)}) %collective-permute-start.79) | collective-permute-done | bytes 2097184 | tf_op jit(solution)/shard_map/ppermute | solution.py:1008
  936.2 16.8 %collective-permute-done.44.refs_15_ = bf16[512,512]{1,0:T(8,128)(2,1)S(1)} collective-permute-done((bf16[512,512]{1,0:T(8,128)(2,1)S(1)}, bf16[512,512]{1,0:T(8,128)(2,1)S(1)}, u32[]{:S(2)}, u32[]{:S(2)}) %collective-permute-start.44) | collective-permute-done | bytes 524320 | tf_op jit(solution)/shard_map/ppermute | solution.py:1008
  953.8 75.8 %shard_map.382 = (bf16[512,512]{1,0:T(8,128)(2,1)}, bf16[512,512]{1,0:T(8,128)(2,1)}, bf16[512,512]{1,0:T(8,128)(2,1)}, bf16[512,512]{1,0:T(8,128)(2,1)}, bf16[5...) custom-call(s32[3]{0:T(128)} %pad_add_fusion.ids, ...), custom_call_target="tpu_custom_call" | custom-call | flops 60000002048 | bytes 20000000 | tf_op jit(solution)/shard_map/pallas_call | solution.py:462
  1149.2 17.2 %collective-permute-done.69 = bf16[512,1024]{1,0:T(8,128)(2,1)S(1)} collective-permute-done((bf16[512,1024]{1,0:T(8,128)(2,1)S(1)}, bf16[512,1024]{1,0:T(8,128)(2,1)S(1)}, u32[]{:S(2)}, u32[]{:S(2)}) %collective-permute-start.69) | collective-permute-done | bytes 1048608 | tf_op jit(solution)/shard_map/ppermute | solution.py:1008
  1182.7 16.9 %collective-permute-done.49 = bf16[3,512,512]{2,1,0:T(8,128)(2,1)S(1)} collective-permute-done((bf16[3,512,512]{2,1,0:T(8,128)(2,1)S(1)}, bf16[3,512,512]{2,1,0:T(8,128)(2,1)S(1)}, u32[]{:S(2)}, u32[]{:S(2)}) %collective-permute-start.49) | collective-permute-done | bytes 1572896 | tf_op jit(solution)/shard_map/ppermute | solution.py:1008
  1209.7 38.7 %collective-permute-done.72 = bf16[128,1024]{1,0:T(8,128)(2,1)S(1)} collective-permute-done((bf16[128,1024]{1,0:T(8,128)(2,1)S(1)}, bf16[128,1024]{1,0:T(8,128)(2,1)S(1)}, u32[]{:S(2)}, u32[]{:S(2)}) %collective-permute-start.72) | collective-permute-done | bytes 262176 | tf_op jit(solution)/shard_map/ppermute | solution.py:1008
  1253.8 31.3 %collective-permute-done.54 = f32[3,2]{0,1:T(2,128)S(1)} collective-permute-done((f32[3,2]{0,1:T(2,128)S(1)}, f32[3,2]{0,1:T(2,128)S(1)}, u32[]{:S(2)}, u32[]{:S(2)}) %collective-permute-start.54) | collective-permute-done | bytes 56 | tf_op jit(solution)/shard_map/ppermute | solution.py:1008
  1331.7 24.2 %collective-permute-done.98 = f32[14336]{0:T(1024)S(1)} collective-permute-done((f32[14336]{0:T(1024)S(1)}, f32[14336]{0:T(1024)S(1)}, u32[]{:S(2)}, u32[]{:S(2)}) %collective-permute-start.98) | collective-permute-done | bytes 57376 | tf_op jit(solution)/shard_map/ppermute | solution.py:1018
  (634 shorter events, 701.1 us)
Async XLA Ops:
  7.0 116.4 %collective-permute-start.13 = (bf16[512,1024]{1,0:T(8,128)(2,1)}, bf16[512,1024]{1,0:T(8,128)(2,1)}, u32[]{:S(2)}, u32[]{:S(2)}) collective-permute-start(bf16[512,1024]{1,0:T(8,128)(2,1)} %constant_dynamic-slice_fusion.9), channel_id=1, source_target_pairs={{0,16},{8,24},{16,0},{24,8},{1,17},{9,25},{17,1},{25,9},{2,18},{10... | collective-permute-start | bytes 3145736 | tf_op jit(solution)/shard_map/ppermute | solution.py:1008
  9.9 115.4 %collective-permute-start.11 = (bf16[512,1024]{1,0:T(8,128)(2,1)}, bf16[512,1024]{1,0:T(8,128)(2,1)}, u32[]{:S(2)}, u32[]{:S(2)}) collective-permute-start(bf16[512,1024]{1,0:T(8,128)(2,1)} %constant_dynamic-slice_fusion.9), channel_id=1, source_target_pairs={{0,8},{8,0},{16,24},{24,16},{1,9},{9,1},{17,25},{25,17},{2,10},{10... | collective-permute-start | bytes 3145736 | tf_op jit(solution)/shard_map/ppermute | solution.py:1008
  14.6 88.5 %collective-permute-start = (bf16[256,2048]{1,0:T(8,128)(2,1)}, bf16[256,2048]{1,0:T(8,128)(2,1)}, u32[]{:S(2)}, u32[]{:S(2)}) collective-permute-start(bf16[256,2048]{1,0:T(8,128)(2,1)} %get-tuple-element.200), channel_id=1, source_target_pairs={{0,4},{1,5},{2,6},{3,7},{4,0},{5,1},{6,2},{7,3},{8,12},{9,13},{10,... | collective-permute-start | bytes 3145736 | tf_op jit(solution)/shard_map/ppermute | solution.py:1008
  18.2 101.9 %collective-permute-start.1 = (bf16[3,512,256]{2,1,0:T(8,128)(2,1)}, bf16[3,512,256]{2,1,0:T(8,128)(2,1)}, u32[]{:S(2)}, u32[]{:S(2)}) collective-permute-start(bf16[3,512,256]{2,1,0:T(8,128)(2,1)} %convert_element_type.372), channel_id=1, source_target_pairs={{0,4},{1,5},{2,6},{3,7},{4,0},{5,1},{6,2},{7,3},{8,12},{9,13},{10,... | collective-permute-start | bytes 2359304 | tf_op jit(solution)/shard_map/ppermute | solution.py:1008
  20.0 122.6 %collective-permute-start.17 = (bf16[256,2048]{1,0:T(8,128)(2,1)}, bf16[256,2048]{1,0:T(8,128)(2,1)}, u32[]{:S(2)}, u32[]{:S(2)}) collective-permute-start(bf16[256,2048]{1,0:T(8,128)(2,1)} %get-tuple-element.198), channel_id=1, source_target_pairs={{0,4},{1,5},{2,6},{3,7},{4,0},{5,1},{6,2},{7,3},{8,12},{9,13},{10,... | collective-permute-start | bytes 3145736 | tf_op jit(solution)/shard_map/ppermute | solution.py:1008
  110.6 126.3 %collective-permute-start.6 = (bf16[512,2048]{1,0:T(8,128)(2,1)}, bf16[512,2048]{1,0:T(8,128)(2,1)}, u32[]{:S(2)}, u32[]{:S(2)}) collective-permute-start(bf16[512,2048]{1,0:T(8,128)(2,1)} %fusion.6.x), channel_id=1, source_target_pairs={{0,2},{1,3},{2,0},{3,1},{4,6},{5,7},{6,4},{7,5},{8,10},{9,11},{10,... | collective-permute-start | bytes 6291464 | tf_op jit(solution)/shard_map/ppermute | solution.py:1008
  121.6 110.1 %collective-permute-start.2 = (bf16[3,512,512]{2,1,0:T(8,128)(2,1)S(1)}, bf16[3,512,512]{2,1,0:T(8,128)(2,1)S(1)}, u32[]{:S(2)}, u32[]{:S(2)}) collective-permute-start(bf16[3,512,512]{2,1,0:T(8,128)(2,1)S(1)} %pad_maximum_fusion.4.w0), channel_id=1, source_target_pairs={{0,8},{8,0},{16,24},{24,16},{1,9},{9,1},{17,25},{25,17},{2,10},{10... | collective-permute-start | bytes 4718600 | tf_op jit(solution)/shard_map/ppermute | solution.py:1008
  125.3 106.0 %collective-permute-start.22 = (bf16[1024,512]{1,0:T(8,128)(2,1)}, bf16[1024,512]{1,0:T(8,128)(2,1)}, u32[]{:S(2)}, u32[]{:S(2)}) collective-permute-start(bf16[1024,512]{1,0:T(8,128)(2,1)} %convert_element_type.375), channel_id=1, source_target_pairs={{0,4},{1,5},{2,6},{3,7},{4,0},{5,1},{6,2},{7,3},{8,12},{9,13},{10,... | collective-permute-start | bytes 3145736 | tf_op jit(solution)/shard_map/ppermute | solution.py:1008
  142.6 91.3 %collective-permute-start.15 = (bf16[512,1024]{1,0:T(8,128)(2,1)}, bf16[512,1024]{1,0:T(8,128)(2,1)}, u32[]{:S(2)}, u32[]{:S(2)}) collective-permute-start(bf16[512,1024]{1,0:T(8,128)(2,1)} %collective-permute-done.13), channel_id=1, source_target_pairs={{0,8},{8,0},{16,24},{24,16},{1,9},{9,1},{17,25},{25,17},{2,10},{10... | collective-permute-start | bytes 3145736 | tf_op jit(solution)/shard_map/ppermute | solution.py:1008
  236.9 90.9 %collective-permute-start.7 = (bf16[512,2048]{1,0:T(8,128)(2,1)}, bf16[512,2048]{1,0:T(8,128)(2,1)}, u32[]{:S(2)}, u32[]{:S(2)}) collective-permute-start(bf16[512,2048]{1,0:T(8,128)(2,1)} %collective-permute-done.6.x), channel_id=1, source_target_pairs={{0,1},{1,0},{2,3},{3,2},{4,5},{5,4},{6,7},{7,6},{8,9},{9,8},{10,11... | collective-permute-start | bytes 6291464 | tf_op jit(solution)/shard_map/ppermute | solution.py:1008
  240.6 97.9 %collective-permute-start.29 = (bf16[512,2048]{1,0:T(8,128)(2,1)}, bf16[512,2048]{1,0:T(8,128)(2,1)}, u32[]{:S(2)}, u32[]{:S(2)}) collective-permute-start(bf16[512,2048]{1,0:T(8,128)(2,1)} %bitcast.14.og), channel_id=1, source_target_pairs={{0,2},{1,3},{2,0},{3,1},{4,6},{5,7},{6,4},{7,5},{8,10},{9,11},{10,... | collective-permute-start | bytes 6291464 | tf_op jit(solution)/shard_map/ppermute | solution.py:1008
  327.8 91.7 %collective-permute-start.20 = (bf16[512,2048]{1,0:T(8,128)(2,1)S(1)}, bf16[512,2048]{1,0:T(8,128)(2,1)}, u32[]{:S(2)}, u32[]{:S(2)}) collective-permute-start(bf16[512,2048]{1,0:T(8,128)(2,1)S(1)} %copy-done.54), channel_id=1, source_target_pairs={{0,16},{8,24},{16,0},{24,8},{1,17},{9,25},{17,1},{25,9},{2,18},{10... | collective-permute-start | bytes 6291464 | tf_op jit(solution)/shard_map/ppermute | solution.py:1008
  336.9 113.2 %collective-permute-start.27 = (bf16[512,2048]{1,0:T(8,128)(2,1)}, bf16[512,2048]{1,0:T(8,128)(2,1)S(1)}, u32[]{:S(2)}, u32[]{:S(2)}) collective-permute-start(bf16[512,2048]{1,0:T(8,128)(2,1)} %bitcast.14.og), channel_id=1, source_target_pairs={{0,1},{1,0},{2,3},{3,2},{4,5},{5,4},{6,7},{7,6},{8,9},{9,8},{10,11... | collective-permute-start | bytes 6291464 | tf_op jit(solution)/shard_map/ppermute | solution.py:1008
  338.6 112.9 %collective-permute-start.31 = (bf16[512,2048]{1,0:T(8,128)(2,1)}, bf16[512,2048]{1,0:T(8,128)(2,1)}, u32[]{:S(2)}, u32[]{:S(2)}) collective-permute-start(bf16[512,2048]{1,0:T(8,128)(2,1)} %collective-permute-done.29.og), channel_id=1, source_target_pairs={{0,1},{1,0},{2,3},{3,2},{4,5},{5,4},{6,7},{7,6},{8,9},{9,8},{10,11... | collective-permute-start | bytes 6291464 | tf_op jit(solution)/shard_map/ppermute | solution.py:1008
  434.1 88.2 %collective-permute-start.25 = (bf16[2048,512]{1,0:T(8,128)(2,1)}, bf16[2048,512]{1,0:T(8,128)(2,1)}, u32[]{:S(2)}, u32[]{:S(2)}) collective-permute-start(bf16[2048,512]{1,0:T(8,128)(2,1)} %collective-permute-done.24.d2.w2), channel_id=1, source_target_pairs={{0,8},{8,0},{16,24},{24,16},{1,9},{9,1},{17,25},{25,17},{2,10},{10... | collective-permute-start | bytes 6291464 | tf_op jit(solution)/shard_map/ppermute | solution.py:1008
  813.6 89.0 %collective-permute-start.79 = (bf16[2048,512]{1,0:T(8,128)(2,1)}, bf16[2048,512]{1,0:T(8,128)(2,1)}, u32[]{:S(2)}, u32[]{:S(2)}) collective-permute-start(bf16[2048,512]{1,0:T(8,128)(2,1)} %convolution_convert_fusion.2), channel_id=1, source_target_pairs={{0,16},{8,24},{16,0},{24,8},{1,17},{9,25},{17,1},{25,9},{2,18},{10... | collective-permute-start | bytes 6291464 | tf_op jit(solution)/shard_map/ppermute | solution.py:1008
  814.3 88.9 %collective-permute-start.81 = (bf16[2048,512]{1,0:T(8,128)(2,1)S(1)}, bf16[2048,512]{1,0:T(8,128)(2,1)}, u32[]{:S(2)}, u32[]{:S(2)}) collective-permute-start(bf16[2048,512]{1,0:T(8,128)(2,1)S(1)} %add_convert_fusion.1), channel_id=1, source_target_pairs={{0,8},{8,0},{16,24},{24,16},{1,9},{9,1},{17,25},{25,17},{2,10},{10... | collective-permute-start | bytes 6291464 | tf_op jit(solution)/shard_map/ppermute | solution.py:1008
  919.3 187.4 %collective-permute-start.64 = (bf16[512,1024]{1,0:T(8,128)(2,1)}, bf16[512,1024]{1,0:T(8,128)(2,1)}, u32[]{:S(2)}, u32[]{:S(2)}) collective-permute-start(bf16[512,1024]{1,0:T(8,128)(2,1)} %constant_dynamic-slice_fusion.4), channel_id=1, source_target_pairs={{0,1},{1,0},{2,3},{3,2},{4,5},{5,4},{6,7},{7,6},{8,9},{9,8},{10,11... | collective-permute-start | bytes 3145736 | tf_op jit(solution)/shard_map/ppermute | solution.py:1008
  921.5 169.3 %collective-permute-start.67 = (bf16[512,1024]{1,0:T(8,128)(2,1)}, bf16[512,1024]{1,0:T(8,128)(2,1)}, u32[]{:S(2)}, u32[]{:S(2)}) collective-permute-start(bf16[512,1024]{1,0:T(8,128)(2,1)} %constant_dynamic-slice_fusion.2), channel_id=1, source_target_pairs={{0,1},{1,0},{2,3},{3,2},{4,5},{5,4},{6,7},{7,6},{8,9},{9,8},{10,11... | collective-permute-start | bytes 3145736 | tf_op jit(solution)/shard_map/ppermute | solution.py:1008
  928.1 181.9 %collective-permute-start.66 = (bf16[512,1024]{1,0:T(8,128)(2,1)}, bf16[512,1024]{1,0:T(8,128)(2,1)}, u32[]{:S(2)}, u32[]{:S(2)}) collective-permute-start(bf16[512,1024]{1,0:T(8,128)(2,1)} %constant_dynamic-slice_fusion.3), channel_id=1, source_target_pairs={{0,1},{1,0},{2,3},{3,2},{4,5},{5,4},{6,7},{7,6},{8,9},{9,8},{10,11... | collective-permute-start | bytes 3145736 | tf_op jit(solution)/shard_map/ppermute | solution.py:1008
  932.8 190.7 %collective-permute-start.78 = (bf16[512,1024]{1,0:T(8,128)(2,1)}, bf16[512,1024]{1,0:T(8,128)(2,1)}, u32[]{:S(2)}, u32[]{:S(2)}) collective-permute-start(bf16[512,1024]{1,0:T(8,128)(2,1)} %slice.203), channel_id=1, source_target_pairs={{0,4},{1,5},{2,6},{3,7},{4,0},{5,1},{6,2},{7,3},{8,12},{9,13},{10,... | collective-permute-start | bytes 3145736 | tf_op jit(solution)/shard_map/ppermute | solution.py:1008
  953.0 172.1 %collective-permute-start.38 = (bf16[256,2048]{1,0:T(8,128)(2,1)}, bf16[256,2048]{1,0:T(8,128)(2,1)}, u32[]{:S(2)}, u32[]{:S(2)}) collective-permute-start(bf16[256,2048]{1,0:T(8,128)(2,1)} %get-tuple-element.196), channel_id=1, source_target_pairs={{0,4},{1,5},{2,6},{3,7},{4,0},{5,1},{6,2},{7,3},{8,12},{9,13},{10,... | collective-permute-start | bytes 3145736 | tf_op jit(solution)/shard_map/ppermute | solution.py:1008
  1144.0 165.1 %collective-permute-start.45 = (bf16[512,2048]{1,0:T(8,128)(2,1)S(1)}, bf16[512,2048]{1,0:T(8,128)(2,1)S(1)}, u32[]{:S(2)}, u32[]{:S(2)}) collective-permute-start(bf16[512,2048]{1,0:T(8,128)(2,1)S(1)} %copy-done.108), channel_id=1, source_target_pairs={{0,1},{1,0},{2,3},{3,2},{4,5},{5,4},{6,7},{7,6},{8,9},{9,8},{10,11... | collective-permute-start | bytes 6291464 | tf_op jit(solution)/shard_map/ppermute | solution.py:1008
  1206.4 102.7 %collective-permute-start.47 = (bf16[512,2048]{1,0:T(8,128)(2,1)S(1)}, bf16[512,2048]{1,0:T(8,128)(2,1)S(1)}, u32[]{:S(2)}, u32[]{:S(2)}) collective-permute-start(bf16[512,2048]{1,0:T(8,128)(2,1)S(1)} %add_convert_fusion.6), channel_id=1, source_target_pairs={{0,2},{1,3},{2,0},{3,1},{4,6},{5,7},{6,4},{7,5},{8,10},{9,11},{10,... | collective-permute-start | bytes 6291464 | tf_op jit(solution)/shard_map/ppermute | solution.py:1008
  (203 other events, 4354.9 us)

commit v2 on v1

--- a/solution.py
+++ b/solution.py
@@ -445,6 +445,7 @@
     )
 
 
+SHARE = 0.3
 LOG2E = 1.4426950408889634
 LANES = 128
 NT = (((1,), (1,)), ((), ()))
@@ -466,7 +467,7 @@
         ),
         out_shape=out_shape,
         compiler_params=pltpu.CompilerParams(vmem_limit_bytes=56 << 20),
-        cost_estimate=pl.CostEstimate(flops=int(flops), bytes_accessed=int(moved), transcendentals=0),
+        cost_estimate=pl.CostEstimate(flops=int(flops * SHARE), bytes_accessed=int(moved * SHARE), transcendentals=0),
     )(*operands)
 
 
@@ -499,18 +500,28 @@
             out[:, here] = block.astype(LOW)
 
 
-def project(ids, x, weights, tables, j):
+def quarters(weight):
+    if isinstance(weight, list):
+        spec = pl.BlockSpec(weight[0].shape, lambda b, ids: (0, 0, 0), pipeline_mode=ONCE)
+        return weight, [spec] * 4
+    kinds, model, width = weight.shape
+    return [weight] * 4, [
+        pl.BlockSpec((kinds, model // 4, width), partial(lambda n, b, ids: (0, ids[1] ^ n, 0), n), pipeline_mode=ONCE)
+        for n in range(4)
+    ]
+
+
+def project(ids, x, weight, tables, j):
     rows, model = x.shape
     sub = rows // 2
+    weights, specs = quarters(weight)
     width = weights[0].shape[2]
     table = pl.BlockSpec((sub, LANES), lambda b, ids: (b * 4 + (ids[0] ^ j), 0))
     out = pl.BlockSpec((sub, width), lambda b, ids: (b, 0))
     return kernel_call(
         project_kernel,
         (2,),
-        [pl.BlockSpec((sub, model), lambda b, ids: (b, 0))]
-        + [pl.BlockSpec(weights[0].shape, lambda b, ids: (0, 0, 0), pipeline_mode=ONCE)] * 4
-        + [table] * 4,
+        [pl.BlockSpec((sub, model), lambda b, ids: (b, 0))] + specs + [table] * 4,
         [out] * 3,
         [jax.ShapeDtypeStruct((rows, width), LOW)] * 3,
         [],
@@ -716,33 +727,45 @@
     return pl.ds(pl.multiple_of(half * 4 * width + (ids[0] ^ j) * width, width), width)
 
 
-def mid_kernel(ids, c0, c1, c2, c3, merged, w0, w1, w2, w3, g_ctx, g_mid, ctx, mixed, middle, lifted):
-    width = c0.shape[1] // 2
-    for j, c in enumerate((c0, c1, c2, c3)):
-        for side in range(2):
-            ctx[:, context_lanes(ids, j, side, width)] = c[:, side * width : (side + 1) * width]
+def mid_kernel(ids, *refs):
+    pieces = refs[:8]
+    merged, weights, (g_ctx, g_mid, ctx, mixed, middle, lifted) = refs[8], sheets(refs[9:13]), refs[13:]
+    width = pieces[0].shape[1]
+    for n, c in enumerate(pieces):
+        ctx[:, context_lanes(ids, n % 4, n // 4, width)] = c[...]
     standard, _ = centred(ctx[...].astype(WIDE))
     mixed[...] = (standard * g_ctx[...]).astype(LOW)
-    total = merged[...].astype(WIDE)
-    depth = w0.shape[0]
-    for k, w in enumerate((w0, w1, w2, w3)):
-        total = total + dot(mixed[:, own_block(ids[1], k, depth)], w[...], NN)
-    middle[...] = total
-    standard, _ = centred(total)
+    depth, half = weights[0].shape
+    for n in range(2):
+        lanes = core_lanes(ids, n, half)
+        total = merged[:, lanes].astype(WIDE)
+        for k in range(4):
+            total = total + dot(mixed[:, own_block(ids[1], k, depth)], weights[4 * n + k][...], NN)
+        middle[:, lanes] = total
+    standard, _ = centred(middle[...])
     lifted[...] = (standard * g_mid[...]).astype(LOW)
+
+
+def sheets(refs):
+    own, pieces, other, others = refs
+    return [own] + [pieces.at[n] for n in range(3)] + [other] + [others.at[n] for n in range(3)]
+
+
+def core_lanes(ids, n, half):
+    return pl.ds(pl.multiple_of((ids[0] % 2 ^ n) * half, half), half)
 
 
 def mid_forward(ids, contexts, merged, weights, g_ctx, g_mid):
     rows, model = merged.shape
+    specs = [pl.BlockSpec(w.shape, partial(lambda n, b, ids: (0,) * n, w.ndim), pipeline_mode=ONCE) for w in weights]
     block = min(256, rows)
     line = lambda width: pl.BlockSpec((block, width), lambda b, ids: (b, 0))
     gain = pl.BlockSpec((1, model), lambda b, ids: (0, 0))
-    weight = pl.BlockSpec(weights[0].shape, lambda b, ids: (0, 0), pipeline_mode=ONCE)
     shape = lambda kind: jax.ShapeDtypeStruct((rows, model), kind)
     return kernel_call(
         mid_kernel,
         (rows // block,),
-        [line(contexts[0].shape[1])] * 4 + [line(model)] + [weight] * 4 + [gain] * 2,
+        [line(contexts[0].shape[1])] * 8 + [line(model)] + specs + [gain] * 2,
         [line(model)] * 4,
         [shape(LOW), shape(LOW), shape(WIDE), shape(LOW)],
         [],
@@ -752,9 +775,10 @@
     )
 
 
-def mid_back_kernel(
-    ids, a, r, middle, og, ctx, w0, w1, w2, w3, g_mid, g_ctx, middle_grad, middle_low, d0, d1, d2, d3, gains, mixed_grad
-):
+def mid_back_kernel(ids, *refs):
+    a, r, middle, og, ctx = refs[:5]
+    weights, (g_mid, g_ctx, middle_grad, middle_low) = sheets(refs[5:9]), refs[9:13]
+    pieces, gains, mixed_grad = refs[13:21], refs[21], refs[22]
     grad = a[...].astype(WIDE) + r[...].astype(WIDE)
     standard, scale = centred(middle[...])
 
@@ -765,42 +789,41 @@
     gains[0:1, :] += jnp.sum(grad * standard, axis=0, keepdims=True)
     total = og[...].astype(WIDE) + norm_back(standard, scale, g_mid[...], grad)
     middle_grad[...] = total
-    low = total.astype(LOW)
-    middle_low[...] = low
-    depth = w0.shape[0]
-    for k, w in enumerate((w0, w1, w2, w3)):
-        mixed_grad[:, own_block(ids[1], k, depth)] = dot(low, w[...], NT)
+    middle_low[...] = total.astype(LOW)
+    depth, half = weights[0].shape
+    own, other = middle_low[:, core_lanes(ids, 0, half)], middle_low[:, core_lanes(ids, 1, half)]
+    for k in range(4):
+        mixed_grad[:, own_block(ids[1], k, depth)] = dot(own, weights[k][...], NT) + dot(other, weights[4 + k][...], NT)
     grad = mixed_grad[...]
     standard, scale = centred(ctx[...].astype(WIDE))
     gains[1:2, :] += jnp.sum(grad * standard, axis=0, keepdims=True)
     mixed_grad[...] = norm_back(standard, scale, g_ctx[...], grad)
-    width = d0.shape[1] // 2
-    for j, d in enumerate((d0, d1, d2, d3)):
-        for side in range(2):
-            d[:, side * width : (side + 1) * width] = mixed_grad[:, context_lanes(ids, j, side, width)].astype(LOW)
+    width = pieces[0].shape[1]
+    for n, d in enumerate(pieces):
+        d[...] = mixed_grad[:, context_lanes(ids, n % 4, n // 4, width)].astype(LOW)
 
 
 def mid_backward(ids, parts, middle, og, ctx, weights, g_mid, g_ctx):
     rows, model = middle.shape
+    specs = [pl.BlockSpec(w.shape, partial(lambda n, b, ids: (0,) * n, w.ndim), pipeline_mode=ONCE) for w in weights]
     block = min(256, rows)
     line = lambda width: pl.BlockSpec((block, width), lambda b, ids: (b, 0))
     gain = pl.BlockSpec((1, model), lambda b, ids: (0, 0))
-    weight = pl.BlockSpec(weights[0].shape, lambda b, ids: (0, 0), pipeline_mode=ONCE)
     shape = lambda width, kind: jax.ShapeDtypeStruct((rows, width), kind)
     result = kernel_call(
         mid_back_kernel,
         (rows // block,),
-        [line(model)] * 5 + [weight] * 4 + [gain] * 2,
-        [line(model)] * 2 + [line(model // 4)] * 4 + [pl.BlockSpec((8, model), lambda b, ids: (0, 0))],
+        [line(model)] * 5 + specs + [gain] * 2,
+        [line(model)] * 2 + [line(model // 8)] * 8 + [pl.BlockSpec((8, model), lambda b, ids: (0, 0))],
         [shape(model, WIDE), shape(model, LOW)]
-        + [shape(model // 4, LOW)] * 4
+        + [shape(model // 8, LOW)] * 8
         + [jax.ShapeDtypeStruct((8, model), WIDE)],
         [pltpu.VMEM((block, model), WIDE)],
         2 * rows * model * model,
         2 * model * model + 18 * rows * model,
         (ids, *parts, middle, og, ctx, *weights, g_mid, g_ctx),
     )
-    return result[0], result[1], result[2:6], result[6]
+    return result[0], result[1], result[2:6], result[6:10], result[10]
 
 
 def gelu_parts(hidden):
@@ -819,154 +842,364 @@
     return out
 
 
-def ffn_first_kernel(ids, x, og, u0, u1, u2, u3, d0, d1, d2, d3, gain, hidden, squashed_grad, sums, acc):
+def halves(count, rows_first):
+    if rows_first:
+        return (
+            lambda u, ids: (jnp.minimum(u, count - 1), 0),
+            lambda u, ids: (jnp.maximum(u - count, 0), 0),
+        )
+    return (
+        lambda u, ids: (0, jnp.minimum(u, count - 1)),
+        lambda u, ids: (0, jnp.maximum(u - count, 0)),
+    )
+
+
+def each_half(work, own, got):
+    near = pl.program_id(0) < pl.num_programs(0) // 2
+
+    @pl.when(near)
+    def _():
+        work(own)
+
+    @pl.when(jnp.logical_not(near))
+    def _():
+        work(got)
+
+
+def remote(source, target, sent, got, device):
+    return pltpu.make_async_remote_copy(
+        src_ref=source, dst_ref=target, send_sem=sent, recv_sem=got, device_id=device, device_id_type=MESH
+    )
+
+
+def ffn_up_kernel(
+    lifted, own_cotangent, up_own, up_got, act, slope, sums, lifted_all, cotangent_all, x, acc, sent, got, local
+):
+    j, u = pl.program_id(0), pl.program_id(1)
+    rows = x.shape[0]
+    half = rows // 2
+    _, _, over_core, over_low, _ = partners()
+    parts = [pl.ds(b * half, half) for b in range(2)]
+
+    def moves(source, whole, base):
+        near = remote(source, whole.at[0], sent.at[base], got.at[base], over_core)
+        far = [
+            remote(source.at[part], whole.at[1, part], sent.at[base + 1 + b], got.at[base + 1 + b], over_low)
+            for b, part in enumerate(parts)
+        ]
+        last = [
+            remote(whole.at[1, part], whole.at[2, part], sent.at[base + 3 + b], got.at[base + 3 + b], over_core)
+            for b, part in enumerate(parts)
+        ]
+        return near, far, last
+
+    near, far, last = moves(lifted, lifted_all, 0)
+    near_c, far_c, last_c = moves(own_cotangent, cotangent_all, 5)
+
+    def load(source):
+        copy = pltpu.make_async_copy(source, x, local)
+        copy.start()
+        copy.wait()
+
+    @pl.when(u == 0)
+    def _():
+        acc[...] = jnp.zeros_like(acc)
+
+    @pl.when((j == 0) & (u == 0))
+    def _():
+        greet((over_core, over_low))
+        for copy in (*far, near, near_c):
+            copy.start()
+        load(lifted)
+
+    @pl.when((j == 1) & (u == 0))
+    def _():
+        near.wait()
+        load(lifted_all.at[0])
+
+    @pl.when((j == 2) & (u == 0))
+    def _():
+        for copy, onward in zip(far, last):
+            copy.wait()
+            onward.start()
+        for copy in far_c:
+            copy.start()
+        load(lifted_all.at[1])
+
+    @pl.when((j == 3) & (u == 0))
+    def _():
+        for copy in last:
+            copy.wait()
+        load(lifted_all.at[2])
+
+    def work(up):
+        for b in range(2):
+            here = slice(b * half, (b + 1) * half)
+            h = dot(x[here, :], up[...], NN)
+            activated, share = gelu_parts(h)
+            low = activated.astype(LOW)
+            act[0, here, :] = low
+            slope[0, here, :] = gelu_slope(h, share).astype(LOW)
+            activated = low.astype(WIDE)
+            acc[0, here, :] += fold(activated)
+            acc[1, here, :] += fold(activated * activated)
+
+    steps = pl.num_programs(1)
+    pl.when(u < steps // 2)(lambda: work(up_own))
+    pl.when(u >= steps // 2)(lambda: work(up_got))
+
+    @pl.when(u == steps - 1)
+    def _():
+        for n in range(2):
+            sums[0, n : n + 1, :] = jnp.sum(acc[n].T, axis=0, keepdims=True)
+        sums[0, 2:8, :] = jnp.zeros_like(sums[0, 2:8, :])
+
+    @pl.when((j == 3) & (u == steps - 1))
+    def _():
+        for copy, onward in zip(far_c, last_c):
+            copy.wait()
+            onward.start()
+        near_c.wait()
+        for copy in last_c:
+            copy.wait()
+
+
+def in_halves(count, rows_first):
+    near, far = (lambda u: jnp.minimum(u, count - 1)), (lambda u: jnp.maximum(u - count, 0))
+    if rows_first:
+        return [lambda j, u: (near(u), 0), lambda j, u: (far(u), 0)]
+    return [lambda j, u: (0, near(u)), lambda j, u: (0, far(u))]
+
+
+def ffn_up(lifted, cotangent, upward):
+    rows, model = lifted.shape
+    units = 2 * upward[0].shape[1]
+    block = min(512, units // 2)
+    count = units // 2 // block
+    out = pl.BlockSpec((1, rows, block), lambda j, u: (j, 0, u))
+    kept = jax.ShapeDtypeStruct((4, rows, units), LOW)
+    others = jax.ShapeDtypeStruct((3, rows, model), LOW)
+    return pl.pallas_call(
+        ffn_up_kernel,
+        grid=(4, 2 * count),
+        in_specs=[ANYWHERE] * 2 + [pl.BlockSpec((model, block), at) for at in in_halves(count, False)],
+        out_specs=[out] * 2 + [pl.BlockSpec((1, 8, rows), lambda j, u: (j, 0, 0))] + [ANYWHERE] * 2,
+        out_shape=[kept] * 2 + [jax.ShapeDtypeStruct((4, 8, rows), WIDE)] + [others] * 2,
+        scratch_shapes=[
+            pltpu.VMEM((rows, model), LOW),
+            pltpu.VMEM((2, rows, LANES), WIDE),
+            pltpu.SemaphoreType.DMA((10,)),
+            pltpu.SemaphoreType.DMA((10,)),
+            pltpu.SemaphoreType.DMA,
+        ],
+        compiler_params=pltpu.CompilerParams(collective_id=2, has_side_effects=True, vmem_limit_bytes=56 << 20),
+        cost_estimate=pl.CostEstimate(flops=80 * 10**9, bytes_accessed=100 << 20, transcendentals=0),
+    )(lifted, cotangent, *upward)
+
+
+def ffn_back_kernel(og, others, down_own, down_got, act, gain, squashed_grad, sums, x, acc, local):
+    j, u = pl.program_id(0), pl.program_id(1)
+    rows = x.shape[0]
+    half = rows // 2
+
+    @pl.when(u == 0)
+    def _():
+        acc[...] = jnp.zeros_like(acc)
+
+    def load(source):
+        copy = pltpu.make_async_copy(source, x, local)
+        copy.start()
+        copy.wait()
+
+    pl.when((u == 0) & (j == 0))(lambda: load(og))
+    pl.when((u == 0) & (j > 0))(lambda: load(others.at[jnp.maximum(j - 1, 0)]))
+
+    def work(down):
+        for b in range(2):
+            here = slice(b * half, (b + 1) * half)
+            s = dot(x[here, :], down[...], NT).astype(LOW)
+            squashed_grad[0, here, :] = s
+            scaled = s.astype(WIDE) * gain[...]
+            acc[0, here, :] += fold(scaled)
+            acc[1, here, :] += fold(scaled * act[0, here, :].astype(WIDE))
+
+    steps = pl.num_programs(1)
+    pl.when(u < steps // 2)(lambda: work(down_own))
+    pl.when(u >= steps // 2)(lambda: work(down_got))
+
+    @pl.when(u == steps - 1)
+    def _():
+        sums[0, 0:2, :] = jnp.zeros_like(sums[0, 0:2, :])
+        for n in range(2):
+            sums[0, n + 2 : n + 3, :] = jnp.sum(acc[n].T, axis=0, keepdims=True)
+        sums[0, 4:8, :] = jnp.zeros_like(sums[0, 4:8, :])
+
+
+def ffn_back(og, others, downward, act, gain):
+    rows, model = og.shape
+    units = act.shape[2]
+    block = min(512, units // 2)
+    count = units // 2 // block
+    line = pl.BlockSpec((1, rows, block), lambda j, u: (j, 0, u))
+    return pl.pallas_call(
+        ffn_back_kernel,
+        grid=(4, 2 * count),
+        in_specs=[ANYWHERE] * 2
+        + [pl.BlockSpec((block, model), at) for at in in_halves(count, True)]
+        + [line, pl.BlockSpec((1, block), lambda j, u: (0, u))],
+        out_specs=[line, pl.BlockSpec((1, 8, rows), lambda j, u: (j, 0, 0))],
+        out_shape=[like(act), jax.ShapeDtypeStruct((4, 8, rows), WIDE)],
+        scratch_shapes=[
+            pltpu.VMEM((rows, model), LOW),
+            pltpu.VMEM((2, rows, LANES), WIDE),
+            pltpu.SemaphoreType.DMA,
+        ],
+        compiler_params=pltpu.CompilerParams(vmem_limit_bytes=56 << 20),
+        cost_estimate=pl.CostEstimate(flops=60 * 10**9, bytes_accessed=100 << 20, transcendentals=0),
+    )(og, others, *downward, act, gain)
+
+
+def ffn_second_kernel(
+    act,
+    slope,
+    squashed_grad,
+    sums,
+    gain,
+    up_own,
+    up_got,
+    squashed,
+    hidden_grad,
+    kept,
+    arrived,
+    gains,
+    acc,
+    send_core,
+    got_core,
+    send_low,
+    sent,
+    got,
+    *,
+    hidden_width,
+):
+    n, u = pl.program_id(0), pl.program_id(1)
+    steps = pl.num_programs(1)
+    rows, block = act.shape[1:]
+    half = rows // 2
+    _, _, over_core, over_low, _ = partners()
+    to_core = [remote(send_core.at[b], got_core.at[b], sent.at[b], got.at[b], over_core) for b in range(2)]
+    to_low = remote(send_low, arrived, sent.at[2], got.at[2], over_low)
+
+    @pl.when((n == 0) & (u == 0))
+    def _():
+        greet((over_core, over_low))
+        gains[...] = jnp.zeros_like(gains)
+
+    @pl.when(u == 0)
+    def _():
+        acc[...] = jnp.zeros_like(acc)
+
+    columns = sums[0].T
+    lanes = pl.ds(pl.multiple_of(u * block, block), block)
+
+    def work(up):
+        for b in range(2):
+            here = slice(b * half, (b + 1) * half)
+            centre = columns[here, 0:1] / hidden_width
+            scale = lax.rsqrt(columns[here, 1:2] / hidden_width - centre * centre + EPS_NORM)
+            mean_one = columns[here, 2:3] / hidden_width
+            mean_two = scale * (columns[here, 3:4] - centre * columns[here, 2:3]) / hidden_width
+            standard = (act[0, here, :].astype(WIDE) - centre) * scale
+            squashed[0, here, :] = (standard * gain[...]).astype(LOW)
+            s = squashed_grad[0, here, :].astype(WIDE)
+            gains[0:1, lanes] += jnp.sum(s * standard, axis=0, keepdims=True)
+            activated_grad = (s * gain[...] - mean_one - standard * mean_two) * scale
+            grad = (activated_grad * slope[0, here, :].astype(WIDE)).astype(LOW)
+            hidden_grad[0, here, :] = grad
+            acc[here, :] += dot(grad, up[...], NT)
+
+    pl.when(u < steps // 2)(lambda: work(up_own))
+    pl.when(u >= steps // 2)(lambda: work(up_got))
+    ends = u == steps - 1
+
+    @pl.when(ends & (n == 0))
+    def _():
+        send_core[0] = acc[...].astype(LOW)
+        to_core[0].start()
+
+    @pl.when(ends & (n == 1))
+    def _():
+        to_core[0].wait()
+        send_low[...] = (acc[...] + got_core[0].astype(WIDE)).astype(LOW)
+        to_low.start()
+
+    @pl.when(ends & (n == 2))
+    def _():
+        send_core[1] = acc[...].astype(LOW)
+        to_core[1].start()
+
+    @pl.when(ends & (n == 3))
+    def _():
+        to_core[1].wait()
+        kept[...] = (acc[...] + got_core[1].astype(WIDE)).astype(LOW)
+        to_low.wait()
+
+
+def ffn_second(act, slope, squashed_grad, sums, gain, upward, hidden_width):
+    _, rows, units = act.shape
+    model = upward[0].shape[0]
+    block = min(512, units // 2)
+    count = units // 2 // block
+    line = pl.BlockSpec((1, rows, block), lambda n, u: (3 - n, 0, u))
+    piece = jax.ShapeDtypeStruct((rows, model), LOW)
+    return pl.pallas_call(
+        partial(ffn_second_kernel, hidden_width=hidden_width),
+        grid=(4, 2 * count),
+        in_specs=[line] * 3
+        + [pl.BlockSpec((1, 8, rows), lambda n, u: (3 - n, 0, 0)), pl.BlockSpec((1, block), lambda n, u: (0, u))]
+        + [pl.BlockSpec((model, block), at) for at in in_halves(count, False)],
+        out_specs=[line] * 2
+        + [pl.BlockSpec((rows, model), lambda n, u: (0, 0)), ANYWHERE, pl.BlockSpec((8, units), lambda n, u: (0, 0))],
+        out_shape=[like(act)] * 2 + [piece] * 2 + [jax.ShapeDtypeStruct((8, units), WIDE)],
+        scratch_shapes=[
+            pltpu.VMEM((rows, model), WIDE),
+            pltpu.VMEM((2, rows, model), LOW),
+            pltpu.VMEM((2, rows, model), LOW),
+            pltpu.VMEM((rows, model), LOW),
+            pltpu.SemaphoreType.DMA((3,)),
+            pltpu.SemaphoreType.DMA((3,)),
+        ],
+        compiler_params=pltpu.CompilerParams(collective_id=3, has_side_effects=True, vmem_limit_bytes=60 << 20),
+        cost_estimate=pl.CostEstimate(flops=80 * 10**9, bytes_accessed=100 << 20, transcendentals=0),
+    )(act, slope, squashed_grad, sums, gain, *upward)
+
+
+def spread_kernel(ids, x, own, got, out, acc):
     step = pl.program_id(0)
-    depth = u0.shape[0]
-    rows = x.shape[0]
-    part = rows // 2
 
     @pl.when(step == 0)
     def _():
         acc[...] = jnp.zeros_like(acc)
 
-    for b in range(2):
-        here = slice(b * part, (b + 1) * part)
-        h = None
-        s = None
-        for k, (u, d) in enumerate(((u0, d0), (u1, d1), (u2, d2), (u3, d3))):
-            lanes = own_block(ids[1], k, depth)
-            one = dot(x[here, lanes], u[...], NN)
-            two = dot(og[here, lanes], d[...], NT)
-            h = one if h is None else h + one
-            s = two if s is None else s + two
-        h = h.astype(LOW)
-        s = s.astype(LOW)
-        hidden[here, :] = h
-        squashed_grad[here, :] = s
-        activated, _ = gelu_parts(h.astype(WIDE))
-        scaled = s.astype(WIDE) * gain[...]
-        acc[0, here, :] += fold(activated)
-        acc[1, here, :] += fold(activated * activated)
-        acc[2, here, :] += fold(scaled)
-        acc[3, here, :] += fold(scaled * activated)
+    def work(weight):
+        acc[...] += dot(x[...], weight[...], NN)
+
+    each_half(work, own, got)
 
     @pl.when(step == pl.num_programs(0) - 1)
     def _():
-        for n in range(4):
-            sums[n : n + 1, :] = jnp.sum(acc[n].T, axis=0, keepdims=True)
-        sums[4:8, :] = jnp.zeros_like(sums[4:8, :])
-
-
-def ffn_first(ids, x, og, upward, downward, gain):
-    rows, model = x.shape
-    units = upward[0].shape[1]
-    block = min(512, units)
-    line = pl.BlockSpec((rows, model), lambda u, ids: (0, 0), pipeline_mode=ONCE)
-    out = pl.BlockSpec((rows, block), lambda u, ids: (0, u))
-    return kernel_call(
-        ffn_first_kernel,
-        (units // block,),
-        [line] * 2
-        + [pl.BlockSpec((model // 4, block), lambda u, ids: (0, u))] * 4
-        + [pl.BlockSpec((block, model // 4), lambda u, ids: (u, 0))] * 4
-        + [pl.BlockSpec((1, block), lambda u, ids: (0, u))],
-        [out] * 2 + [pl.BlockSpec((8, rows), lambda u, ids: (0, 0))],
-        [jax.ShapeDtypeStruct((rows, units), LOW)] * 2 + [jax.ShapeDtypeStruct((8, rows), WIDE)],
-        [pltpu.VMEM((4, rows, LANES), WIDE)],
-        4 * rows * model * units,
-        4 * model * units + 4 * rows * (model + units),
-        (ids, x, og, *upward, *downward, gain),
-    )
-
-
-def ffn_second_kernel(ids, hidden, squashed_grad, sums, gain, u0, u1, u2, u3, squashed, hidden_grad, out, gains, acc, *, hidden_width):
-    step = pl.program_id(0)
-    depth = u0.shape[0]
-    rows = hidden.shape[0]
-    part = rows // 2
-
-    @pl.when(step == 0)
-    def _():
-        acc[...] = jnp.zeros_like(acc)
-
-    columns = sums[...].T
-    gain_sum = None
-    for b in range(2):
-        here = slice(b * part, (b + 1) * part)
-        centre = columns[here, 0:1] / hidden_width
-        scale = lax.rsqrt(columns[here, 1:2] / hidden_width - centre * centre + EPS_NORM)
-        mean_one = columns[here, 2:3] / hidden_width
-        mean_two = scale * (columns[here, 3:4] - centre * columns[here, 2:3]) / hidden_width
-        h = hidden[here, :].astype(WIDE)
-        activated, share = gelu_parts(h)
-        standard = (activated - centre) * scale
-        squashed[here, :] = (standard * gain[...]).astype(LOW)
-        s = squashed_grad[here, :].astype(WIDE)
-        piece = jnp.sum(s * standard, axis=0, keepdims=True)
-        gain_sum = piece if gain_sum is None else gain_sum + piece
-        activated_grad = (s * gain[...] - mean_one - standard * mean_two) * scale
-        grad = (activated_grad * gelu_slope(h, share)).astype(LOW)
-        hidden_grad[here, :] = grad
-        for k, u in enumerate((u0, u1, u2, u3)):
-            acc[here, own_block(ids[1], k, depth)] += dot(grad, u[...], NT)
-    gains[...] = jnp.broadcast_to(gain_sum, gains.shape)
-
-    @pl.when(step == pl.num_programs(0) - 1)
-    def _():
         out[...] = acc[...].astype(LOW)
 
 
-def ffn_second(ids, hidden, squashed_grad, sums, gain, upward, hidden_width):
-    rows, units = hidden.shape
-    model = upward[0].shape[0] * 4
-    block = min(512, units)
-    line = pl.BlockSpec((rows, block), lambda u, ids: (0, u))
-    return kernel_call(
-        partial(ffn_second_kernel, hidden_width=hidden_width),
-        (units // block,),
-        [line] * 2
-        + [pl.BlockSpec((8, rows), lambda u, ids: (0, 0)), pl.BlockSpec((1, block), lambda u, ids: (0, u))]
-        + [pl.BlockSpec((model // 4, block), lambda u, ids: (0, u))] * 4,
-        [line] * 2
-        + [pl.BlockSpec((rows, model), lambda u, ids: (0, 0)), pl.BlockSpec((8, block), lambda u, ids: (0, u))],
-        [jax.ShapeDtypeStruct((rows, units), LOW)] * 2
-        + [jax.ShapeDtypeStruct((rows, model), LOW), jax.ShapeDtypeStruct((8, units), WIDE)],
-        [pltpu.VMEM((rows, model), WIDE)],
-        2 * rows * model * units,
-        2 * model * units + 8 * rows * units + 2 * rows * model,
-        (ids, hidden, squashed_grad, sums, gain, *upward),
-    )
-
-
-def spread_kernel(ids, x, w0, w1, w2, w3, out, acc):
-    step = pl.program_id(0)
-    depth = w0.shape[1]
-    for k, w in enumerate((w0, w1, w2, w3)):
-        lanes = own_block(ids[1], k, depth)
-        part = dot(x[...], w[...], NN)
-
-        @pl.when(step == 0)
-        def _():
-            acc[:, lanes] = part
-
-        @pl.when(step > 0)
-        def _():
-            acc[:, lanes] += part
-
-    @pl.when(step == pl.num_programs(0) - 1)
-    def _():
-        out[...] = acc[...].astype(LOW)
-
-
-def ffn_out(ids, x, downward):
-    rows, units = x.shape
-    model = downward[0].shape[1] * 4
-    block = min(512, units)
+def ffn_out(ids, x, j, downward):
+    _, rows, units = x.shape
+    model = downward[0].shape[1]
+    block = min(512, units // 2)
+    count = units // 2 // block
     return kernel_call(
         spread_kernel,
-        (units // block,),
-        [pl.BlockSpec((rows, block), lambda u, ids: (0, u))]
-        + [pl.BlockSpec((block, model // 4), lambda u, ids: (u, 0))] * 4,
+        (2 * count,),
+        [pl.BlockSpec((pl.Squeezed(), rows, block), lambda u, ids: (j, 0, u))]
+        + [pl.BlockSpec((block, model), at) for at in halves(count, True)],
         [pl.BlockSpec((rows, model), lambda u, ids: (0, 0))],
         [jax.ShapeDtypeStruct((rows, model), LOW)],
         [pltpu.VMEM((rows, model), WIDE)],
@@ -976,85 +1209,243 @@
     )[0]
 
 
-def unproject_kernel(ids, q, k, v, w0, w1, w2, w3, out):
-    depth = w0.shape[1]
-    for n, w in enumerate((w0, w1, w2, w3)):
+def unproject_kernel(ids, *refs):
+    grads, weights, out = refs[0:6], refs[6:14], refs[14]
+    depth = weights[0].shape[1]
+    for n in range(4):
         total = None
-        for f, g in enumerate((q, k, v)):
-            part = dot(g[...], w[f], NT)
-            total = part if total is None else total + part
+        for f in range(3):
+            for half in range(2):
+                part = dot(grads[3 * half + f][...], weights[4 * half + n][f], NT)
+                total = part if total is None else total + part
         out[:, own_block(ids[1], n, depth)] = total.astype(LOW)
 
 
-def unproject(ids, q, k, v, weights):
-    rows, width = q.shape
-    model = weights[0].shape[1] * 4
+def unproject(ids, grads, heads):
+    rows, width = grads[0].shape
+    own, got = quarters(heads[0]), quarters(heads[1])
+    model = heads[1].shape[1]
     block = min(256, rows)
     line = pl.BlockSpec((block, width), lambda b, ids: (b, 0))
     return kernel_call(
         unproject_kernel,
         (rows // block,),
-        [line] * 3 + [pl.BlockSpec(weights[0].shape, lambda b, ids: (0, 0, 0), pipeline_mode=ONCE)] * 4,
+        [line] * 6 + own[1] + got[1],
         [pl.BlockSpec((block, model), lambda b, ids: (b, 0))],
         [jax.ShapeDtypeStruct((rows, model), LOW)],
         [],
-        6 * rows * model * width,
-        6 * model * width + 2 * rows * (3 * width + model),
-        (ids, q, k, v, *weights),
+        12 * rows * model * width,
+        12 * model * width + 2 * rows * (6 * width + model),
+        (ids, *grads, *own[0], *got[0]),
     )[0]
+
+
+def grad_kernel(ids, *refs, chunks, kinds, fixed):
+    xs, ys = refs[:chunks], refs[chunks : chunks * (1 + kinds)]
+    outs, turned = refs[chunks * (1 + kinds) : -1], refs[-1]
+    step = pl.program_id(0)
+    rows = xs[0].shape[0]
+
+    def turn():
+        for j in range(chunks):
+            turned[:, j * rows : (j + 1) * rows] = xs[j][...].T
+
+    if fixed:
+        pl.when(step == 0)(turn)
+    else:
+        turn()
+    for f in range(kinds):
+        total = None
+        for j in range(chunks):
+            part = dot(turned[:, j * rows : (j + 1) * rows], ys[f * chunks + j][...], NN)
+            total = part if total is None else total + part
+        total = total.astype(LOW)
+        if len(outs) == 1:
+            outs[0][f] = total
+        else:
+            for k, out in enumerate(outs):
+
+                @pl.when(step == k)
+                def _():
+                    out[f] = total
+
+
+def weight_grad(ids, xs, ys, x_blocks, side=None, apart=False):
+    chunks, kinds = len(xs), len(ys)
+    rows, x_width = xs[0][0].shape[-2:]
+    y_width = ys[0][0][0].shape[-1]
+
+    def spec(piece, width, at, once):
+        mode = {"pipeline_mode": ONCE} if once else {}
+        if piece[1] is None:
+            return pl.BlockSpec((rows, width), at, **mode)
+        place = lambda b, ids, n=piece[1]: (n, *at(b, ids))
+        return pl.BlockSpec((pl.Squeezed(), rows, width), place, **mode)
+
+    shift = lambda b, ids: (0, ids[1] ^ b if apart else b)
+    still = lambda b, ids: (0, side or 0)
+    share = 1 if side is None else 2
+    if x_blocks:
+        x_width, y_width = x_width // 4, y_width // share
+        x_at, y_at = (x_width, shift, False), (y_width, still, True)
+        whole, out_at = (kinds, 4 * x_width, y_width), lambda b, ids: (0, b, 0)
+    else:
+        x_width, y_width = x_width // share, y_width // 4
+        x_at, y_at = (x_width, still, True), (y_width, shift, False)
+        whole, out_at = (kinds, x_width, 4 * y_width), lambda b, ids: (0, 0, b)
+    out = (kinds, x_width, y_width)
+    if apart:
+        out_specs = [pl.BlockSpec(out, lambda b, ids: (0, 0, 0))] * 4
+        out_shape = [jax.ShapeDtypeStruct(out, LOW)] * 4
+    else:
+        out_specs, out_shape = [pl.BlockSpec(out, out_at)], [jax.ShapeDtypeStruct(whole, LOW)]
+    result = kernel_call(
+        partial(grad_kernel, chunks=chunks, kinds=kinds, fixed=not x_blocks),
+        (4,),
+        [spec(x, *x_at) for x in xs] + [spec(y, *y_at) for group in ys for y in group],
+        out_specs,
+        out_shape,
+        [pltpu.VMEM((x_width, rows * chunks), LOW)],
+        8 * rows * chunks * x_width * y_width * kinds,
+        2 * rows * chunks * (4 * x_width + 4 * y_width * kinds),
+        (ids, *[x[0] for x in xs], *[y[0] for group in ys for y in group]),
+    )
+    return result if apart else result[0]
 
 
 def flip(value, axis, mask):
     return lax.ppermute(value, axis, [(i, i ^ mask) for i in range(lax.axis_size(axis))])
 
 
-def flip_both(value, mask_dp, mask_mp):
-    count_mp = lax.axis_size("mp")
-    pairs = [
-        (d * count_mp + m, (d ^ mask_dp) * count_mp + (m ^ mask_mp))
-        for d in range(lax.axis_size("dp"))
-        for m in range(count_mp)
-    ]
-    return lax.ppermute(value, ("dp", "mp"), pairs)
-
-
-def gather_tokens(chunk):
-    across = flip(chunk, "mp", 2)
-    return [chunk, flip(chunk, "mp", 1), across, flip(across, "mp", 1)]
-
-
-def gather_weight(shard, x_first):
-    if x_first:
-        one = flip(shard, "dp", 1)
-        return [shard, one, flip(shard, "dp", 2), flip(one, "dp", 2)]
-    two = flip(shard, "dp", 2)
-    return [shard, flip(shard, "dp", 1), two, flip(two, "dp", 1)]
-
-
 def add_low(one, two):
     return (one.astype(WIDE) + two.astype(WIDE)).astype(LOW)
 
 
-def scatter_grad(blocks, x_first):
-    if x_first:
-        kept = add_low(blocks[0], flip(blocks[1], "dp", 1))
-        passed = add_low(blocks[2], flip(blocks[3], "dp", 1))
-        return add_low(kept, flip(passed, "dp", 2))
-    kept = add_low(blocks[0], flip(blocks[2], "dp", 2))
-    passed = add_low(blocks[1], flip(blocks[3], "dp", 2))
-    return add_low(kept, flip(passed, "dp", 1))
-
-
-def scatter_tokens(parts):
-    passed = add_low(parts[2], flip(parts[3], "mp", 1))
-    kept = add_low(parts[0], flip(parts[1], "mp", 1))
-    return kept, flip(passed, "mp", 2)
-
-
 def sum_everywhere(value):
-    value = (value + flip(value, "mp", 1)) + (flip(value, "mp", 2) + flip(value, "mp", 3))
-    far = [flip_both(value, n // 2, 4 * (n % 2)) for n in range(1, 8)]
-    return ((value + far[0]) + (far[1] + far[2])) + ((far[3] + far[4]) + (far[5] + far[6]))
+    for mask in (1, 2, 4):
+        value = value + flip(value, "mp", mask)
+    for mask in (1, 2):
+        value = value + flip(value, "dp", mask)
+    return value
+
+
+MESH = pl.DeviceIdType.MESH
+ANYWHERE = pl.BlockSpec(memory_space=pl.ANY)
+
+
+def like(value):
+    return jax.ShapeDtypeStruct(value.shape, value.dtype)
+
+
+def partners():
+    row, column = lax.axis_index("dp"), lax.axis_index("mp")
+    over_x = (row + 1 - 2 * (row % 2), column)
+    over_y = ((row + 2) % 4, column)
+    over_core = (row, column + 1 - 2 * (column % 2))
+    over_low = (row, column + 2 - 4 * ((column // 2) % 2))
+    over_high = (row, (column + 4) % 8)
+    return over_x, over_y, over_core, over_low, over_high
+
+
+def greet(others):
+    barrier = pltpu.get_barrier_semaphore()
+    for other in others:
+        pl.semaphore_signal(barrier, inc=1, device_id=other, device_id_type=MESH)
+    pl.semaphore_wait(barrier, len(others))
+
+
+class Sender:
+    def __init__(self, sent, got):
+        self.sent, self.got, self.count = sent, got, 0
+
+    def __call__(self, source, target, device):
+        copy = pltpu.make_async_remote_copy(
+            src_ref=source,
+            dst_ref=target,
+            send_sem=self.sent.at[self.count],
+            recv_sem=self.got.at[self.count],
+            device_id=device,
+            device_id_type=MESH,
+        )
+        self.count += 1
+        copy.start()
+        return copy
+
+
+def open_kernel(text, head, text_got, head_x, head_y, head_far, sent, got):
+    over_x, over_y, _, _, over_high = partners()
+    greet((over_x, over_y, over_high))
+    send = Sender(sent, got)
+    half = head.shape[1] // 2
+    upper, lower = pl.ds(0, half), pl.ds(half, half)
+    copies = [send(text, text_got, over_high)]
+    first = send(head.at[:, upper], head_x.at[:, upper], over_x)
+    second = send(head.at[:, lower], head_y.at[:, lower], over_y)
+    copies.append(send(head.at[:, lower], head_x.at[:, lower], over_x))
+    copies.append(send(head.at[:, upper], head_y.at[:, upper], over_y))
+    first.wait()
+    copies.append(send(head_x.at[:, upper], head_far.at[:, upper], over_y))
+    second.wait()
+    copies.append(send(head_y.at[:, lower], head_far.at[:, lower], over_x))
+    for copy in copies:
+        copy.wait()
+
+
+def open_exchange(text, head):
+    return pl.pallas_call(
+        open_kernel,
+        in_specs=[ANYWHERE] * 2,
+        out_specs=[ANYWHERE] * 4,
+        out_shape=[like(text), like(head), like(head), like(head)],
+        scratch_shapes=[pltpu.SemaphoreType.DMA((7,)), pltpu.SemaphoreType.DMA((7,))],
+        compiler_params=pltpu.CompilerParams(collective_id=0, has_side_effects=True),
+        cost_estimate=pl.CostEstimate(flops=0, bytes_accessed=100 << 20, transcendentals=0),
+    )(text, head)
+
+
+def normed_kernel(normed, head, outward, near, far, far_near, head_got, pieces, others, sent, got):
+    over_x, over_y, over_core, over_low, over_high = partners()
+    greet((over_x, over_y, over_core, over_low, over_high))
+    send = Sender(sent, got)
+    rows = normed.shape[0] // 2
+    parts = [pl.ds(b * rows, rows) for b in range(2)]
+    crossing = [send(normed.at[part], far.at[part], over_low) for part in parts]
+    copies = [send(normed, near, over_core), send(head, head_got, over_high)]
+    half = outward.shape[0] // 2
+    upper, lower = pl.ds(0, half), pl.ds(half, half)
+    first = send(outward.at[upper], pieces.at[0, upper], over_x)
+    second = send(outward.at[lower], pieces.at[1, lower], over_y)
+    later = [
+        (send(outward.at[lower], pieces.at[0, lower], over_x), 0, lower),
+        (send(outward.at[upper], pieces.at[1, upper], over_y), 1, upper),
+    ]
+    first.wait()
+    later.append((send(pieces.at[0, upper], pieces.at[2, upper], over_y), 2, upper))
+    copies.append(send(pieces.at[0, upper], others.at[0, upper], over_core))
+    second.wait()
+    later.append((send(pieces.at[1, lower], pieces.at[2, lower], over_x), 2, lower))
+    copies.append(send(pieces.at[1, lower], others.at[1, lower], over_core))
+    for copy, part in zip(crossing, parts):
+        copy.wait()
+        copies.append(send(far.at[part], far_near.at[part], over_core))
+    for copy, n, part in later:
+        copy.wait()
+        copies.append(send(pieces.at[n, part], others.at[n, part], over_core))
+    for copy in copies:
+        copy.wait()
+
+
+def normed_exchange(normed, head, outward):
+    pieces = jax.ShapeDtypeStruct((3,) + outward.shape, LOW)
+    return pl.pallas_call(
+        normed_kernel,
+        in_specs=[ANYWHERE] * 3,
+        out_specs=[ANYWHERE] * 6,
+        out_shape=[like(normed)] * 3 + [like(head), pieces, pieces],
+        scratch_shapes=[pltpu.SemaphoreType.DMA((18,)), pltpu.SemaphoreType.DMA((18,))],
+        compiler_params=pltpu.CompilerParams(collective_id=1, has_side_effects=True),
+        cost_estimate=pl.CostEstimate(flops=0, bytes_accessed=100 << 20, transcendentals=0),
+    )(normed, head, outward)
 
 
 def rotary_tables(length):
@@ -1105,35 +1496,22 @@
     def pick(value, index):
         return lax.dynamic_index_in_dim(value, index, 0, keepdims=False)
 
-    def exchange(pair):
-        kept, got = pick(pair, side), flip(pick(pair, 1 - side), "mp", 4)
+    tables = rotary_tables(length)
+
+    def both(kept, got):
         return jnp.where(side == 0, jnp.stack([kept, got]), jnp.stack([got, kept]))
 
-    tables = rotary_tables(length)
-    text = exchange(text_states)
-    head_low = head_master.astype(LOW)
-    head_shard = jnp.concatenate([head_low, flip(head_low, "mp", 4)], axis=2)
-    head_weight = gather_weight(head_shard, True)
-    cotangent = exchange(output_grad).reshape(rows, model_width)
-
-    outward_low = outward_master.astype(LOW)
     core = rank % 2
     half_width = model_width // 2
-    outward_half = lax.dynamic_slice_in_dim(outward_low, core * half_width, half_width, 1)
-    outward_own = gather_weight(outward_half, False)
-    outward_other = [flip(piece, "mp", 1) for piece in outward_own[1:]]
-    outward_weight = [outward_low] + [
-        jnp.where(
-            core == 0,
-            jnp.concatenate([own, other], axis=1),
-            jnp.concatenate([other, own], axis=1),
-        )
-        for own, other in zip(outward_own[1:], outward_other)
-    ]
-    upward_low = upward_master.astype(LOW)
-    upward_weight = gather_weight(jnp.concatenate([upward_low, flip(upward_low, "mp", 4)], axis=1), True)
-    downward_low = downward_master.astype(LOW)
-    downward_weight = gather_weight(jnp.concatenate([downward_low, flip(downward_low, "mp", 4)], axis=0), False)
+    text_out = pick(text_states, 1 - side)
+    head_own = head_master.astype(LOW)
+    upward_own = upward_master.astype(LOW)
+    upward_weight = [lax.all_gather(upward_own, "dp", axis=0, tiled=True)]
+    text_got, *head_parts = open_exchange(text_out, head_own)
+    head_weight = [[head_own] + head_parts]
+    downward_own = downward_master.astype(LOW)
+    downward_weight = [lax.all_gather(downward_own, "dp", axis=1, tiled=True)]
+    text = both(pick(text_states, side), text_got)
 
     gain_in = gains_master[None, :model_width]
     gain_ctx = gains_master[None, model_width : 2 * model_width]
@@ -1169,89 +1547,118 @@
     images = jnp.dot(chosen, pick(image_states, side), preferred_element_type=WIDE).astype(LOW)
     merged = jnp.where(covered[:, None], images, text.reshape(rows, model_width))
 
-    normed = gather_tokens(layer_norm(merged.astype(WIDE), gain_in).astype(LOW))
-    cotangents = gather_tokens(cotangent)
-    projected = [project(ids, chunk, head_weight, tables, j) for j, chunk in enumerate(normed)]
-    queries, keys, values = ([p[n] for p in projected] for n in range(3))
-    contexts, lse = attend(ids, queries, keys, values)
-    arrived = [contexts[0]] + [flip(contexts[j], "mp", j) for j in range(1, 4)]
+    def turn_heads(pieces):
+        return [pieces[0]] + [flip(pieces[j], "mp", j) for j in range(1, 4)]
+
+    normed_own = layer_norm(merged.astype(WIDE), gain_in).astype(LOW)
+    outward_low = outward_master.astype(LOW)
+    outward_own, outward_other = (
+        lax.dynamic_slice_in_dim(outward_low, n * half_width, half_width, 1) for n in (core, 1 - core)
+    )
+    near, far, far_near, head_got, *pieces = normed_exchange(normed_own, head_own, outward_own)
+    outward_weight = [outward_own, pieces[0], outward_other, pieces[1]]
+    normed = [normed_own, near, far, far_near]
+    head_weight.append(lax.all_gather(head_got, "dp", axis=1, tiled=True))
+    upward_weight.append(lax.all_gather(flip(upward_own, "mp", 4), "dp", axis=0, tiled=True))
+    cotangent = both(pick(output_grad, side), flip(pick(output_grad, 1 - side), "mp", 4)).reshape(rows, model_width)
+    downward_weight.append(lax.all_gather(flip(downward_own, "mp", 4), "dp", axis=1, tiled=True))
+
+    queries, keys, values, contexts, logs, arrived = [], [], [], [], [], []
+    for half in range(2):
+        projected = [project(ids, chunk, head_weight[half], tables, j) for j, chunk in enumerate(normed)]
+        for n, group in enumerate((queries, keys, values)):
+            group.append([p[n] for p in projected])
+        context, lse = attend(ids, queries[half], keys[half], values[half])
+        contexts.append(context)
+        logs.append(lse)
+        arrived = arrived + turn_heads(context)
     context, mixed, middle, lifted_own = mid_forward(ids, arrived, merged, outward_weight, gain_ctx, gain_mid)
-    lifted = gather_tokens(lifted_own)
-    first = [ffn_first(ids, x, g, upward_weight, downward_weight, gain_hidden) for x, g in zip(lifted, cotangents)]
-    sums = jnp.stack([f[2] for f in first])
+    act, slope, sums, lifted_others, cotangent_others = ffn_up(lifted_own, cotangent, upward_weight)
+    squashed_grad, back_sums = ffn_back(cotangent, cotangent_others, downward_weight, act, gain_hidden)
+    lifted = [(lifted_own, None)] + [(lifted_others, n) for n in range(3)]
+    cotangents = [(cotangent, None)] + [(cotangent_others, n) for n in range(3)]
+    sums = sums + back_sums
     others = [flip(sums, "mp", k) for k in range(1, 4)]
-    whole_sums = [
-        (sums[j] + others[0][j ^ 1]) + (others[1][j ^ 2] + others[2][j ^ 3]) for j in range(4)
+    sums = jnp.stack(
+        [(sums[j] + others[0][j ^ 1]) + (others[1][j ^ 2] + others[2][j ^ 3]) for j in range(4)]
+    )
+    squashed, hidden_grad, lifted_kept, lifted_got, hidden_gains = ffn_second(
+        act, slope, squashed_grad, sums, gain_hidden, upward_weight, hidden_width
+    )
+
+    def split(value):
+        return [(value, n) for n in range(4)]
+
+    def whole(values):
+        return [(value, None) for value in values]
+
+    down_grad = lax.psum_scatter(
+        weight_grad(ids, split(squashed), [cotangents], False), "dp", scatter_dimension=2, tiled=True
+    )[0]
+    down_got = flip(down_grad[hidden_local:], "mp", 4)
+    middle_grad, middle_low, own_grads, other_grads, mid_gains = mid_backward(
+        ids, (lifted_kept, lifted_got), middle, cotangent, context, outward_weight, gain_mid, gain_ctx
+    )
+    context_heads = [turn_heads(own_grads), turn_heads(other_grads)]
+    outward_blocks = [
+        part[0] for part in weight_grad(ids, whole([mixed]), [whole([middle_low])], True, None, True)
     ]
-    second = [
-        ffn_second(ids, first[j][0], first[j][1], whole_sums[j], gain_hidden, upward_weight, hidden_width)
-        for j in range(4)
-    ]
-    lifted_parts = scatter_tokens([s[2] for s in second])
-    middle_grad, middle_low, context_grads, mid_gains = mid_backward(
-        ids, lifted_parts, middle, cotangent, context, outward_weight, gain_mid, gain_ctx
-    )
-    context_heads = [context_grads[0]] + [flip(context_grads[j], "mp", j) for j in range(1, 4)]
-    query_grads, key_grads, value_grads = attend_back(
-        ids, queries, keys, values, context_heads, contexts, lse, tables
-    )
-    normed_parts = [unproject(ids, *g, head_weight) for g in zip(query_grads, key_grads, value_grads)]
+    up_grad = lax.psum_scatter(
+        weight_grad(ids, lifted, [split(hidden_grad)], True), "dp", scatter_dimension=1, tiled=True
+    )[0]
+    up_got = flip(up_grad[:, hidden_local:], "mp", 4)
+    ffn_parts = [ffn_out(ids, squashed, j, downward_weight) for j in range(4)]
+
+    def scatter_tokens(parts):
+        passed = add_low(parts[2], flip(parts[3], "mp", 1))
+        return add_low(parts[0], flip(parts[1], "mp", 1)), flip(passed, "mp", 2)
+
+    def give_back(pair):
+        got = flip(pick(pair, 1 - side).astype(LOW), "mp", 4)
+        return both(pick(pair, side), got.astype(pair.dtype))
+
+    ffn_kept, ffn_got = scatter_tokens(ffn_parts)
+    output_rows = (middle + (ffn_kept.astype(WIDE) + ffn_got.astype(WIDE))).astype(LOW)
+    layer_output = give_back(output_rows.reshape(2, local_len, model_width))
+
+    def scatter_blocks(blocks, one, two):
+        passed = add_low(blocks[3 - one], flip(blocks[3], "dp", one))
+        return add_low(add_low(blocks[0], flip(blocks[one], "dp", one)), flip(passed, "dp", two))
+
+    head_grads, head_sides = [None, None], [None, None]
+    for half in (1, 0):
+        head_grads[half] = attend_back(
+            ids, queries[half], keys[half], values[half], context_heads[half], contexts[half], logs[half], tables
+        )
+        blocks = weight_grad(ids, whole(normed), [whole(g) for g in head_grads[half]], True, None, True)
+        head_sides[half] = scatter_blocks(blocks, 1, 2)
+    head_sum = head_sides[0].astype(WIDE) + flip(head_sides[1], "mp", 4).astype(WIDE)
+    normed_parts = [None] * 4
+    for j in (3, 2, 1, 0):
+        pieces = [group[j] for half in head_grads for group in half]
+        normed_parts[j] = unproject(ids, pieces, head_weight)
     normed_kept, normed_got = scatter_tokens(normed_parts)
     normed_grad = normed_kept.astype(WIDE) + normed_got.astype(WIDE)
     _, input_back = jax.vjp(layer_norm, merged.astype(WIDE), gain_in)
     merged_part, in_gain_grad = input_back(normed_grad)
-    input_rows = (middle_grad + merged_part).reshape(2, local_len, model_width)
-
-    ffn_kept, ffn_got = scatter_tokens([ffn_out(ids, s[0], downward_weight) for s in second])
-    output_rows = (
-        (middle + (ffn_kept.astype(WIDE) + ffn_got.astype(WIDE))).astype(LOW).reshape(2, local_len, model_width)
-    )
-
-    def give_back(pair):
-        kept = pick(pair, side)
-        got = flip(pick(pair, 1 - side).astype(LOW), "mp", 4).astype(pair.dtype)
-        return jnp.where(side == 0, jnp.stack([kept, got]), jnp.stack([got, kept]))
-
-    layer_output = give_back(output_rows)
-    input_grad = give_back(input_rows)
-
-    tokens = (((0,), (0,)), ((), ()))
-    squashed_rows = jnp.concatenate([s[0] for s in second])
-    hidden_grad_rows = jnp.concatenate([s[1] for s in second])
-    cotangent_rows = jnp.concatenate(cotangents)
-    lifted_rows = jnp.concatenate(lifted)
-    normed_rows = jnp.concatenate(normed)
-    quarter = model_width // 4
-
-    def lanes(value, k):
-        return lax.dynamic_slice_in_dim(value, (place ^ k) * quarter, quarter, 1)
-
-    down_grad = scatter_grad(
-        [dot(squashed_rows, lanes(cotangent_rows, k), tokens).astype(LOW) for k in range(4)], False
-    )
-    down_sum = down_grad[:hidden_local].astype(WIDE) + flip(down_grad[hidden_local:], "mp", 4).astype(WIDE)
-    up_grad = scatter_grad(
-        [dot(lanes(lifted_rows, k), hidden_grad_rows, tokens).astype(LOW) for k in range(4)], True
-    )
-    up_sum = up_grad[:, :hidden_local].astype(WIDE) + flip(up_grad[:, hidden_local:], "mp", 4).astype(WIDE)
-
-    outward_parts = [dot(lanes(mixed, k), middle_low, tokens).astype(LOW) for k in range(4)]
-    outward_parts = [
+    input_grad = give_back((middle_grad + merged_part).reshape(2, local_len, model_width))
+
+    outward_blocks = [
         add_low(
             lax.dynamic_slice_in_dim(part, core * half_width, half_width, 1),
             flip(lax.dynamic_slice_in_dim(part, (1 - core) * half_width, half_width, 1), "mp", 1),
         )
-        for part in outward_parts
+        for part in outward_blocks
     ]
-    outward_grad = scatter_grad(outward_parts, False)
-    bits = ((2, (rank // 2) % 2), (4, side))
-    for mask, bit in bits:
+    outward_grad = scatter_blocks(outward_blocks, 2, 1)
+    low_bit = (rank // 2) % 2
+    for mask, bit in ((2, low_bit), (4, side)):
         size = outward_grad.shape[0] // 2
         outward_grad = add_low(
             lax.dynamic_slice_in_dim(outward_grad, bit * size, size, 0),
             flip(lax.dynamic_slice_in_dim(outward_grad, (1 - bit) * size, size, 0), "mp", mask),
         )
-    for mask, bit, axis in ((4, side, 0), (2, (rank // 2) % 2, 0), (1, core, 1)):
+    for mask, bit, axis in ((4, side, 0), (2, low_bit, 0), (1, core, 1)):
         got = flip(outward_grad, "mp", mask)
         outward_grad = jnp.where(
             bit == 0,
@@ -1260,13 +1667,8 @@
         )
     outward_sum = outward_grad.astype(WIDE)
 
-    head_parts = [jnp.concatenate(g) for g in (query_grads, key_grads, value_grads)]
-    head_grad = scatter_grad(
-        [jnp.stack([dot(lanes(normed_rows, k), g, tokens).astype(LOW) for g in head_parts]) for k in range(4)], True
-    )
-    head_local = head_master.shape[2]
-    head_sum = head_grad[:, :, :head_local].astype(WIDE) + flip(head_grad[:, :, head_local:], "mp", 4).astype(WIDE)
-
+    down_sum = down_grad[:hidden_local].astype(WIDE) + down_got.astype(WIDE)
+    up_sum = up_grad[:, :hidden_local].astype(WIDE) + up_got.astype(WIDE)
     moment_head, square_head, head_dir = adapt_step(head_sum, head_master, head_moment, head_square, DECAY_RATE)
     moment_outward, square_outward, outward_dir = adapt_step(
         outward_sum, outward_master, outward_moment, outward_square, DECAY_RATE
@@ -1291,7 +1693,7 @@
     head_part = jnp.stack(
         [jnp.sum(head_master * head_master, axis=(1, 2)), jnp.sum(head_dir * head_dir, axis=(1, 2))], axis=-1
     )
-    hidden_gain = jnp.concatenate([s[3][0:1] for s in second], axis=0).sum(axis=0)
+    hidden_gain = hidden_gains[0]
     gains_part = jnp.concatenate([in_gain_grad[0], mid_gains[1], mid_gains[0], jnp.zeros((hidden_width,), WIDE)])
     gains_part = lax.dynamic_update_slice(gains_part, hidden_gain[:hidden_local], (hidden_start,))
     gains_part = lax.dynamic_update_slice(gains_part, hidden_gain[hidden_local:], (other_start,))

time: 1440 us -> 1310 us (0.910)
  Pallas kernels: 398 us -> 726 us
  waiting for transfers between devices: 588 us -> 364 us
  matrix products: 104 us -> 1.93 us
  starting transfers between devices: 101 us -> 52.6 us
  other arithmetic: 160 us -> 114 us
  local copies, waits for them, and re-layouts: 72.9 us -> 27.7 us
    pallas_call x0 -> x5, Pallas kernels: none -> 334 us  [the longest x1 101 us: ffn_up(): pl.pallas_call(ffn_up_kernel, grid=(4, 2 * count), in_specs=[ANYWHERE] *...]
    ppermute x82 -> x62, waiting for transfers between devices: 543 us -> 364 us  [flip(): lax.ppermute(value, axis, [(i, i ^ mask) for i in range(lax.axis_size(axi...]
    dot_general x24 -> x0, matrix products: 102 us -> none  [dot(): return lax.dot_general(left, right, dims, preferred_element_type=WIDE)]
    ppermute x21 -> x0, waiting for transfers between devices: 44.7 us -> none  [flip_both(): return lax.ppermute(value, ('dp', 'mp'), pairs)]
    unnamed x267 -> x137, local copies, waits for them, and re-layouts: 40.5 us -> 3.55 us
    ppermute x21 -> x0, starting transfers between devices: 29 us -> none  [flip_both(): return lax.ppermute(value, ('dp', 'mp'), pairs)]
    concatenate x5 -> x0, other arithmetic: 21.4 us -> none  [the longest x1 6.99 us: on_device_paired(): normed_rows = jnp.concatenate(normed)]
    ppermute x82 -> x62, starting transfers between devices: 72.3 us -> 52.1 us  [flip(): lax.ppermute(value, axis, [(i, i ^ mask) for i in range(lax.axis_size(axi...]
  transfers between devices with their start and end apart: 103 -> 69, of which waited for: 39 -> 29; matrix products, arithmetic and copies ran while one was open for 14% -> 8% of each run, Pallas kernels for 23% -> 36%
where the time goes in v2:
time: 1310 us
  Pallas kernels  726 us (55%)
  waiting for transfers between devices  364 us (28%)
  other arithmetic  114 us (9%)
  starting transfers between devices  52.6 us (4%)
  local copies, waits for them, and re-layouts  27.7 us (2%)
  between operations  20.3 us (2%)
    pallas_call x27, Pallas kernels, kernel_call(): pl.pallas_call(body, grid_spec=pltpu.PrefetchScalarGridSpec(num_scalar_pr...  392 us
    ppermute x62, waiting for transfers between devices, flip(): lax.ppermute(value, axis, [(i, i ^ mask) for i in range(lax.axis_size(axi...  364 us
    pallas_call x1, Pallas kernels, ffn_up(): pl.pallas_call(ffn_up_kernel, grid=(4, 2 * count), in_specs=[ANYWHERE] *...  101 us
    pallas_call x1, Pallas kernels, ffn_second(): pl.pallas_call(partial(ffn_second_kernel, hidden_width=hidden_width), gri...  71.7 us
    pallas_call x1, Pallas kernels, normed_exchange(): pl.pallas_call(normed_kernel, in_specs=[ANYWHERE] * 3, out_specs=[ANYWHER...  71.5 us
    ppermute x62, starting transfers between devices, flip(): lax.ppermute(value, axis, [(i, i ^ mask) for i in range(lax.axis_size(axi...  52.1 us
    pallas_call x1, Pallas kernels, open_exchange(): pl.pallas_call(open_kernel, in_specs=[ANYWHERE] * 2, out_specs=[ANYWHERE]...  51.4 us
    pallas_call x1, Pallas kernels, ffn_back(): pl.pallas_call(ffn_back_kernel, grid=(4, 2 * count), in_specs=[ANYWHERE]...  38.9 us
  transfers between devices with their start and end apart: 69, of which 29 were waited for; matrix products, arithmetic and copies ran while one was open for 8% of the time, Pallas kernels for 36%

profile of v2, /device:TPU:0, one launch (start us, length us, event | category | flops | bytes accessed | tf_op | source)
XLA Modules:
  0.0 1307.1 jit_solution(14798764901921946197)
XLA Ops:
  14.5 51.4 %shard_map.363 = (bf16[256,2048]{1,0:T(8,128)(2,1)}, bf16[3,512,256]{2,1,0:T(8,128)(2,1)}, bf16[3,512,256]{2,1,0:T(8,128)(2,1)}, bf16[3,512,256]{2,1,0:T(8,128)(2,1)}) custom-call(bf16[256,2048]{1,0:T(8,128)(2,1)} %get-tuple-element.280.text, bf16[3,512,256]{2,1,0:T(8,128)(2,1)} %convert_element_type.268.head.w0.refs_6_), custom_call_target="tpu_custom_call" | custom-call | bytes 104857600 | tf_op jit(solution)/shard_map/pallas_call | solution.py:1395
  76.1 71.5 %shard_map.365 = (bf16[512,2048]{1,0:T(8,128)(2,1)}, bf16[512,2048]{1,0:T(8,128)(2,1)}, bf16[512,2048]{1,0:T(8,128)(2,1)}, bf16[3,512,256]{2,1,0:T(8,128)(2,1)},...) custom-call(bf16[512,2048]{1,0:T(8,128)(2,1)} %fusion.6.x.normed.refs_0_, ...), custom_call_target="tpu_custom_call" | custom-call | bytes 104857600 | tf_op jit(solution)/shard_map/pallas_call | solution.py:1440
  150.8 48.0 %collective-permute-done.7 = bf16[512,1024]{1,0:T(8,128)(2,1)S(1)} collective-permute-done((bf16[512,1024]{1,0:T(8,128)(2,1)}, bf16[512,1024]{1,0:T(8,128)(2,1)S(1)}, u32[]{:S(2)}, u32[]{:S(2)}) %collective-permute-start.7) | collective-permute-done | bytes 1048608 | tf_op jit(solution)/shard_map/ppermute | solution.py:1317
  237.4 23.3 %shard_map.369 = (bf16[512,256]{1,0:T(8,128)(2,1)}, bf16[512,256]{1,0:T(8,128)(2,1)}, bf16[512,256]{1,0:T(8,128)(2,1)}, bf16[512,256]{1,0:T(8,128)(2,1)}, f32[2,2,2048]{2,1,0:T(2,128)}) custom-call(s32[3]{0:T(128)} %pad_add_fusion.ids, bf16[512,256]{1,0:T(8,128)(2,1)} %get-tuple-element.133.refs_0_, bf16[512,256]{1,0:T(8,128)(2,1)} %get-tuple-element.135.refs_1_, ...), custom_call_target="tpu_custom_call" | custom-call | flops 12000000000 | bytes 3000000 | tf_op jit(solution)/shard_map/pallas_call | solution.py:463
  293.2 22.8 %shard_map.374 = (bf16[512,256]{1,0:T(8,128)(2,1)}, bf16[512,256]{1,0:T(8,128)(2,1)}, bf16[512,256]{1,0:T(8,128)(2,1)}, bf16[512,256]{1,0:T(8,128)(2,1)}, f32[2,2,2048]{2,1,0:T(2,128)}) custom-call(s32[3]{0:T(128)} %pad_add_fusion.ids, bf16[512,256]{1,0:T(8,128)(2,1)} %get-tuple-element.153.refs_0_, bf16[512,256]{1,0:T(8,128)(2,1)} %get-tuple-element.154.refs_1_, ...), custom_call_target="tpu_custom_call" | custom-call | flops 12000000000 | bytes 3000000 | tf_op jit(solution)/shard_map/pallas_call | solution.py:463
  330.9 15.0 %shard_map.375 = (bf16[512,2048]{1,0:T(8,128)(2,1)}, bf16[512,2048]{1,0:T(8,128)(2,1)}, f32[512,2048]{1,0:T(8,128)}, bf16[512,2048]{1,0:T(8,128)(2,1)}) custom-call(s32[3]{0:T(128)} %pad_add_fusion.ids, bf16[512,256]{1,0:T(8,128)(2,1)} %get-tuple-element.148.refs_0_.refs_16_, bf16[512,256]{1,0:T(8,128)(2,1)} %copy-done.46, ...), custom_call_target="tpu_custom_call" | custom-call | flops 1288490240 | bytes 6920601 | tf_op jit(solution)/shard_map/pallas_call | solution.py:463
  345.9 100.5 %shard_map.376 = (bf16[4,512,2048]{2,1,0:T(8,128)(2,1)}, bf16[4,512,2048]{2,1,0:T(8,128)(2,1)}, f32[4,8,512]{2,1,0:T(8,128)}, bf16[3,512,2048]{2,1,0:T(8,128)(2,1)}, bf16[3,512,2048]{2,1,0:T(8,128)(2,1)}) custom-call(bf16[512,2048]{1,0:T(8,128)(2,1)} %get-tuple-element.172.lifted.refs_0_, bf16[512,2048]{1,0:T(8,128)(2,1)} %bitcast.102, ...), custom_call_target="tpu_custom_call" | custom-call | flops 80000000000 | bytes 104857600 | tf_op jit(solution)/shard_map/pallas_call | solution.py:982
  446.5 38.9 %shard_map.377 = (bf16[4,512,2048]{2,1,0:T(8,128)(2,1)}, f32[4,8,512]{2,1,0:T(8,128)}) custom-call(bf16[512,2048]{1,0:T(8,128)(2,1)} %bitcast.103, bf16[3,512,2048]{2,1,0:T(8,128)(2,1)} %get-tuple-element.175.others.refs_5_.refs_6_.refs_7_, bf16[1024,2048]{1,0:T(8,128)(2,1)} %all-gather.12.cloned.1.call-done.down_own.own, ...), custom_call_target="tpu_custom_call" | custom-call | flops 60000002048 | bytes 104857600 | tf_op jit(solution)/shard_map/pallas_call | solution.py:1044
  492.6 71.7 %shard_map.378 = (bf16[4,512,2048]{2,1,0:T(8,128)(2,1)}, bf16[4,512,2048]{2,1,0:T(8,128)(2,1)}, bf16[512,2048]{1,0:T(8,128)(2,1)}, bf16[512,2048]{1,0:T(8,128)(2,1)}, f32[8,2048]{1,0:T(8,128)}) custom-call(bf16[4,512,2048]{2,1,0:T(8,128)(2,1)} %get-tuple-element.173.act, bf16[4,512,2048]{2,1,0:T(8,128)(2,1)} %get-tuple-element.174.slope, ...), custom_call_target="tpu_custom_call" | custom-call | flops 80000000000 | bytes 104857600 | tf_op jit(solution)/shard_map/pallas_call | solution.py:1154
  564.3 24.6 %shard_map.393 = bf16[1,2048,2048]{2,1,0:T(8,128)(2,1)} custom-call(s32[3]{0:T(128)} %pad_add_fusion.ids, bf16[512,2048]{1,0:T(8,128)(2,1)} %get-tuple-element.172.lifted.refs_0_, bf16[3,512,2048]{2,1,0:T(8,128)(2,1)} %get-tuple-element.232.refs_1_.refs_2_.refs_3_, bf16[3,512,2048]{2,1,0:T(8,128)(2,1)} %get-tuple-element.232.refs_1_.refs_2_.refs_3_, ...), custom_call_target="tpu_custom_call" | custom-call | flops 5153960960 | bytes 12582912 | tf_op jit(solution)/shard_map/pallas_call | solution.py:463
  589.1 21.0 %shard_map.383 = (f32[512,2048]{1,0:T(8,128)}, bf16[512,2048]{1,0:T(8,128)(2,1)}, bf16[512,256]{1,0:T(8,128)(2,1)}, bf16[512,256]{1,0:T(8,128)(2,1)}, bf16[512,2...) custom-call(s32[3]{0:T(128)} %pad_add_fusion.ids, ...), custom_call_target="tpu_custom_call" | custom-call | flops 1288490240 | bytes 8178892 | tf_op jit(solution)/shard_map/pallas_call | solution.py:463
  630.3 27.5 %shard_map.394 = bf16[1,2048,2048]{2,1,0:T(8,128)(2,1)} custom-call(s32[3]{0:T(128)} %pad_add_fusion.ids, bf16[4,512,2048]{2,1,0:T(8,128)(2,1)} %get-tuple-element.179.x.refs_0_.refs_1_.refs_2_.refs_3_, bf16[4,512,2048]{2,1,0:T(8,128)(2,1)} %get-tuple-element.179.x.refs_0_.refs_1_.refs_2_.refs_3_, ...), custom_call_target="tpu_custom_call" | custom-call | flops 5153960960 | bytes 12582912 | tf_op jit(solution)/shard_map/pallas_call | solution.py:463
  692.9 40.5 %shard_map.385 = (bf16[512,256]{1,0:T(8,128)(2,1)}, bf16[512,256]{1,0:T(8,128)(2,1)}, bf16[512,256]{1,0:T(8,128)(2,1)}, bf16[512,256]{1,0:T(8,128)(2,1)}, bf16[5...) custom-call(s32[3]{0:T(128)} %pad_add_fusion.ids, ...), custom_call_target="tpu_custom_call" | custom-call | flops 17999998976 | bytes 6000000 | tf_op jit(solution)/shard_map/pallas_call | solution.py:463
  733.4 18.4 %shard_map.391 = (bf16[3,512,256]{2,1,0:T(8,128)(2,1)}, bf16[3,512,256]{2,1,0:T(8,128)(2,1)}, bf16[3,512,256]{2,1,0:T(8,128)(2,1)}, bf16[3,512,256]{2,1,0:T(8,128)(2,1)}) custom-call(s32[3]{0:T(128)} %pad_add_fusion.ids, bf16[512,2048]{1,0:T(8,128)(2,1)} %fusion.6.x.normed.refs_0_, bf16[512,2048]{1,0:T(8,128)(2,1)} %get-tuple-element.134.x.refs_1_, ...), custom_call_target="tpu_custom_call" | custom-call | flops 1932735232 | bytes 6291456 | tf_op jit(solution)/shard_map/pallas_call | solution.py:463
  754.0 40.7 %shard_map.384 = (bf16[512,256]{1,0:T(8,128)(2,1)}, bf16[512,256]{1,0:T(8,128)(2,1)}, bf16[512,256]{1,0:T(8,128)(2,1)}, bf16[512,256]{1,0:T(8,128)(2,1)}, bf16[5...) custom-call(s32[3]{0:T(128)} %pad_add_fusion.ids, ...), custom_call_target="tpu_custom_call" | custom-call | flops 17999998976 | bytes 6000000 | tf_op jit(solution)/shard_map/pallas_call | solution.py:463
  794.7 18.5 %shard_map.390 = (bf16[3,512,256]{2,1,0:T(8,128)(2,1)}, bf16[3,512,256]{2,1,0:T(8,128)(2,1)}, bf16[3,512,256]{2,1,0:T(8,128)(2,1)}, bf16[3,512,256]{2,1,0:T(8,128)(2,1)}) custom-call(s32[3]{0:T(128)} %pad_add_fusion.ids, bf16[512,2048]{1,0:T(8,128)(2,1)} %fusion.6.x.normed.refs_0_, bf16[512,2048]{1,0:T(8,128)(2,1)} %get-tuple-element.134.x.refs_1_, ...), custom_call_target="tpu_custom_call" | custom-call | flops 1932735232 | bytes 6291456 | tf_op jit(solution)/shard_map/pallas_call | solution.py:463
  907.3 17.2 %collective-permute-done.32 = bf16[3,512,256]{2,1,0:T(8,128)(2,1)S(1)} collective-permute-done((bf16[3,512,256]{2,1,0:T(8,128)(2,1)S(1)}, bf16[3,512,256]{2,1,0:T(8,128)(2,1)S(1)}, u32[]{:S(2)}, u32[]{:S(2)}) %collective-permute-start.32) | collective-permute-done | bytes 786464 | tf_op jit(solution)/shard_map/ppermute | solution.py:1317
  933.2 53.7 %collective-permute-done.34 = f32[3,2]{0,1:T(2,128)S(1)} collective-permute-done((f32[3,2]{0,1:T(2,128)S(1)}, f32[3,2]{0,1:T(2,128)S(1)}, u32[]{:S(2)}, u32[]{:S(2)}) %collective-permute-start.34) | collective-permute-done | bytes 56 | tf_op jit(solution)/shard_map/ppermute | solution.py:1317
  1010.0 33.7 %collective-permute-done.46 = bf16[128,1024]{1,0:T(8,128)(2,1)} collective-permute-done((bf16[128,1024]{1,0:T(8,128)(2,1)S(1)}, bf16[128,1024]{1,0:T(8,128)(2,1)}, u32[]{:S(2)}, u32[]{:S(2)}) %collective-permute-start.46) | collective-permute-done | bytes 262176 | tf_op jit(solution)/shard_map/ppermute | solution.py:1317
  1071.7 20.3 %collective-permute-done.58 = f32[14336]{0:T(1024)S(1)} collective-permute-done((f32[14336]{0:T(1024)S(1)}, f32[14336]{0:T(1024)S(1)}, u32[]{:S(2)}, u32[]{:S(2)}) %collective-permute-start.58) | collective-permute-done | bytes 57376 | tf_op jit(solution)/shard_map/ppermute | solution.py:1317
  1095.0 16.9 %collective-permute-done.59 = f32[14336]{0:T(1024)S(1)} collective-permute-done((f32[14336]{0:T(1024)S(1)}, f32[14336]{0:T(1024)S(1)}, u32[]{:S(2)}, u32[]{:S(2)}) %collective-permute-start.59) | collective-permute-done | bytes 57376 | tf_op jit(solution)/shard_map/ppermute | solution.py:1317
  1135.9 22.6 %collective-permute-done.25 = bf16[256,2048]{1,0:T(8,128)(2,1)S(1)} collective-permute-done((bf16[256,2048]{1,0:T(8,128)(2,1)S(1)}, bf16[256,2048]{1,0:T(8,128)(2,1)S(1)}, u32[]{:S(2)}, u32[]{:S(2)}) %collective-permute-start.25) | collective-permute-done | bytes 1048608 | tf_op jit(solution)/shard_map/ppermute | solution.py:1317
  1180.2 54.5 %collective-permute-done.50 = bf16[512,1024]{1,0:T(8,128)(2,1)} collective-permute-done((bf16[512,1024]{1,0:T(8,128)(2,1)}, bf16[512,1024]{1,0:T(8,128)(2,1)}, u32[]{:S(2)}, u32[]{:S(2)}) %collective-permute-start.50) | collective-permute-done | bytes 1048608 | tf_op jit(solution)/shard_map/ppermute | solution.py:1317
  1241.8 15.2 %collective-permute-done.51 = bf16[1024,512]{1,0:T(8,128)(2,1)S(1)} collective-permute-done((bf16[1024,512]{1,0:T(8,128)(2,1)S(1)}, bf16[1024,512]{1,0:T(8,128)(2,1)S(1)}, u32[]{:S(2)}, u32[]{:S(2)}) %collective-permute-start.51) | collective-permute-done | bytes 1048608 | tf_op jit(solution)/shard_map/ppermute | solution.py:1317
  (411 shorter events, 418.4 us)
Async XLA Ops:
  7.2 260.5 %all-gather.6.cloned.1.call-start = ((), (), s32[]{:S(2)}) async-start(), calls=%async_computation.2 | async-start | bytes 3932160 | tf_op jit(solution)/shard_map/all_gather | solution.py:1561
  147.7 198.2 %all-gather.8.cloned.1.call-start = ((), (), s32[]{:S(2)}) async-start(), calls=%async_computation.3 | async-start | bytes 5242880 | tf_op jit(solution)/shard_map/all_gather | solution.py:1509
  150.6 195.2 %all-gather.10.cloned.1.call-start = ((), (), s32[]{:S(2)}) async-start(), calls=%async_computation.4 | async-start | bytes 5242880 | tf_op jit(solution)/shard_map/all_gather | solution.py:1562
  199.7 246.7 %all-gather.12.cloned.1.call-start = ((), (), s32[]{:S(2)}) async-start(), calls=%async_computation.5 | async-start | bytes 5242880 | tf_op jit(solution)/shard_map/all_gather | solution.py:1513
  200.9 245.5 %all-gather.14.cloned.1.call-start = ((), (), s32[]{:S(2)}) async-start(), calls=%async_computation.6 | async-start | bytes 5242880 | tf_op jit(solution)/shard_map/all_gather | solution.py:1564
  267.6 893.5 %reduce-scatter.3.cloned.1.call-start = ((), (), s32[]{:S(2)}) async-start(), calls=%async_computation.7 | async-start | bytes 10485760 | tf_op jit(solution)/shard_map/reduce_scatter | solution.py:1606
  589.0 574.4 %reduce-scatter.5.cloned.1.call-start = ((), (), s32[]{:S(2)}) async-start(), calls=%async_computation.8 | async-start | bytes 10485760 | tf_op jit(solution)/shard_map/reduce_scatter | solution.py:1595
  610.1 80.9 %collective-permute-start.19 = (bf16[512,256]{1,0:T(8,128)(2,1)}, bf16[512,256]{1,0:T(8,128)(2,1)}, u32[]{:S(2)}, u32[]{:S(2)}) collective-permute-start(bf16[512,256]{1,0:T(8,128)(2,1)} %get-tuple-element.193), channel_id=1, source_target_pairs={{0,1},{1,0},{2,3},{3,2},{4,5},{5,4},{6,7},{7,6},{8,9},{9,8},{10,11... | collective-permute-start | bytes 786440 | tf_op jit(solution)/shard_map/ppermute | solution.py:1317
  610.2 82.0 %collective-permute-start.20 = (bf16[512,256]{1,0:T(8,128)(2,1)}, bf16[512,256]{1,0:T(8,128)(2,1)}, u32[]{:S(2)}, u32[]{:S(2)}) collective-permute-start(bf16[512,256]{1,0:T(8,128)(2,1)} %get-tuple-element.194), channel_id=1, source_target_pairs={{0,2},{1,3},{2,0},{3,1},{4,6},{5,7},{6,4},{7,5},{8,10},{9,11},{10,... | collective-permute-start | bytes 786440 | tf_op jit(solution)/shard_map/ppermute | solution.py:1317
  611.3 81.5 %collective-permute-start.21 = (bf16[512,256]{1,0:T(8,128)(2,1)}, bf16[512,256]{1,0:T(8,128)(2,1)}, u32[]{:S(2)}, u32[]{:S(2)}) collective-permute-start(bf16[512,256]{1,0:T(8,128)(2,1)} %get-tuple-element.195), channel_id=1, source_target_pairs={{0,3},{1,2},{2,1},{3,0},{4,7},{5,6},{6,5},{7,4},{8,11},{9,10},{10,... | collective-permute-start | bytes 786440 | tf_op jit(solution)/shard_map/ppermute | solution.py:1317
  612.1 139.7 %collective-permute-start.16 = (bf16[512,256]{1,0:T(8,128)(2,1)}, bf16[512,256]{1,0:T(8,128)(2,1)}, u32[]{:S(2)}, u32[]{:S(2)}) collective-permute-start(bf16[512,256]{1,0:T(8,128)(2,1)} %get-tuple-element.185), channel_id=1, source_target_pairs={{0,1},{1,0},{2,3},{3,2},{4,5},{5,4},{6,7},{7,6},{8,9},{9,8},{10,11... | collective-permute-start | bytes 786440 | tf_op jit(solution)/shard_map/ppermute | solution.py:1317
  612.4 140.9 %collective-permute-start.17 = (bf16[512,256]{1,0:T(8,128)(2,1)}, bf16[512,256]{1,0:T(8,128)(2,1)}, u32[]{:S(2)}, u32[]{:S(2)}) collective-permute-start(bf16[512,256]{1,0:T(8,128)(2,1)} %get-tuple-element.186), channel_id=1, source_target_pairs={{0,2},{1,3},{2,0},{3,1},{4,6},{5,7},{6,4},{7,5},{8,10},{9,11},{10,... | collective-permute-start | bytes 786440 | tf_op jit(solution)/shard_map/ppermute | solution.py:1317
  692.2 135.7 %collective-permute-start.39 = (bf16[512,1024]{1,0:T(8,128)(2,1)S(1)}, bf16[512,1024]{1,0:T(8,128)(2,1)}, u32[]{:S(2)}, u32[]{:S(2)}) collective-permute-start(bf16[512,1024]{1,0:T(8,128)(2,1)S(1)} %dynamic-slice_bitcast_fusion.2), channel_id=1, source_target_pairs={{0,1},{1,0},{2,3},{3,2},{4,5},{5,4},{6,7},{7,6},{8,9},{9,8},{10,11... | collective-permute-start | bytes 3145736 | tf_op jit(solution)/shard_map/ppermute | solution.py:1317
  692.8 123.6 %collective-permute-start.42 = (bf16[512,1024]{1,0:T(8,128)(2,1)S(1)}, bf16[512,1024]{1,0:T(8,128)(2,1)S(1)}, u32[]{:S(2)}, u32[]{:S(2)}) collective-permute-start(bf16[512,1024]{1,0:T(8,128)(2,1)S(1)} %copy-done.38), channel_id=1, source_target_pairs={{0,1},{1,0},{2,3},{3,2},{4,5},{5,4},{6,7},{7,6},{8,9},{9,8},{10,11... | collective-permute-start | bytes 3145736 | tf_op jit(solution)/shard_map/ppermute | solution.py:1317
  751.8 74.7 %collective-permute-start.30 = (bf16[3,512,256]{2,1,0:T(8,128)(2,1)}, bf16[3,512,256]{2,1,0:T(8,128)(2,1)S(1)}, u32[]{:S(2)}, u32[]{:S(2)}) collective-permute-start(bf16[3,512,256]{2,1,0:T(8,128)(2,1)} %get-tuple-element.225), channel_id=1, source_target_pairs={{0,8},{8,0},{16,24},{24,16},{1,9},{9,1},{17,25},{25,17},{2,10},{10... | collective-permute-start | bytes 2359304 | tf_op jit(solution)/shard_map/ppermute | solution.py:1317
  816.4 70.9 %collective-permute-start.13 = (bf16[512,2048]{1,0:T(8,128)(2,1)}, bf16[512,2048]{1,0:T(8,128)(2,1)S(1)}, u32[]{:S(2)}, u32[]{:S(2)}) collective-permute-start(bf16[512,2048]{1,0:T(8,128)(2,1)} %shard_map.382), channel_id=1, source_target_pairs={{0,1},{1,0},{2,3},{3,2},{4,5},{5,4},{6,7},{7,6},{8,9},{9,8},{10,11... | collective-permute-start | bytes 6291464 | tf_op jit(solution)/shard_map/ppermute | solution.py:1317
  826.5 78.1 %collective-permute-start.23 = (bf16[512,2048]{1,0:T(8,128)(2,1)}, bf16[512,2048]{1,0:T(8,128)(2,1)S(1)}, u32[]{:S(2)}, u32[]{:S(2)}) collective-permute-start(bf16[512,2048]{1,0:T(8,128)(2,1)} %shard_map.389), channel_id=1, source_target_pairs={{0,1},{1,0},{2,3},{3,2},{4,5},{5,4},{6,7},{7,6},{8,9},{9,8},{10,11... | collective-permute-start | bytes 6291464 | tf_op jit(solution)/shard_map/ppermute | solution.py:1317
  907.3 150.5 %collective-permute-start.12 = (bf16[512,2048]{1,0:T(8,128)(2,1)}, bf16[512,2048]{1,0:T(8,128)(2,1)}, u32[]{:S(2)}, u32[]{:S(2)}) collective-permute-start(bf16[512,2048]{1,0:T(8,128)(2,1)} %shard_map.380), channel_id=1, source_target_pairs={{0,1},{1,0},{2,3},{3,2},{4,5},{5,4},{6,7},{7,6},{8,9},{9,8},{10,11... | collective-permute-start | bytes 6291464 | tf_op jit(solution)/shard_map/ppermute | solution.py:1317
  924.5 139.8 %collective-permute-start.22 = (bf16[512,2048]{1,0:T(8,128)(2,1)}, bf16[512,2048]{1,0:T(8,128)(2,1)S(1)}, u32[]{:S(2)}, u32[]{:S(2)}) collective-permute-start(bf16[512,2048]{1,0:T(8,128)(2,1)} %shard_map.387), channel_id=1, source_target_pairs={{0,1},{1,0},{2,3},{3,2},{4,5},{5,4},{6,7},{7,6},{8,9},{9,8},{10,11... | collective-permute-start | bytes 6291464 | tf_op jit(solution)/shard_map/ppermute | solution.py:1317
  927.4 130.4 %collective-permute-start.14 = (bf16[512,2048]{1,0:T(8,128)(2,1)}, bf16[512,2048]{1,0:T(8,128)(2,1)}, u32[]{:S(2)}, u32[]{:S(2)}) collective-permute-start(bf16[512,2048]{1,0:T(8,128)(2,1)} %add_convert_fusion.3), channel_id=1, source_target_pairs={{0,2},{1,3},{2,0},{3,1},{4,6},{5,7},{6,4},{7,5},{8,10},{9,11},{10,... | collective-permute-start | bytes 6291464 | tf_op jit(solution)/shard_map/ppermute | solution.py:1317
  995.0 69.3 %collective-permute-start.24 = (bf16[512,2048]{1,0:T(8,128)(2,1)}, bf16[512,2048]{1,0:T(8,128)(2,1)S(1)}, u32[]{:S(2)}, u32[]{:S(2)}) collective-permute-start(bf16[512,2048]{1,0:T(8,128)(2,1)} %add_convert_fusion), channel_id=1, source_target_pairs={{0,2},{1,3},{2,0},{3,1},{4,6},{5,7},{6,4},{7,5},{8,10},{9,11},{10,... | collective-permute-start | bytes 6291464 | tf_op jit(solution)/shard_map/ppermute | solution.py:1317
  1062.0 72.3 %collective-permute-start.15 = (bf16[256,2048]{1,0:T(8,128)(2,1)S(1)}, bf16[256,2048]{1,0:T(8,128)(2,1)S(1)}, u32[]{:S(2)}, u32[]{:S(2)}) collective-permute-start(bf16[256,2048]{1,0:T(8,128)(2,1)S(1)} %get-tuple-element.274), channel_id=1, source_target_pairs={{0,4},{1,5},{2,6},{3,7},{4,0},{5,1},{6,2},{7,3},{8,12},{9,13},{10,... | collective-permute-start | bytes 3145736 | tf_op jit(solution)/shard_map/ppermute | solution.py:1317
  1163.4 71.2 %collective-permute-start.50 = (bf16[512,1024]{1,0:T(8,128)(2,1)}, bf16[512,1024]{1,0:T(8,128)(2,1)}, u32[]{:S(2)}, u32[]{:S(2)}) collective-permute-start(bf16[512,1024]{1,0:T(8,128)(2,1)} %slice.205), channel_id=1, source_target_pairs={{0,4},{1,5},{2,6},{3,7},{4,0},{5,1},{6,2},{7,3},{8,12},{9,13},{10,... | collective-permute-start | bytes 3145736 | tf_op jit(solution)/shard_map/ppermute | solution.py:1317
  1164.8 92.1 %collective-permute-start.51 = (bf16[1024,512]{1,0:T(8,128)(2,1)S(1)}, bf16[1024,512]{1,0:T(8,128)(2,1)S(1)}, u32[]{:S(2)}, u32[]{:S(2)}) collective-permute-start(bf16[1024,512]{1,0:T(8,128)(2,1)S(1)} %slice_bitcast_fusion), channel_id=1, source_target_pairs={{0,4},{1,5},{2,6},{3,7},{4,0},{5,1},{6,2},{7,3},{8,12},{9,13},{10,... | collective-permute-start | bytes 3145736 | tf_op jit(solution)/shard_map/ppermute | solution.py:1317
  (113 other events, 2525.7 us)
Sparse Core Ops, SparseCore 0:
  147.8 43.1 all-gather.5
  193.4 52.6 all-gather.7
  248.5 52.6 all-gather.9
  303.5 52.5 all-gather.11
  357.8 52.5 all-gather.13
  589.1 86.4 reduce-scatter.2
  679.0 95.1 reduce-scatter.4

commit v3 on v2

--- a/solution.py
+++ b/solution.py
@@ -453,26 +453,47 @@
 LOW = jnp.bfloat16
 WIDE = jnp.float32
 ONCE = pl.Buffered(1)
+MESH = pl.DeviceIdType.MESH
+ANYWHERE = pl.BlockSpec(memory_space=pl.ANY)
+
+
+def like(value):
+    return jax.ShapeDtypeStruct(value.shape, value.dtype)
 
 
 def dot(left, right, dims):
     return lax.dot_general(left, right, dims, preferred_element_type=WIDE)
 
 
-def kernel_call(body, grid, in_specs, out_specs, out_shape, scratch, flops, moved, operands):
+def kernel_call(body, grid, in_specs, out_specs, out_shape, scratch, flops, moved, operands, done=(), carry=()):
+    count, extra, outs = len(operands), len(done) + len(carry), len(out_specs)
+
+    def whole(*refs):
+        inner = refs[count + extra :]
+        body(*refs[:count], *inner[:outs], *inner[outs + len(carry) :])
+
     return pl.pallas_call(
-        body,
+        whole,
         grid_spec=pltpu.PrefetchScalarGridSpec(
-            num_scalar_prefetch=1, grid=grid, in_specs=in_specs, out_specs=out_specs, scratch_shapes=scratch
+            num_scalar_prefetch=1,
+            grid=grid,
+            in_specs=list(in_specs) + [ANYWHERE] * extra,
+            out_specs=list(out_specs) + [ANYWHERE] * len(carry),
+            scratch_shapes=scratch,
         ),
-        out_shape=out_shape,
+        out_shape=list(out_shape) + [like(value) for value in carry],
+        input_output_aliases={count + len(done) + n: outs + n for n in range(len(carry))},
         compiler_params=pltpu.CompilerParams(vmem_limit_bytes=56 << 20),
         cost_estimate=pl.CostEstimate(flops=int(flops * SHARE), bytes_accessed=int(moved * SHARE), transcendentals=0),
-    )(*operands)
+    )(*operands, *done, *carry)
+
+
+def mate(rank, j):
+    return (rank, rank + 1 - 2 * (rank % 2), (rank + 2) % 4, 3 - rank)[j]
 
 
 def own_rows(sub, rank, j, b):
-    return pl.ds(pl.multiple_of(b * 4 * sub + (rank ^ j) * sub, sub), sub)
+    return pl.ds(pl.multiple_of(b * 4 * sub + mate(rank, j) * sub, sub), sub)
 
 
 def own_block(place, k, width):
@@ -590,7 +611,7 @@
             o_[j][b * sub : (b + 1) * sub, :] = os[own_rows(sub, rank, j, b), :]
 
 
-def attend(ids, queries, keys, values):
+def attend(ids, queries, keys, values, done=(), carry=()):
     rows, width = queries[0].shape
     length, pairs = rows * 4, width // LANES
     chunk = pl.BlockSpec((rows, LANES), lambda p, ids: (0, p))
@@ -605,16 +626,26 @@
         40e9,
         10e6,
         (ids, *queries, *keys, *values),
-    )
-    return result[:4], result[4]
-
-
-def attend_back_kernel(ids, *refs, bq, bk):
+        done,
+        carry,
+    )
+    return result[:4], result[4], *result[5:]
+
+
+def attend_back_kernel(*refs, bq, bk):
     q_, k_, v_, d_, o_ = refs[0:4], refs[4:8], refs[8:12], refs[12:16], refs[16:20]
-    lse_ref, cq, sq, ck, sk = refs[20:25]
-    dq_, dk_, dv_ = refs[25:29], refs[29:33], refs[33:37]
-    qs, ks, vs, ds, kt, dqt, dks, dvs, delta = refs[37:]
-    rank = ids[0]
+    lse_ref, cq, sq, ck, sk, away = refs[20:26]
+    dq_, dk_, dv_, back = refs[-15:-11]
+    qs, ks, vs, ds, kt, dqt, dks, dvs, delta, sent, got = refs[-11:]
+    over_high = partners()[4]
+    crossing = remote(away, back, sent, got, over_high)
+
+    @pl.when(pl.program_id(0) == 0)
+    def _():
+        greet((over_high,))
+        crossing.start()
+
+    rank = lax.axis_index("mp") % 4
     length = qs.shape[0]
     sub = q_[0].shape[0] // 2
     for j in range(4):
@@ -671,26 +702,32 @@
             rows = own_rows(sub, rank, j, b)
             here = slice(b * sub, (b + 1) * sub)
             query_grad = dqt[:, rows].T * 0.125
-            dq_[j][here, :] = (query_grad * cq[rows, :] - swap_halves(query_grad) * sq[rows, :]).astype(LOW)
+            dq_[j, here, :] = (query_grad * cq[rows, :] - swap_halves(query_grad) * sq[rows, :]).astype(LOW)
             key_grad = dks[rows, :]
-            dk_[j][here, :] = (key_grad * ck[rows, :] - swap_halves(key_grad) * sk[rows, :]).astype(LOW)
-            dv_[j][here, :] = dvs[rows, :]
-
-
-def attend_back(ids, queries, keys, values, cotangents, contexts, lse, tables):
+            dk_[j, here, :] = (key_grad * ck[rows, :] - swap_halves(key_grad) * sk[rows, :]).astype(LOW)
+            dv_[j, here, :] = dvs[rows, :]
+
+    @pl.when(pl.program_id(0) == pl.num_programs(0) - 1)
+    def _():
+        crossing.wait()
+
+
+def attend_back(queries, keys, values, cotangents, contexts, lse, tables, away, number, done):
     rows, width = queries[0].shape
     length, pairs = rows * 4, width // LANES
-    chunk = pl.BlockSpec((rows, LANES), lambda p, ids: (0, p))
-    whole = pl.BlockSpec((length, LANES), lambda p, ids: (0, 0), pipeline_mode=ONCE)
+    chunk = pl.BlockSpec((rows, LANES), lambda p: (0, p))
+    whole = pl.BlockSpec((length, LANES), lambda p: (0, 0), pipeline_mode=ONCE)
     low = pltpu.VMEM((length, LANES), LOW)
     block = min(512, length)
-    result = kernel_call(
+    return pl.pallas_call(
         partial(attend_back_kernel, bq=block, bk=block),
-        (pairs,),
-        [chunk] * 20 + [pl.BlockSpec((1, 2, length), lambda p, ids: (p, 0, 0))] + [whole] * 4,
-        [chunk] * 12,
-        [jax.ShapeDtypeStruct((rows, width), LOW)] * 12,
-        [
+        grid=(pairs,),
+        in_specs=[chunk] * 20 + [pl.BlockSpec((1, 2, length), lambda p: (p, 0, 0))]
+        + [whole] * 4
+        + [ANYWHERE] * (1 + len(done)),
+        out_specs=[pl.BlockSpec((4, rows, LANES), lambda p: (0, 0, p))] * 3 + [ANYWHERE],
+        out_shape=[jax.ShapeDtypeStruct((4, rows, width), LOW)] * 3 + [like(away)],
+        scratch_shapes=[
             low,
             low,
             low,
@@ -700,12 +737,14 @@
             pltpu.VMEM((length, LANES), WIDE),
             low,
             pltpu.VMEM((2, length), WIDE),
+            pltpu.SemaphoreType.DMA,
+            pltpu.SemaphoreType.DMA,
         ],
-        60e9,
-        20e6,
-        (ids, *queries, *keys, *values, *cotangents, *contexts, lse, *tables),
-    )
-    return result[0:4], result[4:8], result[8:12]
+        compiler_params=pltpu.CompilerParams(
+            collective_id=number, has_side_effects=True, vmem_limit_bytes=56 << 20
+        ),
+        cost_estimate=pl.CostEstimate(flops=40 * 10**9, bytes_accessed=20 << 20, transcendentals=0),
+    )(*queries, *keys, *values, *cotangents, *contexts, lse, *tables, away, *done)
 
 
 def centred(block):
@@ -755,7 +794,7 @@
     return pl.ds(pl.multiple_of((ids[0] % 2 ^ n) * half, half), half)
 
 
-def mid_forward(ids, contexts, merged, weights, g_ctx, g_mid):
+def mid_forward(ids, contexts, merged, weights, g_ctx, g_mid, carry):
     rows, model = merged.shape
     specs = [pl.BlockSpec(w.shape, partial(lambda n, b, ids: (0,) * n, w.ndim), pipeline_mode=ONCE) for w in weights]
     block = min(256, rows)
@@ -772,6 +811,8 @@
         2 * rows * model * model,
         2 * model * model + 14 * rows * model,
         (ids, *contexts, merged, *weights, g_ctx, g_mid),
+        (),
+        carry,
     )
 
 
@@ -873,7 +914,7 @@
 
 
 def ffn_up_kernel(
-    lifted, own_cotangent, up_own, up_got, act, slope, sums, lifted_all, cotangent_all, x, acc, sent, got, local
+    lifted, up_own, up_got, act, slope, sums, lifted_all, x, acc, sent, got, local
 ):
     j, u = pl.program_id(0), pl.program_id(1)
     rows = x.shape[0]
@@ -894,7 +935,6 @@
         return near, far, last
 
     near, far, last = moves(lifted, lifted_all, 0)
-    near_c, far_c, last_c = moves(own_cotangent, cotangent_all, 5)
 
     def load(source):
         copy = pltpu.make_async_copy(source, x, local)
@@ -908,7 +948,7 @@
     @pl.when((j == 0) & (u == 0))
     def _():
         greet((over_core, over_low))
-        for copy in (*far, near, near_c):
+        for copy in (*far, near):
             copy.start()
         load(lifted)
 
@@ -922,8 +962,6 @@
         for copy, onward in zip(far, last):
             copy.wait()
             onward.start()
-        for copy in far_c:
-            copy.start()
         load(lifted_all.at[1])
 
     @pl.when((j == 3) & (u == 0))
@@ -954,15 +992,6 @@
             sums[0, n : n + 1, :] = jnp.sum(acc[n].T, axis=0, keepdims=True)
         sums[0, 2:8, :] = jnp.zeros_like(sums[0, 2:8, :])
 
-    @pl.when((j == 3) & (u == steps - 1))
-    def _():
-        for copy, onward in zip(far_c, last_c):
-            copy.wait()
-            onward.start()
-        near_c.wait()
-        for copy in last_c:
-            copy.wait()
-
 
 def in_halves(count, rows_first):
     near, far = (lambda u: jnp.minimum(u, count - 1)), (lambda u: jnp.maximum(u - count, 0))
@@ -971,7 +1000,7 @@
     return [lambda j, u: (0, near(u)), lambda j, u: (0, far(u))]
 
 
-def ffn_up(lifted, cotangent, upward):
+def ffn_up(lifted, upward):
     rows, model = lifted.shape
     units = 2 * upward[0].shape[1]
     block = min(512, units // 2)
@@ -982,22 +1011,22 @@
     return pl.pallas_call(
         ffn_up_kernel,
         grid=(4, 2 * count),
-        in_specs=[ANYWHERE] * 2 + [pl.BlockSpec((model, block), at) for at in in_halves(count, False)],
-        out_specs=[out] * 2 + [pl.BlockSpec((1, 8, rows), lambda j, u: (j, 0, 0))] + [ANYWHERE] * 2,
-        out_shape=[kept] * 2 + [jax.ShapeDtypeStruct((4, 8, rows), WIDE)] + [others] * 2,
+        in_specs=[ANYWHERE] + [pl.BlockSpec((model, block), at) for at in in_halves(count, False)],
+        out_specs=[out] * 2 + [pl.BlockSpec((1, 8, rows), lambda j, u: (j, 0, 0)), ANYWHERE],
+        out_shape=[kept] * 2 + [jax.ShapeDtypeStruct((4, 8, rows), WIDE), others],
         scratch_shapes=[
             pltpu.VMEM((rows, model), LOW),
             pltpu.VMEM((2, rows, LANES), WIDE),
-            pltpu.SemaphoreType.DMA((10,)),
-            pltpu.SemaphoreType.DMA((10,)),
+            pltpu.SemaphoreType.DMA((5,)),
+            pltpu.SemaphoreType.DMA((5,)),
             pltpu.SemaphoreType.DMA,
         ],
         compiler_params=pltpu.CompilerParams(collective_id=2, has_side_effects=True, vmem_limit_bytes=56 << 20),
         cost_estimate=pl.CostEstimate(flops=80 * 10**9, bytes_accessed=100 << 20, transcendentals=0),
-    )(lifted, cotangent, *upward)
-
-
-def ffn_back_kernel(og, others, down_own, down_got, act, gain, squashed_grad, sums, x, acc, local):
+    )(lifted, *upward)
+
+
+def ffn_back_kernel(og, near, far, last, down_own, down_got, act, gain, squashed_grad, sums, x, acc, local):
     j, u = pl.program_id(0), pl.program_id(1)
     rows = x.shape[0]
     half = rows // 2
@@ -1011,8 +1040,8 @@
         copy.start()
         copy.wait()
 
-    pl.when((u == 0) & (j == 0))(lambda: load(og))
-    pl.when((u == 0) & (j > 0))(lambda: load(others.at[jnp.maximum(j - 1, 0)]))
+    for n, source in enumerate((og, near, far, last)):
+        pl.when((u == 0) & (j == n))(partial(load, source))
 
     def work(down):
         for b in range(2):
@@ -1044,7 +1073,7 @@
     return pl.pallas_call(
         ffn_back_kernel,
         grid=(4, 2 * count),
-        in_specs=[ANYWHERE] * 2
+        in_specs=[ANYWHERE] * 4
         + [pl.BlockSpec((block, model), at) for at in in_halves(count, True)]
         + [line, pl.BlockSpec((1, block), lambda j, u: (0, u))],
         out_specs=[line, pl.BlockSpec((1, 8, rows), lambda j, u: (j, 0, 0))],
@@ -1056,7 +1085,7 @@
         ],
         compiler_params=pltpu.CompilerParams(vmem_limit_bytes=56 << 20),
         cost_estimate=pl.CostEstimate(flops=60 * 10**9, bytes_accessed=100 << 20, transcendentals=0),
-    )(og, others, *downward, act, gain)
+    )(og, *others, *downward, act, gain)
 
 
 def ffn_second_kernel(
@@ -1209,35 +1238,95 @@
     )[0]
 
 
-def unproject_kernel(ids, *refs):
-    grads, weights, out = refs[0:6], refs[6:14], refs[14]
-    depth = weights[0].shape[1]
-    for n in range(4):
-        total = None
-        for f in range(3):
-            for half in range(2):
-                part = dot(grads[3 * half + f][...], weights[4 * half + n][f], NT)
-                total = part if total is None else total + part
-        out[:, own_block(ids[1], n, depth)] = total.astype(LOW)
-
-
-def unproject(ids, grads, heads):
-    rows, width = grads[0].shape
-    own, got = quarters(heads[0]), quarters(heads[1])
-    model = heads[1].shape[1]
-    block = min(256, rows)
-    line = pl.BlockSpec((block, width), lambda b, ids: (b, 0))
-    return kernel_call(
+def unproject_kernel(*refs):
+    grads, owns, got_weight, away = refs[0:6], refs[6:10], refs[10], refs[11:13]
+    kept, arrived, *back = refs[13:17]
+    acc, send_core, got_core, send_low, sent, got = refs[17:]
+    n, b = pl.program_id(0), pl.program_id(1)
+    rows = acc.shape[0]
+    depth = owns[0].shape[1]
+    place = lax.axis_index("dp")
+    _, _, over_core, over_low, over_high = partners()
+    here = pl.ds(pl.multiple_of(b * rows, rows), rows)
+
+    def to_core(slot, half):
+        s = 2 * slot + half
+        return remote(send_core.at[s], got_core.at[s], sent.at[s], got.at[s], over_core)
+
+    def to_low(half):
+        part = pl.ds(half * rows, rows)
+        return remote(send_low.at[half], arrived.at[part], sent.at[4 + half], got.at[4 + half], over_low)
+
+    crossing = [remote(away[i], back[i], sent.at[6 + i], got.at[6 + i], over_high) for i in range(2)]
+
+    @pl.when((n == 0) & (b == 0))
+    def _():
+        greet((over_core, over_low, over_high))
+        for copy in crossing:
+            copy.start()
+
+    acc[...] = sum(dot(grads[3 + f][0], got_weight[f], NT) for f in range(3))
+    for k in range(4):
+        lanes = pl.ds(pl.multiple_of(mate(place, k) * depth, depth), depth)
+        acc[:, lanes] += sum(dot(grads[f][0], owns[k][f], NT) for f in range(3))
+
+    for half in range(2):
+
+        @pl.when((n == 0) & (b == half))
+        def _():
+            send_core[half] = acc[...].astype(LOW)
+            to_core(0, half).start()
+
+        @pl.when((n == 1) & (b == half))
+        def _():
+            to_core(0, half).wait()
+            send_low[half] = (acc[...] + got_core[half].astype(WIDE)).astype(LOW)
+            to_low(half).start()
+
+        @pl.when((n == 2) & (b == half))
+        def _():
+            send_core[2 + half] = acc[...].astype(LOW)
+            to_core(1, half).start()
+
+        @pl.when((n == 3) & (b == half))
+        def _():
+            to_core(1, half).wait()
+            kept[here, :] = (acc[...] + got_core[2 + half].astype(WIDE)).astype(LOW)
+
+    @pl.when((n == 3) & (b == 1))
+    def _():
+        to_low(0).wait()
+        to_low(1).wait()
+        for copy in crossing:
+            copy.wait()
+
+
+def unproject(grads, heads, away):
+    _, rows, width = grads[0].shape
+    own, got = heads
+    model = got.shape[1]
+    half = rows // 2
+    line = pl.BlockSpec((1, half, width), lambda n, b: (3 - n, b, 0))
+    still = lambda value: pl.BlockSpec(value.shape, lambda n, b: (0,) * value.ndim, pipeline_mode=ONCE)
+    piece = jax.ShapeDtypeStruct((rows, model), LOW)
+    buffer = lambda count: pltpu.VMEM((count, half, model), LOW)
+    return pl.pallas_call(
         unproject_kernel,
-        (rows // block,),
-        [line] * 6 + own[1] + got[1],
-        [pl.BlockSpec((block, model), lambda b, ids: (b, 0))],
-        [jax.ShapeDtypeStruct((rows, model), LOW)],
-        [],
-        12 * rows * model * width,
-        12 * model * width + 2 * rows * (6 * width + model),
-        (ids, *grads, *own[0], *got[0]),
-    )[0]
+        grid=(4, 2),
+        in_specs=[line] * 6 + [still(w) for w in own] + [still(got), ANYWHERE, ANYWHERE],
+        out_specs=[pl.BlockSpec((rows, model), lambda n, b: (0, 0)), ANYWHERE, ANYWHERE, ANYWHERE],
+        out_shape=[piece, piece] + [like(value) for value in away],
+        scratch_shapes=[
+            pltpu.VMEM((half, model), WIDE),
+            buffer(4),
+            buffer(4),
+            buffer(2),
+            pltpu.SemaphoreType.DMA((8,)),
+            pltpu.SemaphoreType.DMA((8,)),
+        ],
+        compiler_params=pltpu.CompilerParams(collective_id=6, has_side_effects=True, vmem_limit_bytes=56 << 20),
+        cost_estimate=pl.CostEstimate(flops=40 * 10**9, bytes_accessed=20 << 20, transcendentals=0),
+    )(*grads, *own, got, *away)
 
 
 def grad_kernel(ids, *refs, chunks, kinds, fixed):
@@ -1270,7 +1359,7 @@
                     out[f] = total
 
 
-def weight_grad(ids, xs, ys, x_blocks, side=None, apart=False):
+def weight_grad(ids, xs, ys, x_blocks, done=(), side=None, apart=False):
     chunks, kinds = len(xs), len(ys)
     rows, x_width = xs[0][0].shape[-2:]
     y_width = ys[0][0][0].shape[-1]
@@ -1309,6 +1398,7 @@
         8 * rows * chunks * x_width * y_width * kinds,
         2 * rows * chunks * (4 * x_width + 4 * y_width * kinds),
         (ids, *[x[0] for x in xs], *[y[0] for group in ys for y in group]),
+        done,
     )
     return result if apart else result[0]
 
@@ -1322,19 +1412,9 @@
 
 
 def sum_everywhere(value):
-    for mask in (1, 2, 4):
-        value = value + flip(value, "mp", mask)
-    for mask in (1, 2):
-        value = value + flip(value, "dp", mask)
+    for axis, mask in (("dp", 1), ("dp", 2), ("mp", 1), ("mp", 2), ("mp", 4)):
+        value = value + flip(value, axis, mask)
     return value
-
-
-MESH = pl.DeviceIdType.MESH
-ANYWHERE = pl.BlockSpec(memory_space=pl.ANY)
-
-
-def like(value):
-    return jax.ShapeDtypeStruct(value.shape, value.dtype)
 
 
 def partners():
@@ -1403,14 +1483,14 @@
     )(text, head)
 
 
-def normed_kernel(normed, head, outward, near, far, far_near, head_got, pieces, others, sent, got):
+def normed_kernel(normed, head, outward, upward, near, far, far_near, head_got, pieces, others, up_got, sent, got):
     over_x, over_y, over_core, over_low, over_high = partners()
     greet((over_x, over_y, over_core, over_low, over_high))
     send = Sender(sent, got)
     rows = normed.shape[0] // 2
     parts = [pl.ds(b * rows, rows) for b in range(2)]
     crossing = [send(normed.at[part], far.at[part], over_low) for part in parts]
-    copies = [send(normed, near, over_core), send(head, head_got, over_high)]
+    copies = [send(normed, near, over_core), send(head, head_got, over_high), send(upward, up_got, over_high)]
     half = outward.shape[0] // 2
     upper, lower = pl.ds(0, half), pl.ds(half, half)
     first = send(outward.at[upper], pieces.at[0, upper], over_x)
@@ -1435,17 +1515,17 @@
         copy.wait()
 
 
-def normed_exchange(normed, head, outward):
+def normed_exchange(normed, head, outward, upward):
     pieces = jax.ShapeDtypeStruct((3,) + outward.shape, LOW)
     return pl.pallas_call(
         normed_kernel,
-        in_specs=[ANYWHERE] * 3,
-        out_specs=[ANYWHERE] * 6,
-        out_shape=[like(normed)] * 3 + [like(head), pieces, pieces],
-        scratch_shapes=[pltpu.SemaphoreType.DMA((18,)), pltpu.SemaphoreType.DMA((18,))],
+        in_specs=[ANYWHERE] * 4,
+        out_specs=[ANYWHERE] * 7,
+        out_shape=[like(normed)] * 3 + [like(head), pieces, pieces, like(upward)],
+        scratch_shapes=[pltpu.SemaphoreType.DMA((19,)), pltpu.SemaphoreType.DMA((19,))],
         compiler_params=pltpu.CompilerParams(collective_id=1, has_side_effects=True),
         cost_estimate=pl.CostEstimate(flops=0, bytes_accessed=100 << 20, transcendentals=0),
-    )(normed, head, outward)
+    )(normed, head, outward, upward)
 
 
 def rotary_tables(length):
@@ -1555,28 +1635,40 @@
     outward_own, outward_other = (
         lax.dynamic_slice_in_dim(outward_low, n * half_width, half_width, 1) for n in (core, 1 - core)
     )
-    near, far, far_near, head_got, *pieces = normed_exchange(normed_own, head_own, outward_own)
+    near, far, far_near, head_got, *pieces, upward_got = normed_exchange(
+        normed_own, head_own, outward_own, upward_own
+    )
     outward_weight = [outward_own, pieces[0], outward_other, pieces[1]]
     normed = [normed_own, near, far, far_near]
     head_weight.append(lax.all_gather(head_got, "dp", axis=1, tiled=True))
-    upward_weight.append(lax.all_gather(flip(upward_own, "mp", 4), "dp", axis=0, tiled=True))
+    upward_weight.append(lax.all_gather(upward_got, "dp", axis=0, tiled=True))
     cotangent = both(pick(output_grad, side), flip(pick(output_grad, 1 - side), "mp", 4)).reshape(rows, model_width)
-    downward_weight.append(lax.all_gather(flip(downward_own, "mp", 4), "dp", axis=1, tiled=True))
+    cotangent_far = flip(cotangent, "mp", 2)
+    cotangent_others = [flip(cotangent, "mp", 1), cotangent_far, flip(cotangent_far, "mp", 1)]
 
     queries, keys, values, contexts, logs, arrived = [], [], [], [], [], []
     for half in range(2):
         projected = [project(ids, chunk, head_weight[half], tables, j) for j, chunk in enumerate(normed)]
         for n, group in enumerate((queries, keys, values)):
             group.append([p[n] for p in projected])
-        context, lse = attend(ids, queries[half], keys[half], values[half])
+        if half == 0:
+            context, lse, leaving = attend(
+                ids, queries[half], keys[half], values[half], [], [downward_own]
+            )
+            downward_got = flip(leaving, "mp", 4)
+        else:
+            context, lse = attend(ids, queries[half], keys[half], values[half])
         contexts.append(context)
         logs.append(lse)
         arrived = arrived + turn_heads(context)
-    context, mixed, middle, lifted_own = mid_forward(ids, arrived, merged, outward_weight, gain_ctx, gain_mid)
-    act, slope, sums, lifted_others, cotangent_others = ffn_up(lifted_own, cotangent, upward_weight)
+    context, mixed, middle, lifted_own, downward_got = mid_forward(
+        ids, arrived, merged, outward_weight, gain_ctx, gain_mid, [downward_got]
+    )
+    downward_weight.append(lax.all_gather(downward_got, "dp", axis=1, tiled=True))
+    act, slope, sums, lifted_others = ffn_up(lifted_own, upward_weight)
     squashed_grad, back_sums = ffn_back(cotangent, cotangent_others, downward_weight, act, gain_hidden)
     lifted = [(lifted_own, None)] + [(lifted_others, n) for n in range(3)]
-    cotangents = [(cotangent, None)] + [(cotangent_others, n) for n in range(3)]
+    cotangents = [(value, None) for value in [cotangent] + cotangent_others]
     sums = sums + back_sums
     others = [flip(sums, "mp", k) for k in range(1, 4)]
     sums = jnp.stack(
@@ -1595,18 +1687,13 @@
     down_grad = lax.psum_scatter(
         weight_grad(ids, split(squashed), [cotangents], False), "dp", scatter_dimension=2, tiled=True
     )[0]
-    down_got = flip(down_grad[hidden_local:], "mp", 4)
     middle_grad, middle_low, own_grads, other_grads, mid_gains = mid_backward(
         ids, (lifted_kept, lifted_got), middle, cotangent, context, outward_weight, gain_mid, gain_ctx
     )
     context_heads = [turn_heads(own_grads), turn_heads(other_grads)]
-    outward_blocks = [
-        part[0] for part in weight_grad(ids, whole([mixed]), [whole([middle_low])], True, None, True)
-    ]
     up_grad = lax.psum_scatter(
         weight_grad(ids, lifted, [split(hidden_grad)], True), "dp", scatter_dimension=1, tiled=True
     )[0]
-    up_got = flip(up_grad[:, hidden_local:], "mp", 4)
     ffn_parts = [ffn_out(ids, squashed, j, downward_weight) for j in range(4)]
 
     def scatter_tokens(parts):
@@ -1619,52 +1706,50 @@
 
     ffn_kept, ffn_got = scatter_tokens(ffn_parts)
     output_rows = (middle + (ffn_kept.astype(WIDE) + ffn_got.astype(WIDE))).astype(LOW)
-    layer_output = give_back(output_rows.reshape(2, local_len, model_width))
-
-    def scatter_blocks(blocks, one, two):
-        passed = add_low(blocks[3 - one], flip(blocks[3], "dp", one))
-        return add_low(add_low(blocks[0], flip(blocks[one], "dp", one)), flip(passed, "dp", two))
-
-    head_grads, head_sides = [None, None], [None, None]
+    output_rows = output_rows.reshape(2, local_len, model_width)
+
+    head_grads, head_sides, backs = [None, None], [None, None], [None, None]
+    leaving = (pick(output_rows, 1 - side), down_grad[hidden_local:])
     for half in (1, 0):
-        head_grads[half] = attend_back(
-            ids, queries[half], keys[half], values[half], context_heads[half], contexts[half], logs[half], tables
+        *head_grads[half], backs[half] = attend_back(
+            queries[half],
+            keys[half],
+            values[half],
+            context_heads[half],
+            contexts[half],
+            logs[half],
+            tables,
+            leaving[half],
+            4 + half,
+            [ffn_kept] if half else [],
         )
-        blocks = weight_grad(ids, whole(normed), [whole(g) for g in head_grads[half]], True, None, True)
-        head_sides[half] = scatter_blocks(blocks, 1, 2)
-    head_sum = head_sides[0].astype(WIDE) + flip(head_sides[1], "mp", 4).astype(WIDE)
-    normed_parts = [None] * 4
-    for j in (3, 2, 1, 0):
-        pieces = [group[j] for half in head_grads for group in half]
-        normed_parts[j] = unproject(ids, pieces, head_weight)
-    normed_kept, normed_got = scatter_tokens(normed_parts)
+        head_part = weight_grad(ids, whole(normed), [split(g) for g in head_grads[half]], True)
+        head_sides[half] = lax.psum_scatter(head_part, "dp", scatter_dimension=1, tiled=True)
+        if half == 1:
+            outward_part = weight_grad(ids, whole([mixed]), [whole([middle_low])], True, [head_part])[0]
+            outward_sent = lax.dynamic_slice_in_dim(outward_part, (1 - core) * half_width, half_width, 1)
+            outward_half = add_low(
+                lax.dynamic_slice_in_dim(outward_part, core * half_width, half_width, 1), flip(outward_sent, "mp", 1)
+            )
+    output_got, down_got = backs
+    layer_output = both(pick(output_rows, side), output_got)
+    normed_kept, normed_got, up_got, head_got_grad = unproject(
+        head_grads[0] + head_grads[1], head_weight, [up_grad[:, hidden_local:], head_sides[1]]
+    )
+    head_sum = head_sides[0].astype(WIDE) + head_got_grad.astype(WIDE)
     normed_grad = normed_kept.astype(WIDE) + normed_got.astype(WIDE)
     _, input_back = jax.vjp(layer_norm, merged.astype(WIDE), gain_in)
     merged_part, in_gain_grad = input_back(normed_grad)
     input_grad = give_back((middle_grad + merged_part).reshape(2, local_len, model_width))
 
-    outward_blocks = [
-        add_low(
-            lax.dynamic_slice_in_dim(part, core * half_width, half_width, 1),
-            flip(lax.dynamic_slice_in_dim(part, (1 - core) * half_width, half_width, 1), "mp", 1),
-        )
-        for part in outward_blocks
-    ]
-    outward_grad = scatter_blocks(outward_blocks, 2, 1)
-    low_bit = (rank // 2) % 2
-    for mask, bit in ((2, low_bit), (4, side)):
-        size = outward_grad.shape[0] // 2
-        outward_grad = add_low(
-            lax.dynamic_slice_in_dim(outward_grad, bit * size, size, 0),
-            flip(lax.dynamic_slice_in_dim(outward_grad, (1 - bit) * size, size, 0), "mp", mask),
-        )
-    for mask, bit, axis in ((4, side, 0), (2, low_bit, 0), (1, core, 1)):
-        got = flip(outward_grad, "mp", mask)
-        outward_grad = jnp.where(
-            bit == 0,
-            jnp.concatenate([outward_grad, got], axis=axis),
-            jnp.concatenate([got, outward_grad], axis=axis),
-        )
+    outward_grad = lax.psum_scatter(outward_half, "dp", scatter_dimension=0, tiled=True)
+    outward_grad = lax.psum(outward_grad, "mp", axis_index_groups=[[0, 2, 4, 6], [1, 3, 5, 7]])
+    outward_got = flip(outward_grad, "mp", 1)
+    outward_grad = jnp.where(
+        core == 0,
+        jnp.concatenate([outward_grad, outward_got], axis=1),
+        jnp.concatenate([outward_got, outward_grad], axis=1),
+    )
     outward_sum = outward_grad.astype(WIDE)
 
     down_sum = down_grad[:hidden_local].astype(WIDE) + down_got.astype(WIDE)
@@ -1680,26 +1765,21 @@
         down_sum, downward_master, downward_moment, downward_square, DECAY_RATE
     )
     owner = (model_rank == 0).astype(WIDE)
-    norm_early = sum_everywhere(
-        jnp.concatenate(
-            [
-                pair_sums(outward_master, outward_dir) * owner,
-                pair_sums(upward_master, upward_dir),
-                pair_sums(downward_master, downward_dir),
-            ],
-            axis=0,
-        )
-    )
-    head_part = jnp.stack(
-        [jnp.sum(head_master * head_master, axis=(1, 2)), jnp.sum(head_dir * head_dir, axis=(1, 2))], axis=-1
+    norm_part = jnp.concatenate(
+        [
+            jnp.stack([jnp.sum(head_master * head_master, axis=(1, 2)), jnp.sum(head_dir * head_dir, axis=(1, 2))], axis=-1),
+            pair_sums(outward_master, outward_dir) * owner,
+            pair_sums(upward_master, upward_dir),
+            pair_sums(downward_master, downward_dir),
+        ],
+        axis=0,
     )
     hidden_gain = hidden_gains[0]
     gains_part = jnp.concatenate([in_gain_grad[0], mid_gains[1], mid_gains[0], jnp.zeros((hidden_width,), WIDE)])
     gains_part = lax.dynamic_update_slice(gains_part, hidden_gain[:hidden_local], (hidden_start,))
     gains_part = lax.dynamic_update_slice(gains_part, hidden_gain[hidden_local:], (other_start,))
-    gains_sum = sum_everywhere(gains_part)
-    head_norms = sum_everywhere(head_part)
-    norm_sums = jnp.concatenate([head_norms, norm_early], axis=0)
+    every = sum_everywhere(jnp.concatenate([gains_part, norm_part.reshape(-1)]))
+    gains_sum, norm_sums = every[: gains_part.shape[0]], every[gains_part.shape[0] :].reshape(6, 2)
     moment_gains, square_gains, gains_dir = adapt_step(gains_sum, gains_master, gains_moment, gains_square, 0.0)
     gains_sums = jnp.stack(
         [
@@ -1709,11 +1789,11 @@
         axis=-1,
     )
     updated_head = trust_move(
-        head_master, head_dir, head_norms[:, 0][:, None, None], head_norms[:, 1][:, None, None]
-    )
-    updated_outward = trust_move(outward_master, outward_dir, norm_early[0, 0], norm_early[0, 1])
-    updated_upward = trust_move(upward_master, upward_dir, norm_early[1, 0], norm_early[1, 1])
-    updated_downward = trust_move(downward_master, downward_dir, norm_early[2, 0], norm_early[2, 1])
+        head_master, head_dir, norm_sums[:3, 0][:, None, None], norm_sums[:3, 1][:, None, None]
+    )
+    updated_outward = trust_move(outward_master, outward_dir, norm_sums[3, 0], norm_sums[3, 1])
+    updated_upward = trust_move(upward_master, upward_dir, norm_sums[4, 0], norm_sums[4, 1])
+    updated_downward = trust_move(downward_master, downward_dir, norm_sums[5, 0], norm_sums[5, 1])
     updated_gains = trust_move(
         gains_master,
         gains_dir,

time: 1310 us -> 1190 us (0.908)
  waiting for transfers between devices: 364 us -> 186 us
  Pallas kernels: 726 us -> 795 us
  starting transfers between devices: 52.6 us -> 20 us
    ppermute x62 -> x31, waiting for transfers between devices: 364 us -> 127 us  [flip(): lax.ppermute(value, axis, [(i, i ^ mask) for i in range(lax.axis_size(axi...]
    pallas_call x29 -> x26, Pallas kernels: 564 us -> 633 us  [the longest x21 260 us: kernel_call(): pl.pallas_call(whole, grid_spec=pltpu.PrefetchScalarGridSpec(num_scalar_p...]
    psum x0 -> x1, waiting for transfers between devices: none -> 39.2 us  [on_device_paired(): lax.psum(outward_grad, 'mp', axis_index_groups=[[0, 2, 4, 6], [1, 3, 5, 7]])]
    ppermute x62 -> x31, starting transfers between devices: 52.1 us -> 19.4 us  [flip(): lax.ppermute(value, axis, [(i, i ^ mask) for i in range(lax.axis_size(axi...]
    all_gather x1, waiting for transfers between devices: 0.02 us -> 18.1 us  [on_device_paired(): downward_weight = [lax.all_gather(downward_own, 'dp', axis=1, tiled=True)]]
  transfers between devices with their start and end apart: 69 -> 42, of which waited for: 29 -> 19; matrix products, arithmetic and copies ran while one was open for 8% -> 7% of each run, Pallas kernels for 36% -> 43%
where the time goes in v3:
time: 1190 us; the launch traced here: 1180 us
  Pallas kernels  795 us (67%)
  waiting for transfers between devices  186 us (16%)
  other arithmetic  122 us (10%)
  local copies, waits for them, and re-layouts  38.4 us (3%)
  starting transfers between devices  20 us (2%)
  between operations  19.4 us (2%)
    pallas_call x21, Pallas kernels, kernel_call(): pl.pallas_call(whole, grid_spec=pltpu.PrefetchScalarGridSpec(num_scalar_p...  260 us
    ppermute x31, waiting for transfers between devices, flip(): lax.ppermute(value, axis, [(i, i ^ mask) for i in range(lax.axis_size(axi...  127 us
    pallas_call x2, Pallas kernels, attend_back(): pl.pallas_call(partial(attend_back_kernel, bq=block, bk=block), grid=(pai...  109 us
    pallas_call x1, Pallas kernels, unproject(): pl.pallas_call(unproject_kernel, grid=(4, 2), in_specs=[line] * 6 + [stil...  99.1 us
    pallas_call x1, Pallas kernels, normed_exchange(): pl.pallas_call(normed_kernel, in_specs=[ANYWHERE] * 4, out_specs=[ANYWHER...  94 us
    pallas_call x1, Pallas kernels, ffn_second(): pl.pallas_call(partial(ffn_second_kernel, hidden_width=hidden_width), gri...  71.6 us
    pallas_call x1, Pallas kernels, ffn_up(): pl.pallas_call(ffn_up_kernel, grid=(4, 2 * count), in_specs=[ANYWHERE] +...  70.8 us
    pallas_call x1, Pallas kernels, open_exchange(): pl.pallas_call(open_kernel, in_specs=[ANYWHERE] * 2, out_specs=[ANYWHERE]...  51.4 us
  transfers between devices with their start and end apart: 42, of which 19 were waited for; matrix products, arithmetic and copies ran while one was open for 7% of the time, Pallas kernels for 43%

profile of v3, /device:TPU:0, one launch (start us, length us, event | category | flops | bytes accessed | tf_op | source)
XLA Modules:
  0.0 1183.2 jit_solution(17828077704469645242)
XLA Ops:
  14.5 51.4 %shard_map.363 = (bf16[256,2048]{1,0:T(8,128)(2,1)}, bf16[3,512,256]{2,1,0:T(8,128)(2,1)}, bf16[3,512,256]{2,1,0:T(8,128)(2,1)}, bf16[3,512,256]{2,1,0:T(8,128)(2,1)}) custom-call(bf16[256,2048]{1,0:T(8,128)(2,1)} %get-tuple-element.280.text, bf16[3,512,256]{2,1,0:T(8,128)(2,1)} %convert_element_type.115.head.refs_2_.refs_6_), custom_call_target="tpu_custom_call" | custom-call | bytes 104857600 | tf_op jit(solution)/shard_map/pallas_call | solution.py:1475
  82.5 94.0 %shard_map.365 = (bf16[512,2048]{1,0:T(8,128)(2,1)}, bf16[512,2048]{1,0:T(8,128)(2,1)}, bf16[512,2048]{1,0:T(8,128)(2,1)}, bf16[3,512,256]{2,1,0:T(8,128)(2,1)},...) custom-call(bf16[512,2048]{1,0:T(8,128)(2,1)} %fusion.7.refs_1_.normed, ...), custom_call_target="tpu_custom_call" | custom-call | bytes 104857600 | tf_op jit(solution)/shard_map/pallas_call | solution.py:1520
  256.7 18.1 %all-gather.12.cloned.1.call-done.down_own.refs_2_ = bf16[1024,2048]{1,0:T(8,128)(2,1)} async-done(((bf16[1024,512]{1,0:T(8,128)(2,1)}), bf16[1024,2048]{1,0:T(8,128)(2,1)}) %all-gather.12.cloned.1.call-update) | async-done | bytes 4194320 | tf_op jit(solution)/shard_map/all_gather | solution.py:1593
  274.8 22.8 %shard_map.369 = (bf16[512,256]{1,0:T(8,128)(2,1)}, bf16[512,256]{1,0:T(8,128)(2,1)}, bf16[512,256]{1,0:T(8,128)(2,1)}, bf16[512,256]{1,0:T(8,128)(2,1)}, f32[2,...) custom-call(s32[3]{0:T(128)} %pad_add_fusion.refs_0_, ...), custom_call_target="tpu_custom_call", output_to_operand_aliasing={{5}: (13, {})} | custom-call | flops 12000000000 | bytes 3000000 | tf_op jit(solution)/shard_map/pallas_call | solution.py:475
  300.1 22.8 %shard_map.374 = (bf16[512,256]{1,0:T(8,128)(2,1)}, bf16[512,256]{1,0:T(8,128)(2,1)}, bf16[512,256]{1,0:T(8,128)(2,1)}, bf16[512,256]{1,0:T(8,128)(2,1)}, f32[2,2,2048]{2,1,0:T(2,128)}) custom-call(s32[3]{0:T(128)} %pad_add_fusion.refs_0_, bf16[512,256]{1,0:T(8,128)(2,1)} %get-tuple-element.131.refs_1_.refs_0_, ...), custom_call_target="tpu_custom_call" | custom-call | flops 12000000000 | bytes 3000000 | tf_op jit(solution)/shard_map/pallas_call | solution.py:475
  326.7 25.2 %collective-permute-done.4.refs_7_ = bf16[512,256]{1,0:T(8,128)(2,1)} collective-permute-done((bf16[512,256]{1,0:T(8,128)(2,1)}, bf16[512,256]{1,0:T(8,128)(2,1)}, u32[]{:S(2)}, u32[]{:S(2)}) %collective-permute-start.4) | collective-permute-done | bytes 262176 | tf_op jit(solution)/shard_map/ppermute | solution.py:1407
  369.7 14.1 %shard_map.375 = (bf16[512,2048]{1,0:T(8,128)(2,1)}, bf16[512,2048]{1,0:T(8,128)(2,1)}, f32[512,2048]{1,0:T(8,128)}, bf16[512,2048]{1,0:T(8,128)(2,1)}, bf16[1024,512]{1,0:T(8,128)(2,1)}) custom-call(s32[3]{0:T(128)} %pad_add_fusion.refs_0_, bf16[512,256]{1,0:T(8,128)(2,1)} %get-tuple-element.126.refs_1_.refs_16_, ...), custom_call_target="tpu_custom_call", output_to_operand_aliasing={{4}: (16, {})} | custom-call | flops 1288490240 | bytes 6920601 | tf_op jit(solution)/shard_map/pallas_call | solution.py:475
  384.4 70.8 %shard_map.376 = (bf16[4,512,2048]{2,1,0:T(8,128)(2,1)}, bf16[4,512,2048]{2,1,0:T(8,128)(2,1)}, f32[4,8,512]{2,1,0:T(8,128)}, bf16[3,512,2048]{2,1,0:T(8,128)(2,1)}) custom-call(bf16[512,2048]{1,0:T(8,128)(2,1)} %get-tuple-element.151.lifted.refs_1_, bf16[2048,1024]{1,0:T(8,128)(2,1)} %all-gather.8.cloned.1.call-done.up_own, ...), custom_call_target="tpu_custom_call" | custom-call | flops 80000000000 | bytes 104857600 | tf_op jit(solution)/shard_map/pallas_call | solution.py:1011
  455.3 38.9 %shard_map.377 = (bf16[4,512,2048]{2,1,0:T(8,128)(2,1)}, f32[4,8,512]{2,1,0:T(8,128)}) custom-call(bf16[512,2048]{1,0:T(8,128)(2,1)} %bitcast.87, bf16[512,2048]{1,0:T(8,128)(2,1)} %collective-permute-done.8.near.refs_6_, bf16[512,2048]{1,0:T(8,128)(2,1)} %collective-permute-done.9.far.refs_7_, bf16[512,2048]{1,0:T(8,128)(2,1)} %collective-permute-done.10.last.refs_8_, ...), custom_call_target="tpu_custom_call" | custom-call | flops 60000002048 | bytes 104857600 | tf_op jit(solution)/shard_map/pallas_call | solution.py:1073
  501.4 71.6 %shard_map.378 = (bf16[4,512,2048]{2,1,0:T(8,128)(2,1)}, bf16[4,512,2048]{2,1,0:T(8,128)(2,1)}, bf16[512,2048]{1,0:T(8,128)(2,1)}, bf16[512,2048]{1,0:T(8,128)(2,1)}, f32[8,2048]{1,0:T(8,128)}) custom-call(bf16[4,512,2048]{2,1,0:T(8,128)(2,1)} %get-tuple-element.153.act, bf16[4,512,2048]{2,1,0:T(8,128)(2,1)} %get-tuple-element.154.slope, ...), custom_call_target="tpu_custom_call" | custom-call | flops 80000000000 | bytes 104857600 | tf_op jit(solution)/shard_map/pallas_call | solution.py:1183
  573.0 27.3 %shard_map.385 = bf16[1,2048,2048]{2,1,0:T(8,128)(2,1)} custom-call(s32[3]{0:T(128)} %pad_add_fusion.refs_0_, bf16[4,512,2048]{2,1,0:T(8,128)(2,1)} %get-tuple-element.159.refs_1_.refs_2_.refs_3_.refs_4_, bf16[4,512,2048]{2,1,0:T(8,128)(2,1)} %get-tuple-element.159.refs_1_.refs_2_.refs_3_.refs_4_, ...), custom_call_target="tpu_custom_call" | custom-call | flops 5153960960 | bytes 12582912 | tf_op jit(solution)/shard_map/pallas_call | solution.py:475
  600.4 24.7 %shard_map.387 = bf16[1,2048,2048]{2,1,0:T(8,128)(2,1)} custom-call(s32[3]{0:T(128)} %pad_add_fusion.refs_0_, bf16[512,2048]{1,0:T(8,128)(2,1)} %get-tuple-element.151.lifted.refs_1_, bf16[3,512,2048]{2,1,0:T(8,128)(2,1)} %get-tuple-element.181.refs_2_.refs_3_.refs_4_, bf16[3,512,2048]{2,1,0:T(8,128)(2,1)} %get-tuple-element.181.refs_2_.refs_3_.refs_4_, ...), custom_call_target="tpu_custom_call" | custom-call | flops 5153960960 | bytes 12582912 | tf_op jit(solution)/shard_map/pallas_call | solution.py:475
  625.1 11.4 shard_map.382
  636.6 10.9 shard_map.380
  663.4 20.9 %shard_map.383 = (f32[512,2048]{1,0:T(8,128)}, bf16[512,2048]{1,0:T(8,128)(2,1)}, bf16[512,256]{1,0:T(8,128)(2,1)}, bf16[512,256]{1,0:T(8,128)(2,1)}, bf16[512,2...) custom-call(s32[3]{0:T(128)} %pad_add_fusion.refs_0_, ...), custom_call_target="tpu_custom_call" | custom-call | flops 1288490240 | bytes 8178892 | tf_op jit(solution)/shard_map/pallas_call | solution.py:475
  686.2 11.0 shard_map.379
  698.6 12.5 %collective-permute-done.16 = bf16[512,2048]{1,0:T(8,128)(2,1)} collective-permute-done((bf16[512,2048]{1,0:T(8,128)(2,1)}, bf16[512,2048]{1,0:T(8,128)(2,1)}, u32[]{:S(2)}, u32[]{:S(2)}) %collective-permute-start.16) | collective-permute-done | bytes 2097184 | tf_op jit(solution)/shard_map/ppermute | solution.py:1407
  721.3 54.5 %shard_map.386 = (bf16[4,512,256]{2,1,0:T(8,128)(2,1)}, bf16[4,512,256]{2,1,0:T(8,128)(2,1)}, bf16[4,512,256]{2,1,0:T(8,128)(2,1)}, bf16[1024,512]{1,0:T(8,128)(2,1)}) custom-call(bf16[512,256]{1,0:T(8,128)(2,1)} %get-tuple-element.131.refs_1_.refs_0_, bf16[512,256]{1,0:T(8,128)(2,1)} %get-tuple-element.132.refs_2_.refs_1_, ...), custom_call_target="tpu_custom_call" | custom-call | flops 40000000000 | bytes 20971520 | tf_op jit(solution)/shard_map/pallas_call | solution.py:722
  775.8 11.8 shard_map.388.refs_3_
  825.9 54.4 %shard_map.384 = (bf16[4,512,256]{2,1,0:T(8,128)(2,1)}, bf16[4,512,256]{2,1,0:T(8,128)(2,1)}, bf16[4,512,256]{2,1,0:T(8,128)(2,1)}, bf16[256,2048]{1,0:T(8,128)(2,1)}) custom-call(bf16[512,256]{1,0:T(8,128)(2,1)} %get-tuple-element.111.refs_1_.refs_0_, bf16[512,256]{1,0:T(8,128)(2,1)} %get-tuple-element.113.refs_2_.refs_1_, ...), custom_call_target="tpu_custom_call" | custom-call | flops 40000000000 | bytes 20971520 | tf_op jit(solution)/shard_map/pallas_call | solution.py:722
  880.3 11.9 %shard_map.390 = bf16[3,2048,256]{2,1,0:T(8,128)(2,1)} custom-call(s32[3]{0:T(128)} %pad_add_fusion.refs_0_, bf16[512,2048]{1,0:T(8,128)(2,1)} %fusion.7.refs_1_.normed, bf16[512,2048]{1,0:T(8,128)(2,1)} %get-tuple-element.112.refs_1_.refs_2_, bf16[512,2048]{1,0:T(8,128)(2,1)} %get-tuple-element.114.refs_1_.refs_3_, ...), custom_call_target="tpu_custom_call" | custom-call | flops 1932735232 | bytes 6291456 | tf_op jit(solution)/shard_map/pallas_call | solution.py:475
  904.1 99.1 %shard_map.389 = (bf16[512,2048]{1,0:T(8,128)(2,1)}, bf16[512,2048]{1,0:T(8,128)(2,1)}, bf16[512,1024]{1,0:T(8,128)(2,1)}, bf16[3,512,256]{2,1,0:T(8,128)(2,1)}) custom-call(bf16[4,512,256]{2,1,0:T(8,128)(2,1)} %get-tuple-element.170.refs_0_.refs_5_.refs_6_.refs_7_.refs_8_, ...), custom_call_target="tpu_custom_call" | custom-call | flops 40000000000 | bytes 20971520 | tf_op jit(solution)/shard_map/pallas_call | solution.py:1313
  1020.5 39.2 %all-reduce.2.cloned.1.call-done = bf16[512,1024]{1,0:T(8,128)(2,1)} async-done(((bf16[512,1024]{1,0:T(8,128)(2,1)}), bf16[512,1024]{1,0:T(8,128)(2,1)}) %all-reduce.2.cloned.1.call-update) | async-done | bytes 1048592 | tf_op jit(solution)/shard_map/psum | solution.py:1746
  1091.7 40.5 %collective-permute-done.23 = bf16[256,2048]{1,0:T(8,128)(2,1)S(1)} collective-permute-done((bf16[256,2048]{1,0:T(8,128)(2,1)S(1)}, bf16[256,2048]{1,0:T(8,128)(2,1)S(1)}, u32[]{:S(2)}, u32[]{:S(2)}) %collective-permute-start.23) | collective-permute-done | bytes 1048608 | tf_op jit(solution)/shard_map/ppermute | solution.py:1407
  (331 shorter events, 304.0 us)
Async XLA Ops:
  7.2 223.6 %all-gather.6.cloned.1.call-start = ((), (), s32[]{:S(2)}) async-start(), calls=%async_computation.5 | async-start | bytes 3932160 | tf_op jit(solution)/shard_map/all_gather | solution.py:1643
  176.5 98.3 %all-gather.12.cloned.1.call-start = ((), (), s32[]{:S(2)}) async-start(), calls=%async_computation.8 | async-start | bytes 5242880 | tf_op jit(solution)/shard_map/all_gather | solution.py:1593
  177.7 206.1 %all-gather.10.cloned.1.call-start = ((), (), s32[]{:S(2)}) async-start(), calls=%async_computation.7 | async-start | bytes 5242880 | tf_op jit(solution)/shard_map/all_gather | solution.py:1644
  178.4 206.0 %all-gather.8.cloned.1.call-start = ((), (), s32[]{:S(2)}) async-start(), calls=%async_computation.6 | async-start | bytes 5242880 | tf_op jit(solution)/shard_map/all_gather | solution.py:1589
  179.0 276.3 %all-gather.14.cloned.1.call-start = ((), (), s32[]{:S(2)}) async-start(), calls=%async_computation.9 | async-start | bytes 5242880 | tf_op jit(solution)/shard_map/all_gather | solution.py:1667
  180.5 48.1 %collective-permute-start.7 = (bf16[256,2048]{1,0:T(8,128)(2,1)}, bf16[256,2048]{1,0:T(8,128)(2,1)}, u32[]{:S(2)}, u32[]{:S(2)}) collective-permute-start(bf16[256,2048]{1,0:T(8,128)(2,1)} %get-tuple-element.276), channel_id=1, source_target_pairs={{0,4},{1,5},{2,6},{3,7},{4,0},{5,1},{6,2},{7,3},{8,12},{9,13},{10,... | collective-permute-start | bytes 3145736 | tf_op jit(solution)/shard_map/ppermute | solution.py:1407
  230.7 94.1 %collective-permute-start.9 = (bf16[512,2048]{1,0:T(8,128)(2,1)S(1)}, bf16[512,2048]{1,0:T(8,128)(2,1)}, u32[]{:S(2)}, u32[]{:S(2)}) collective-permute-start(bf16[512,2048]{1,0:T(8,128)(2,1)S(1)} %bitcast.85), channel_id=1, source_target_pairs={{0,2},{1,3},{2,0},{3,1},{4,6},{5,7},{6,4},{7,5},{8,10},{9,11},{10,... | collective-permute-start | bytes 6291464 | tf_op jit(solution)/shard_map/ppermute | solution.py:1407
  297.6 71.1 %collective-permute-start.6 = (bf16[1024,512]{1,0:T(8,128)(2,1)}, bf16[1024,512]{1,0:T(8,128)(2,1)S(1)}, u32[]{:S(2)}, u32[]{:S(2)}) collective-permute-start(bf16[1024,512]{1,0:T(8,128)(2,1)} %get-tuple-element.149), channel_id=1, source_target_pairs={{0,4},{1,5},{2,6},{3,7},{4,0},{5,1},{6,2},{7,3},{8,12},{9,13},{10,... | collective-permute-start | bytes 3145736 | tf_op jit(solution)/shard_map/ppermute | solution.py:1407
  325.2 38.0 %collective-permute-start.1 = (bf16[512,256]{1,0:T(8,128)(2,1)}, bf16[512,256]{1,0:T(8,128)(2,1)}, u32[]{:S(2)}, u32[]{:S(2)}) collective-permute-start(bf16[512,256]{1,0:T(8,128)(2,1)} %get-tuple-element.128.refs_18_), channel_id=1, source_target_pairs={{0,2},{1,3},{2,0},{3,1},{4,6},{5,7},{6,4},{7,5},{8,10},{9,11},{10,... | collective-permute-start | bytes 786440 | tf_op jit(solution)/shard_map/ppermute | solution.py:1407
  357.4 97.8 %collective-permute-start.8 = (bf16[512,2048]{1,0:T(8,128)(2,1)S(1)}, bf16[512,2048]{1,0:T(8,128)(2,1)}, u32[]{:S(2)}, u32[]{:S(2)}) collective-permute-start(bf16[512,2048]{1,0:T(8,128)(2,1)S(1)} %bitcast.86), channel_id=1, source_target_pairs={{0,1},{1,0},{2,3},{3,2},{4,5},{5,4},{6,7},{7,6},{8,9},{9,8},{10,11... | collective-permute-start | bytes 6291464 | tf_op jit(solution)/shard_map/ppermute | solution.py:1407
  357.6 97.7 %collective-permute-start.10 = (bf16[512,2048]{1,0:T(8,128)(2,1)}, bf16[512,2048]{1,0:T(8,128)(2,1)}, u32[]{:S(2)}, u32[]{:S(2)}) collective-permute-start(bf16[512,2048]{1,0:T(8,128)(2,1)} %collective-permute-done.9.far.refs_7_), channel_id=1, source_target_pairs={{0,1},{1,0},{2,3},{3,2},{4,5},{5,4},{6,7},{7,6},{8,9},{9,8},{10,11... | collective-permute-start | bytes 6291464 | tf_op jit(solution)/shard_map/ppermute | solution.py:1407
  383.8 333.6 %reduce-scatter.6.cloned.1.call-start = ((), (), s32[]{:S(2)}) async-start(), calls=%async_computation.10 | async-start | bytes 10485760 | tf_op jit(solution)/shard_map/reduce_scatter | solution.py:1687
  600.4 292.9 %reduce-scatter.8.cloned.1.call-start = ((), (), s32[]{:S(2)}) async-start(), calls=%async_computation.11 | async-start | bytes 10485760 | tf_op jit(solution)/shard_map/reduce_scatter | solution.py:1694
  625.1 278.9 %reduce-scatter.10.cloned.1.call-start = ((), (), s32[]{:S(2)}) async-start(), calls=%async_computation.12 | async-start | bytes 3932160 | tf_op jit(solution)/shard_map/reduce_scatter | solution.py:1727
  647.5 49.8 %collective-permute-start.14 = (bf16[512,2048]{1,0:T(8,128)(2,1)}, bf16[512,2048]{1,0:T(8,128)(2,1)S(1)}, u32[]{:S(2)}, u32[]{:S(2)}) collective-permute-start(bf16[512,2048]{1,0:T(8,128)(2,1)} %shard_map.380), channel_id=1, source_target_pairs={{0,1},{1,0},{2,3},{3,2},{4,5},{5,4},{6,7},{7,6},{8,9},{9,8},{10,11... | collective-permute-start | bytes 6291464 | tf_op jit(solution)/shard_map/ppermute | solution.py:1407
  662.3 48.8 %collective-permute-start.16 = (bf16[512,2048]{1,0:T(8,128)(2,1)}, bf16[512,2048]{1,0:T(8,128)(2,1)}, u32[]{:S(2)}, u32[]{:S(2)}) collective-permute-start(bf16[512,2048]{1,0:T(8,128)(2,1)} %add_convert_fusion.1), channel_id=1, source_target_pairs={{0,2},{1,3},{2,0},{3,1},{4,6},{5,7},{6,4},{7,5},{8,10},{9,11},{10,... | collective-permute-start | bytes 6291464 | tf_op jit(solution)/shard_map/ppermute | solution.py:1407
  684.3 35.3 %collective-permute-start.20 = (bf16[512,256]{1,0:T(8,128)(2,1)}, bf16[512,256]{1,0:T(8,128)(2,1)S(1)}, u32[]{:S(2)}, u32[]{:S(2)}) collective-permute-start(bf16[512,256]{1,0:T(8,128)(2,1)} %get-tuple-element.174), channel_id=1, source_target_pairs={{0,1},{1,0},{2,3},{3,2},{4,5},{5,4},{6,7},{7,6},{8,9},{9,8},{10,11... | collective-permute-start | bytes 786440 | tf_op jit(solution)/shard_map/ppermute | solution.py:1407
  684.4 35.2 %collective-permute-start.21 = (bf16[512,256]{1,0:T(8,128)(2,1)}, bf16[512,256]{1,0:T(8,128)(2,1)S(1)}, u32[]{:S(2)}, u32[]{:S(2)}) collective-permute-start(bf16[512,256]{1,0:T(8,128)(2,1)} %get-tuple-element.175), channel_id=1, source_target_pairs={{0,2},{1,3},{2,0},{3,1},{4,6},{5,7},{6,4},{7,5},{8,10},{9,11},{10,... | collective-permute-start | bytes 786440 | tf_op jit(solution)/shard_map/ppermute | solution.py:1407
  685.2 35.4 %collective-permute-start.22 = (bf16[512,256]{1,0:T(8,128)(2,1)}, bf16[512,256]{1,0:T(8,128)(2,1)S(1)}, u32[]{:S(2)}, u32[]{:S(2)}) collective-permute-start(bf16[512,256]{1,0:T(8,128)(2,1)} %get-tuple-element.176), channel_id=1, source_target_pairs={{0,3},{1,2},{2,1},{3,0},{4,7},{5,6},{6,5},{7,4},{8,11},{9,10},{10,... | collective-permute-start | bytes 786440 | tf_op jit(solution)/shard_map/ppermute | solution.py:1407
  787.6 221.7 %reduce-scatter.14.cloned.1.call-start = ((), (), s32[]{:S(2)}) async-start(), calls=%async_computation.14 | async-start | bytes 5242880 | tf_op jit(solution)/shard_map/reduce_scatter | solution.py:1745
  811.1 198.2 %reduce-scatter.12.cloned.1.call-start = ((), (), s32[]{:S(2)}) async-start(), calls=%async_computation.13 | async-start | bytes 3932160 | tf_op jit(solution)/shard_map/reduce_scatter | solution.py:1727
  892.2 167.4 %all-reduce.2.cloned.1.call-start = ((), (), s32[]{:S(2)}) async-start(), calls=%async_computation.15 | async-start | bytes 2097152 | tf_op jit(solution)/shard_map/psum | solution.py:1746
  1083.5 48.7 %collective-permute-start.23 = (bf16[256,2048]{1,0:T(8,128)(2,1)S(1)}, bf16[256,2048]{1,0:T(8,128)(2,1)S(1)}, u32[]{:S(2)}, u32[]{:S(2)}) collective-permute-start(bf16[256,2048]{1,0:T(8,128)(2,1)S(1)} %fusion.25), channel_id=1, source_target_pairs={{0,4},{1,5},{2,6},{3,7},{4,0},{5,1},{6,2},{7,3},{8,12},{9,13},{10,... | collective-permute-start | bytes 3145736 | tf_op jit(solution)/shard_map/ppermute | solution.py:1407
  1091.0 41.5 %collective-permute-start.29 = (f32[14348]{0:T(1024)S(1)}, f32[14348]{0:T(1024)S(1)}, u32[]{:S(2)}, u32[]{:S(2)}) collective-permute-start(f32[14348]{0:T(1024)S(1)} %add.422), channel_id=1, source_target_pairs={{0,2},{1,3},{2,0},{3,1},{4,6},{5,7},{6,4},{7,5},{8,10},{9,11},{10,... | collective-permute-start | bytes 172184 | tf_op jit(solution)/shard_map/ppermute | solution.py:1407
  (82 other events, 1169.3 us)
Sparse Core Ops, SparseCore 0:
  176.6 43.1 all-gather.5
  222.2 52.5 all-gather.11
  276.6 52.7 all-gather.9
  331.7 52.6 all-gather.7
  386.7 52.5 all-gather.13
  600.5 85.9 reduce-scatter.5
  689.9 86.3 reduce-scatter.7
  787.7 43.3 reduce-scatter.9
  834.7 52.6 reduce-scatter.13
  892.3 43.0 reduce-scatter.11
  1009.4 50.1 all-reduce.1

commit v4 on v3

--- a/solution.py
+++ b/solution.py
@@ -492,6 +492,16 @@
     return (rank, rank + 1 - 2 * (rank % 2), (rank + 2) % 4, 3 - rank)[j]
 
 
+def hand_on(value, done):
+    return pl.pallas_call(
+        lambda *refs: None,
+        in_specs=[ANYWHERE] * (1 + len(done)),
+        out_specs=ANYWHERE,
+        out_shape=like(value),
+        input_output_aliases={0: 0},
+    )(value, *done)
+
+
 def own_rows(sub, rank, j, b):
     return pl.ds(pl.multiple_of(b * 4 * sub + mate(rank, j) * sub, sub), sub)
 
@@ -532,7 +542,7 @@
     ]
 
 
-def project(ids, x, weight, tables, j):
+def project(ids, x, weight, tables, j, done=(), carry=()):
     rows, model = x.shape
     sub = rows // 2
     weights, specs = quarters(weight)
@@ -549,6 +559,8 @@
         6 * rows * model * width,
         6 * model * width + 8 * rows * model,
         (ids, x, *weights, *tables),
+        done,
+        carry,
     )
 
 
@@ -877,9 +889,9 @@
 
 
 def fold(block):
-    out = block[:, :LANES]
-    for p in range(1, block.shape[1] // LANES):
-        out = out + block[:, p * LANES : (p + 1) * LANES]
+    out = block[..., :LANES]
+    for p in range(1, block.shape[-1] // LANES):
+        out = out + block[..., p * LANES : (p + 1) * LANES]
     return out
 
 
@@ -1240,8 +1252,8 @@
 
 def unproject_kernel(*refs):
     grads, owns, got_weight, away = refs[0:6], refs[6:10], refs[10], refs[11:13]
-    kept, arrived, *back = refs[13:17]
-    acc, send_core, got_core, send_low, sent, got = refs[17:]
+    kept, arrived, *back = refs[-10:-6]
+    acc, send_core, got_core, send_low, sent, got = refs[-6:]
     n, b = pl.program_id(0), pl.program_id(1)
     rows = acc.shape[0]
     depth = owns[0].shape[1]
@@ -1301,7 +1313,7 @@
             copy.wait()
 
 
-def unproject(grads, heads, away):
+def unproject(grads, heads, away, done):
     _, rows, width = grads[0].shape
     own, got = heads
     model = got.shape[1]
@@ -1313,7 +1325,7 @@
     return pl.pallas_call(
         unproject_kernel,
         grid=(4, 2),
-        in_specs=[line] * 6 + [still(w) for w in own] + [still(got), ANYWHERE, ANYWHERE],
+        in_specs=[line] * 6 + [still(w) for w in own] + [still(got)] + [ANYWHERE] * (2 + len(done)),
         out_specs=[pl.BlockSpec((rows, model), lambda n, b: (0, 0)), ANYWHERE, ANYWHERE, ANYWHERE],
         out_shape=[piece, piece] + [like(value) for value in away],
         scratch_shapes=[
@@ -1326,7 +1338,7 @@
         ],
         compiler_params=pltpu.CompilerParams(collective_id=6, has_side_effects=True, vmem_limit_bytes=56 << 20),
         cost_estimate=pl.CostEstimate(flops=40 * 10**9, bytes_accessed=20 << 20, transcendentals=0),
-    )(*grads, *own, got, *away)
+    )(*grads, *own, got, *away, *done)
 
 
 def grad_kernel(ids, *refs, chunks, kinds, fixed):
@@ -1483,7 +1495,7 @@
     )(text, head)
 
 
-def normed_kernel(normed, head, outward, upward, near, far, far_near, head_got, pieces, others, up_got, sent, got):
+def normed_kernel(normed, head, outward, upward, _, near, far, far_near, head_got, pieces, others, up_got, sent, got):
     over_x, over_y, over_core, over_low, over_high = partners()
     greet((over_x, over_y, over_core, over_low, over_high))
     send = Sender(sent, got)
@@ -1515,29 +1527,134 @@
         copy.wait()
 
 
-def normed_exchange(normed, head, outward, upward):
+def normed_exchange(normed, head, outward, upward, done):
     pieces = jax.ShapeDtypeStruct((3,) + outward.shape, LOW)
     return pl.pallas_call(
         normed_kernel,
-        in_specs=[ANYWHERE] * 4,
+        in_specs=[ANYWHERE] * 5,
         out_specs=[ANYWHERE] * 7,
         out_shape=[like(normed)] * 3 + [like(head), pieces, pieces, like(upward)],
         scratch_shapes=[pltpu.SemaphoreType.DMA((19,)), pltpu.SemaphoreType.DMA((19,))],
         compiler_params=pltpu.CompilerParams(collective_id=1, has_side_effects=True),
         cost_estimate=pl.CostEstimate(flops=0, bytes_accessed=100 << 20, transcendentals=0),
-    )(normed, head, outward, upward)
+    )(normed, head, outward, upward, done)
+
+
+def adapt(kept, got, master, moment, square):
+    gradient = kept if got is None else kept + got
+    moment_new = BETA_ONE * moment + (1.0 - BETA_ONE) * gradient
+    square_new = BETA_TWO * square + (1.0 - BETA_TWO) * gradient * gradient
+    return moment_new, square_new, direction_of(master, moment_new, square_new)
+
+
+def direction_of(master, moment_new, square_new):
+    root = jnp.sqrt(square_new / (1.0 - BETA_TWO**STEP)) + EPS_ADAM
+    return moment_new / (1.0 - BETA_ONE**STEP) / root + DECAY_RATE * master
+
+
+def close_kernel(*refs, groups, first_steps):
+    kept, got, merged, middle, gain = refs[:5]
+    count = 5 + sum(groups) + 3 * len(groups)
+    weights, outs = refs[5:count], refs[count:]
+    moments, (rows, gains, norms, arrived) = outs[: 2 * len(groups)], outs[2 * len(groups) : 2 * len(groups) + 4]
+    sending, sent, got_sem = outs[2 * len(groups) + 4 :]
+    step = pl.program_id(0)
+    over_high = partners()[4]
+    side = lax.axis_index("mp") // 4
+    crossing = remote(sending, arrived, sent, got_sem, over_high)
+
+    @pl.when(step == 0)
+    def _():
+        greet((over_high,))
+        gains[...] = jnp.zeros_like(gains)
+        norms[...] = jnp.zeros_like(norms)
+
+    @pl.when(step < first_steps)
+    def _():
+        grad = kept[...].astype(WIDE) + got[...].astype(WIDE)
+        standard, scale = centred(merged[...].astype(WIDE))
+        gains[0:1, :] += jnp.sum(grad * standard, axis=0, keepdims=True)
+        total = middle[...] + norm_back(standard, scale, gain[...], grad)
+        rows[...] = total
+        half = first_steps // 2
+        here = pl.ds(pl.multiple_of((step % half) * total.shape[0], total.shape[0]), total.shape[0])
+
+        @pl.when(step // half != side)
+        def _():
+            sending[here, :] = total.astype(LOW)
+
+    @pl.when(step == first_steps - 1)
+    def _():
+        crossing.start()
+
+    at = 0
+    for n, size in enumerate(groups):
+        grads, (master, moment, square) = weights[at : at + size], weights[at + size : at + size + 3]
+        at += size + 3
+        wide = [g[...].astype(WIDE) for g in grads] + [None]
+        moment_new, square_new, direction = adapt(wide[0], wide[1], master[...], moment[...], square[...])
+        moments[2 * n][...] = moment_new
+        moments[2 * n + 1][...] = square_new
+        for k, value in enumerate((master[...], direction)):
+            norms[k, n : n + 1, :] += jnp.sum(fold(value * value), axis=0, keepdims=True)
+
+    @pl.when(step == pl.num_programs(0) - 1)
+    def _():
+        crossing.wait()
+
+
+def close(kept, got, merged, middle, gain, weights):
+    rows, model = kept.shape
+    steps, first_steps = 16, 4
+    line = pl.BlockSpec((rows // first_steps, model), lambda i: (jnp.minimum(i, first_steps - 1), 0))
+    in_specs, out_specs, out_shape, operands = [line] * 4 + [pl.BlockSpec((1, model), lambda i: (0, 0))], [], [], []
+    for group in weights:
+        shape = group[-1].shape
+        block = shape[:-2] + (shape[-2] // steps, shape[-1])
+        spec = pl.BlockSpec(block, lambda i, lead=len(shape) - 2: (0,) * lead + (i, 0))
+        in_specs += [spec] * len(group)
+        out_specs += [spec] * 2
+        out_shape += [jax.ShapeDtypeStruct(shape, WIDE)] * 2
+        operands += group
+    out_specs += [
+        line,
+        pl.BlockSpec((8, model), lambda i: (0, 0)),
+        pl.BlockSpec((2, 8, LANES), lambda i: (0, 0, 0)),
+        ANYWHERE,
+    ]
+    out_shape += [
+        jax.ShapeDtypeStruct((rows, model), WIDE),
+        jax.ShapeDtypeStruct((8, model), WIDE),
+        jax.ShapeDtypeStruct((2, 8, LANES), WIDE),
+        jax.ShapeDtypeStruct((rows // 2, model), LOW),
+    ]
+    return pl.pallas_call(
+        partial(close_kernel, groups=[len(group) - 3 for group in weights], first_steps=first_steps),
+        grid=(steps,),
+        in_specs=in_specs,
+        out_specs=out_specs,
+        out_shape=out_shape,
+        scratch_shapes=[
+            pltpu.VMEM((rows // 2, model), LOW),
+            pltpu.SemaphoreType.DMA,
+            pltpu.SemaphoreType.DMA,
+        ],
+        compiler_params=pltpu.CompilerParams(collective_id=7, has_side_effects=True, vmem_limit_bytes=56 << 20),
+        cost_estimate=pl.CostEstimate(flops=10**9, bytes_accessed=100 << 20, transcendentals=0),
+    )(kept, got, merged, middle, gain, *operands)
 
 
 def rotary_tables(length):
-    cosine, sine_part, exponent = xpos_tables(length, HEAD_DIM)
-    out = []
-    for polarity in (1.0, -1.0):
-        factor = jnp.exp(polarity * exponent)
-        near = (cosine * factor)[:, 0]
-        far = (sine_part * factor)[:, 0]
-        out.append(jnp.concatenate([near] * 4, axis=-1))
-        out.append(jnp.concatenate([-far, far, -far, far], axis=-1))
-    return out
+    lane = jnp.arange(LANES, dtype=jnp.int32)
+    pair_index = (lane % (HEAD_DIM // 2)).astype(WIDE)[None]
+    sign = jnp.where(lane % HEAD_DIM < HEAD_DIM // 2, -1.0, 1.0)[None]
+    angular = jnp.exp(-(2.0 * pair_index / HEAD_DIM) * jnp.log(10000.0))
+    zeta_base = (2.0 * pair_index + 0.4 * HEAD_DIM) / (1.4 * HEAD_DIM)
+    position = jnp.arange(length, dtype=WIDE)[:, None]
+    cosine, sine_part = jnp.cos(position * angular), jnp.sin(position * angular) * sign
+    exponent = position / 512.0 * jnp.log(zeta_base)
+    up, down = jnp.exp(exponent), jnp.exp(-exponent)
+    return [cosine * up, sine_part * up, cosine * down, sine_part * down]
 
 
 def on_device_paired(
@@ -1636,28 +1753,30 @@
         lax.dynamic_slice_in_dim(outward_low, n * half_width, half_width, 1) for n in (core, 1 - core)
     )
     near, far, far_near, head_got, *pieces, upward_got = normed_exchange(
-        normed_own, head_own, outward_own, upward_own
+        normed_own, head_own, outward_own, upward_own, upward_weight[0]
     )
     outward_weight = [outward_own, pieces[0], outward_other, pieces[1]]
     normed = [normed_own, near, far, far_near]
     head_weight.append(lax.all_gather(head_got, "dp", axis=1, tiled=True))
     upward_weight.append(lax.all_gather(upward_got, "dp", axis=0, tiled=True))
-    cotangent = both(pick(output_grad, side), flip(pick(output_grad, 1 - side), "mp", 4)).reshape(rows, model_width)
-    cotangent_far = flip(cotangent, "mp", 2)
-    cotangent_others = [flip(cotangent, "mp", 1), cotangent_far, flip(cotangent_far, "mp", 1)]
+    got_cotangent = flip(pick(output_grad, 1 - side), "mp", 4)
 
     queries, keys, values, contexts, logs, arrived = [], [], [], [], [], []
     for half in range(2):
-        projected = [project(ids, chunk, head_weight[half], tables, j) for j, chunk in enumerate(normed)]
+        projected = []
+        for j, chunk in enumerate(normed):
+            carry = [downward_own, got_cotangent] if half == 1 and j == 0 else []
+            done = [projected[0][0]] if j > 0 else []
+            outs = project(ids, chunk, head_weight[half], tables, j, done, carry)
+            projected.append(outs[:3])
+            if carry:
+                downward_got = flip(outs[3], "mp", 4)
+                cotangent = both(pick(output_grad, side), outs[4]).reshape(rows, model_width)
+                cotangent_far = flip(cotangent, "mp", 2)
+                cotangent_others = [flip(cotangent, "mp", 1), cotangent_far, flip(cotangent_far, "mp", 1)]
         for n, group in enumerate((queries, keys, values)):
             group.append([p[n] for p in projected])
-        if half == 0:
-            context, lse, leaving = attend(
-                ids, queries[half], keys[half], values[half], [], [downward_own]
-            )
-            downward_got = flip(leaving, "mp", 4)
-        else:
-            context, lse = attend(ids, queries[half], keys[half], values[half])
+        context, lse = attend(ids, queries[half], keys[half], values[half])
         contexts.append(context)
         logs.append(lse)
         arrived = arrived + turn_heads(context)
@@ -1691,9 +1810,8 @@
         ids, (lifted_kept, lifted_got), middle, cotangent, context, outward_weight, gain_mid, gain_ctx
     )
     context_heads = [turn_heads(own_grads), turn_heads(other_grads)]
-    up_grad = lax.psum_scatter(
-        weight_grad(ids, lifted, [split(hidden_grad)], True), "dp", scatter_dimension=1, tiled=True
-    )[0]
+    up_part = weight_grad(ids, lifted, [split(hidden_grad)], True)
+    up_grad = lax.psum_scatter(up_part, "dp", scatter_dimension=1, tiled=True)[0]
     ffn_parts = [ffn_out(ids, squashed, j, downward_weight) for j in range(4)]
 
     def scatter_tokens(parts):
@@ -1731,46 +1849,48 @@
             outward_half = add_low(
                 lax.dynamic_slice_in_dim(outward_part, core * half_width, half_width, 1), flip(outward_sent, "mp", 1)
             )
+            outward_grad = lax.psum_scatter(outward_half, "dp", scatter_dimension=0, tiled=True)
     output_got, down_got = backs
     layer_output = both(pick(output_rows, side), output_got)
     normed_kept, normed_got, up_got, head_got_grad = unproject(
-        head_grads[0] + head_grads[1], head_weight, [up_grad[:, hidden_local:], head_sides[1]]
-    )
-    head_sum = head_sides[0].astype(WIDE) + head_got_grad.astype(WIDE)
-    normed_grad = normed_kept.astype(WIDE) + normed_got.astype(WIDE)
-    _, input_back = jax.vjp(layer_norm, merged.astype(WIDE), gain_in)
-    merged_part, in_gain_grad = input_back(normed_grad)
-    input_grad = give_back((middle_grad + merged_part).reshape(2, local_len, model_width))
-
-    outward_grad = lax.psum_scatter(outward_half, "dp", scatter_dimension=0, tiled=True)
+        head_grads[0] + head_grads[1], head_weight, [up_grad[:, hidden_local:], head_sides[1]], [head_part, outward_grad]
+    )
+    result = close(
+        normed_kept,
+        normed_got,
+        merged,
+        middle_grad,
+        gain_in,
+        [
+            [up_grad[:, :hidden_local], up_got, upward_master, upward_moment, upward_square],
+            [down_grad[:hidden_local], down_got, downward_master, downward_moment, downward_square],
+        ],
+    )
+    moment_upward, square_upward, moment_downward, square_downward = result[:4]
+    input_rows, in_gain_grad, norm_lanes, input_got = result[4:]
+    moment_head, square_head, head_dir = adapt_step(
+        head_sides[0].astype(WIDE) + head_got_grad.astype(WIDE), head_master, head_moment, head_square, DECAY_RATE
+    )
     outward_grad = lax.psum(outward_grad, "mp", axis_index_groups=[[0, 2, 4, 6], [1, 3, 5, 7]])
+    outward_grad = hand_on(outward_grad, [input_got])
     outward_got = flip(outward_grad, "mp", 1)
     outward_grad = jnp.where(
         core == 0,
         jnp.concatenate([outward_grad, outward_got], axis=1),
         jnp.concatenate([outward_got, outward_grad], axis=1),
     )
-    outward_sum = outward_grad.astype(WIDE)
-
-    down_sum = down_grad[:hidden_local].astype(WIDE) + down_got.astype(WIDE)
-    up_sum = up_grad[:, :hidden_local].astype(WIDE) + up_got.astype(WIDE)
-    moment_head, square_head, head_dir = adapt_step(head_sum, head_master, head_moment, head_square, DECAY_RATE)
     moment_outward, square_outward, outward_dir = adapt_step(
-        outward_sum, outward_master, outward_moment, outward_square, DECAY_RATE
-    )
-    moment_upward, square_upward, upward_dir = adapt_step(
-        up_sum, upward_master, upward_moment, upward_square, DECAY_RATE
-    )
-    moment_downward, square_downward, downward_dir = adapt_step(
-        down_sum, downward_master, downward_moment, downward_square, DECAY_RATE
-    )
+        outward_grad.astype(WIDE), outward_master, outward_moment, outward_square, DECAY_RATE
+    )
+    upward_dir = direction_of(upward_master, moment_upward, square_upward)
+    downward_dir = direction_of(downward_master, moment_downward, square_downward)
+    input_grad = both(pick(input_rows.reshape(2, local_len, model_width), side), input_got.astype(WIDE))
     owner = (model_rank == 0).astype(WIDE)
     norm_part = jnp.concatenate(
         [
             jnp.stack([jnp.sum(head_master * head_master, axis=(1, 2)), jnp.sum(head_dir * head_dir, axis=(1, 2))], axis=-1),
             pair_sums(outward_master, outward_dir) * owner,
-            pair_sums(upward_master, upward_dir),
-            pair_sums(downward_master, downward_dir),
+            jnp.sum(norm_lanes, axis=-1)[:, :2].T,
         ],
         axis=0,
     )

time: 1190 us -> 1180 us (level)
  Pallas kernels: 795 us -> 880 us
  waiting for transfers between devices: 186 us -> 126 us
  other arithmetic: 122 us -> 87.5 us
    pallas_call x1 -> x3, Pallas kernels: 94 us -> 181 us  [the longest x1 94.2 us: normed_exchange(): pl.pallas_call(normed_kernel, in_specs=[ANYWHERE] * 5, out_specs=[ANYWHER...]
    ppermute x31 -> x30, waiting for transfers between devices: 127 us -> 78.7 us  [flip(): lax.ppermute(value, axis, [(i, i ^ mask) for i in range(lax.axis_size(axi...]
    reduce_scatter x2, waiting for transfers between devices: 0.03 us -> 44.2 us  [on_device_paired(): lax.psum_scatter(head_part, 'dp', scatter_dimension=1, tiled=True)]
    psum x1, waiting for transfers between devices: 39.2 us -> 1.48 us  [on_device_paired(): lax.psum(outward_grad, 'mp', axis_index_groups=[[0, 2, 4, 6], [1, 3, 5, 7]])]
    all_gather x1, waiting for transfers between devices: 18.1 us -> 0.01 us  [on_device_paired(): downward_weight = [lax.all_gather(downward_own, 'dp', axis=1, tiled=True)]]
  transfers between devices with their start and end apart: 42 -> 41, of which waited for: 19 -> 18; matrix products, arithmetic and copies ran while one was open for 7% -> 6% of each run, Pallas kernels for 43% -> 55%
where the time goes in v4:
time: 1180 us
  Pallas kernels  880 us (75%)
  waiting for transfers between devices  126 us (11%)
  other arithmetic  87.5 us (7%)
  local copies, waits for them, and re-layouts  40.5 us (3%)
  starting transfers between devices  21.7 us (2%)
  between operations  19.3 us (2%)
    pallas_call x21, Pallas kernels, kernel_call(): pl.pallas_call(whole, grid_spec=pltpu.PrefetchScalarGridSpec(num_scalar_p...  260 us
    pallas_call x2, Pallas kernels, attend_back(): pl.pallas_call(partial(attend_back_kernel, bq=block, bk=block), grid=(pai...  108 us
    pallas_call x1, Pallas kernels, unproject(): pl.pallas_call(unproject_kernel, grid=(4, 2), in_specs=[line] * 6 + [stil...  98.1 us
    pallas_call x1, Pallas kernels, normed_exchange(): pl.pallas_call(normed_kernel, in_specs=[ANYWHERE] * 5, out_specs=[ANYWHER...  94.2 us
    pallas_call x1, Pallas kernels, close(): pl.pallas_call(partial(close_kernel, groups=[len(group) - 3 for group in...  86.8 us
    ppermute x30, waiting for transfers between devices, flip(): lax.ppermute(value, axis, [(i, i ^ mask) for i in range(lax.axis_size(axi...  78.7 us
    pallas_call x1, Pallas kernels, ffn_second(): pl.pallas_call(partial(ffn_second_kernel, hidden_width=hidden_width), gri...  71.7 us
    pallas_call x1, Pallas kernels, ffn_up(): pl.pallas_call(ffn_up_kernel, grid=(4, 2 * count), in_specs=[ANYWHERE] +...  70.8 us
  transfers between devices with their start and end apart: 41, of which 18 were waited for; matrix products, arithmetic and copies ran while one was open for 6% of the time, Pallas kernels for 55%

profile of v4, /device:TPU:0, one launch (start us, length us, event | category | flops | bytes accessed | tf_op | source)
XLA Modules:
  0.0 1177.3 jit_solution(6290400080689923913)
XLA Ops:
  23.3 51.2 %shard_map.363 = (bf16[256,2048]{1,0:T(8,128)(2,1)}, bf16[3,512,256]{2,1,0:T(8,128)(2,1)}, bf16[3,512,256]{2,1,0:T(8,128)(2,1)}, bf16[3,512,256]{2,1,0:T(8,128)(2,1)}) custom-call(bf16[256,2048]{1,0:T(8,128)(2,1)} %get-tuple-element.292.text, bf16[3,512,256]{2,1,0:T(8,128)(2,1)} %convert_element_type.175.head.refs_2_.refs_6_), custom_call_target="tpu_custom_call" | custom-call | bytes 104857600 | tf_op jit(solution)/shard_map/pallas_call | solution.py:1487
  84.4 94.2 %shard_map.365 = (bf16[512,2048]{1,0:T(8,128)(2,1)}, bf16[512,2048]{1,0:T(8,128)(2,1)}, bf16[512,2048]{1,0:T(8,128)(2,1)}, bf16[3,512,256]{2,1,0:T(8,128)(2,1)},...) custom-call(bf16[512,2048]{1,0:T(8,128)(2,1)} %fusion.5.refs_1_.normed, ...), custom_call_target="tpu_custom_call" | custom-call | bytes 104857600 | tf_op jit(solution)/shard_map/pallas_call | solution.py:1532
  213.1 15.9 %collective-permute-done.3.refs_11_ = bf16[256,2048]{1,0:T(8,128)(2,1)S(1)} collective-permute-done((bf16[256,2048]{1,0:T(8,128)(2,1)}, bf16[256,2048]{1,0:T(8,128)(2,1)S(1)}, u32[]{:S(2)}, u32[]{:S(2)}) %collective-permute-start.3) | collective-permute-done | bytes 1048608 | tf_op jit(solution)/shard_map/ppermute | solution.py:1419
  238.7 23.1 %shard_map.369 = (bf16[512,256]{1,0:T(8,128)(2,1)}, bf16[512,256]{1,0:T(8,128)(2,1)}, bf16[512,256]{1,0:T(8,128)(2,1)}, bf16[512,256]{1,0:T(8,128)(2,1)}, f32[2,2,2048]{2,1,0:T(2,128)}) custom-call(s32[3]{0:T(128)} %pad_add_fusion.refs_0_, bf16[512,256]{1,0:T(8,128)(2,1)} %get-tuple-element.120.refs_10_.refs_1_.refs_0_, ...), custom_call_target="tpu_custom_call" | custom-call | flops 12000000000 | bytes 3000000 | tf_op jit(solution)/shard_map/pallas_call | solution.py:475
  285.3 22.8 %shard_map.374 = (bf16[512,256]{1,0:T(8,128)(2,1)}, bf16[512,256]{1,0:T(8,128)(2,1)}, bf16[512,256]{1,0:T(8,128)(2,1)}, bf16[512,256]{1,0:T(8,128)(2,1)}, f32[2,2,2048]{2,1,0:T(2,128)}) custom-call(s32[3]{0:T(128)} %pad_add_fusion.refs_0_, bf16[512,256]{1,0:T(8,128)(2,1)} %get-tuple-element.140.refs_10_.refs_1_.refs_0_, ...), custom_call_target="tpu_custom_call" | custom-call | flops 12000000000 | bytes 3000000 | tf_op jit(solution)/shard_map/pallas_call | solution.py:475
  330.4 13.9 %shard_map.375 = (bf16[512,2048]{1,0:T(8,128)(2,1)}, bf16[512,2048]{1,0:T(8,128)(2,1)}, f32[512,2048]{1,0:T(8,128)}, bf16[512,2048]{1,0:T(8,128)(2,1)}, bf16[1024,512]{1,0:T(8,128)(2,1)}) custom-call(s32[3]{0:T(128)} %pad_add_fusion.refs_0_, bf16[512,256]{1,0:T(8,128)(2,1)} %get-tuple-element.135.refs_1_.refs_16_, ...), custom_call_target="tpu_custom_call", output_to_operand_aliasing={{4}: (16, {})} | custom-call | flops 1288490240 | bytes 6920601 | tf_op jit(solution)/shard_map/pallas_call | solution.py:475
  345.2 70.8 %shard_map.376 = (bf16[4,512,2048]{2,1,0:T(8,128)(2,1)}, bf16[4,512,2048]{2,1,0:T(8,128)(2,1)}, f32[4,8,512]{2,1,0:T(8,128)}, bf16[3,512,2048]{2,1,0:T(8,128)(2,1)}) custom-call(bf16[512,2048]{1,0:T(8,128)(2,1)} %get-tuple-element.160.lifted.refs_1_, bf16[2048,1024]{1,0:T(8,128)(2,1)} %all-gather.6.cloned.1.call-done._.up_own, ...), custom_call_target="tpu_custom_call" | custom-call | flops 80000000000 | bytes 104857600 | tf_op jit(solution)/shard_map/pallas_call | solution.py:1023
  416.1 38.9 %shard_map.377 = (bf16[4,512,2048]{2,1,0:T(8,128)(2,1)}, f32[4,8,512]{2,1,0:T(8,128)}) custom-call(bf16[512,2048]{1,0:T(8,128)(2,1)} %bitcast.74, bf16[512,2048]{1,0:T(8,128)(2,1)} %collective-permute-done.8.near.refs_6_, bf16[512,2048]{1,0:T(8,128)(2,1)} %collective-permute-done.9.far.refs_7_, bf16[512,2048]{1,0:T(8,128)(2,1)} %collective-permute-done.10.last.refs_8_, ...), custom_call_target="tpu_custom_call" | custom-call | flops 60000002048 | bytes 104857600 | tf_op jit(solution)/shard_map/pallas_call | solution.py:1085
  462.1 71.7 %shard_map.378 = (bf16[4,512,2048]{2,1,0:T(8,128)(2,1)}, bf16[4,512,2048]{2,1,0:T(8,128)(2,1)}, bf16[512,2048]{1,0:T(8,128)(2,1)}, bf16[512,2048]{1,0:T(8,128)(2,1)}, f32[8,2048]{1,0:T(8,128)}) custom-call(bf16[4,512,2048]{2,1,0:T(8,128)(2,1)} %get-tuple-element.162.act, bf16[4,512,2048]{2,1,0:T(8,128)(2,1)} %get-tuple-element.163.slope, ...), custom_call_target="tpu_custom_call" | custom-call | flops 80000000000 | bytes 104857600 | tf_op jit(solution)/shard_map/pallas_call | solution.py:1195
  533.8 27.5 %shard_map.385 = bf16[1,2048,2048]{2,1,0:T(8,128)(2,1)} custom-call(s32[3]{0:T(128)} %pad_add_fusion.refs_0_, bf16[4,512,2048]{2,1,0:T(8,128)(2,1)} %get-tuple-element.169.refs_1_.refs_2_.refs_3_.refs_4_, bf16[4,512,2048]{2,1,0:T(8,128)(2,1)} %get-tuple-element.169.refs_1_.refs_2_.refs_3_.refs_4_, ...), custom_call_target="tpu_custom_call" | custom-call | flops 5153960960 | bytes 12582912 | tf_op jit(solution)/shard_map/pallas_call | solution.py:475
  561.4 24.7 %shard_map.387 = bf16[1,2048,2048]{2,1,0:T(8,128)(2,1)} custom-call(s32[3]{0:T(128)} %pad_add_fusion.refs_0_, bf16[512,2048]{1,0:T(8,128)(2,1)} %get-tuple-element.160.lifted.refs_1_, bf16[3,512,2048]{2,1,0:T(8,128)(2,1)} %get-tuple-element.190.refs_2_.refs_3_.refs_4_, bf16[3,512,2048]{2,1,0:T(8,128)(2,1)} %get-tuple-element.190.refs_2_.refs_3_.refs_4_, ...), custom_call_target="tpu_custom_call" | custom-call | flops 5153960960 | bytes 12582912 | tf_op jit(solution)/shard_map/pallas_call | solution.py:475
  586.1 11.0 shard_map.382
  597.1 10.7 shard_map.380
  608.6 10.6 shard_map.381
  623.1 20.7 %shard_map.383 = (f32[512,2048]{1,0:T(8,128)}, bf16[512,2048]{1,0:T(8,128)(2,1)}, bf16[512,256]{1,0:T(8,128)(2,1)}, bf16[512,256]{1,0:T(8,128)(2,1)}, bf16[512,2...) custom-call(s32[3]{0:T(128)} %pad_add_fusion.refs_0_, ...), custom_call_target="tpu_custom_call" | custom-call | flops 1288490240 | bytes 8178892 | tf_op jit(solution)/shard_map/pallas_call | solution.py:475
  646.0 11.1 shard_map.379
  658.5 13.4 %collective-permute-done.16 = bf16[512,2048]{1,0:T(8,128)(2,1)} collective-permute-done((bf16[512,2048]{1,0:T(8,128)(2,1)}, bf16[512,2048]{1,0:T(8,128)(2,1)}, u32[]{:S(2)}, u32[]{:S(2)}) %collective-permute-start.16) | collective-permute-done | bytes 2097184 | tf_op jit(solution)/shard_map/ppermute | solution.py:1419
  682.1 54.2 %shard_map.386 = (bf16[4,512,256]{2,1,0:T(8,128)(2,1)}, bf16[4,512,256]{2,1,0:T(8,128)(2,1)}, bf16[4,512,256]{2,1,0:T(8,128)(2,1)}, bf16[1024,512]{1,0:T(8,128)(2,1)}) custom-call(bf16[512,256]{1,0:T(8,128)(2,1)} %get-tuple-element.140.refs_10_.refs_1_.refs_0_, bf16[512,256]{1,0:T(8,128)(2,1)} %get-tuple-element.141.refs_2_.refs_1_, ...), custom_call_target="tpu_custom_call" | custom-call | flops 40000000000 | bytes 20971520 | tf_op jit(solution)/shard_map/pallas_call | solution.py:734
  736.3 11.8 %shard_map.388.refs_3_ = bf16[3,2048,256]{2,1,0:T(8,128)(2,1)} custom-call(s32[3]{0:T(128)} %pad_add_fusion.refs_0_, bf16[512,2048]{1,0:T(8,128)(2,1)} %fusion.5.refs_1_.normed, bf16[512,2048]{1,0:T(8,128)(2,1)} %get-tuple-element.121.refs_1_.refs_2_, bf16[512,2048]{1,0:T(8,128)(2,1)} %get-tuple-element.123.refs_1_.refs_3_, ...), custom_call_target="tpu_custom_call" | custom-call | flops 1932735232 | bytes 6291456 | tf_op jit(solution)/shard_map/pallas_call | solution.py:475
  786.9 53.6 %shard_map.384 = (bf16[4,512,256]{2,1,0:T(8,128)(2,1)}, bf16[4,512,256]{2,1,0:T(8,128)(2,1)}, bf16[4,512,256]{2,1,0:T(8,128)(2,1)}, bf16[256,2048]{1,0:T(8,128)(2,1)}) custom-call(bf16[512,256]{1,0:T(8,128)(2,1)} %get-tuple-element.120.refs_10_.refs_1_.refs_0_, bf16[512,256]{1,0:T(8,128)(2,1)} %get-tuple-element.122.refs_2_.refs_1_, ...), custom_call_target="tpu_custom_call" | custom-call | flops 40000000000 | bytes 20971520 | tf_op jit(solution)/shard_map/pallas_call | solution.py:734
  840.5 11.9 %shard_map.389.refs_13_ = bf16[3,2048,256]{2,1,0:T(8,128)(2,1)} custom-call(s32[3]{0:T(128)} %pad_add_fusion.refs_0_, bf16[512,2048]{1,0:T(8,128)(2,1)} %fusion.5.refs_1_.normed, bf16[512,2048]{1,0:T(8,128)(2,1)} %get-tuple-element.121.refs_1_.refs_2_, bf16[512,2048]{1,0:T(8,128)(2,1)} %get-tuple-element.123.refs_1_.refs_3_, ...), custom_call_target="tpu_custom_call" | custom-call | flops 1932735232 | bytes 6291456 | tf_op jit(solution)/shard_map/pallas_call | solution.py:475
  855.4 98.1 %shard_map.391 = (bf16[512,2048]{1,0:T(8,128)(2,1)}, bf16[512,2048]{1,0:T(8,128)(2,1)}, bf16[512,1024]{1,0:T(8,128)(2,1)}, bf16[3,512,256]{2,1,0:T(8,128)(2,1)}) custom-call(bf16[4,512,256]{2,1,0:T(8,128)(2,1)} %get-tuple-element.179.refs_5_.refs_6_.refs_7_.refs_8_.refs_0_, ...), custom_call_target="tpu_custom_call" | custom-call | flops 40000000000 | bytes 20971520 | tf_op jit(solution)/shard_map/pallas_call | solution.py:1325
  955.9 86.8 %shard_map.392 = (f32[512,1024]{1,0:T(8,128)}, f32[512,1024]{1,0:T(8,128)}, f32[1024,512]{1,0:T(8,128)}, f32[1024,512]{1,0:T(8,128)}, f32[512,2048]{1,0:T(8,128)...) custom-call(bf16[512,2048]{1,0:T(8,128)(2,1)} %get-tuple-element.194.refs_0_, ...), custom_call_target="tpu_custom_call" | custom-call | flops 1000000000 | bytes 104857600 | tf_op jit(solution)/shard_map/pallas_call | solution.py:1631
  1046.5 44.2 %reduce-scatter.14.cloned.1.call-done = bf16[3,512,256]{2,1,0:T(8,128)(2,1)} async-done(((bf16[3,2048,256]{2,1,0:T(8,128)(2,1)}), bf16[3,512,256]{2,1,0:T(8,128)(2,1)}) %reduce-scatter.14.cloned.1.call-update) | async-done | bytes 786448 | tf_op jit(solution)/shard_map/reduce_scatter | solution.py:1845
  (298 shorter events, 265.1 us)
Async XLA Ops:
  7.2 77.2 %all-gather.6.cloned.1.call-start = ((), (), s32[]{:S(2)}) async-start(), calls=%async_computation.5 | async-start | bytes 5242880 | tf_op jit(solution)/shard_map/all_gather | solution.py:1706
  10.2 218.9 %all-gather.12.cloned.1.call-start = ((), (), s32[]{:S(2)}) async-start(), calls=%async_computation.8 | async-start | bytes 5242880 | tf_op jit(solution)/shard_map/all_gather | solution.py:1710
  12.9 216.1 %all-gather.8.cloned.1.call-start = ((), (), s32[]{:S(2)}) async-start(), calls=%async_computation.6 | async-start | bytes 3932160 | tf_op jit(solution)/shard_map/all_gather | solution.py:1760
  178.6 166.6 %all-gather.10.cloned.1.call-start = ((), (), s32[]{:S(2)}) async-start(), calls=%async_computation.7 | async-start | bytes 5242880 | tf_op jit(solution)/shard_map/all_gather | solution.py:1761
  179.2 236.9 %all-gather.14.cloned.1.call-start = ((), (), s32[]{:S(2)}) async-start(), calls=%async_computation.9 | async-start | bytes 5242880 | tf_op jit(solution)/shard_map/all_gather | solution.py:1786
  181.0 48.0 %collective-permute-start.3 = (bf16[256,2048]{1,0:T(8,128)(2,1)}, bf16[256,2048]{1,0:T(8,128)(2,1)S(1)}, u32[]{:S(2)}, u32[]{:S(2)}) collective-permute-start(bf16[256,2048]{1,0:T(8,128)(2,1)} %get-tuple-element.288), channel_id=1, source_target_pairs={{0,4},{1,5},{2,6},{3,7},{4,0},{5,1},{6,2},{7,3},{8,12},{9,13},{10,... | collective-permute-start | bytes 3145736 | tf_op jit(solution)/shard_map/ppermute | solution.py:1419
  238.6 105.8 %collective-permute-start.9 = (bf16[512,2048]{1,0:T(8,128)(2,1)S(1)}, bf16[512,2048]{1,0:T(8,128)(2,1)}, u32[]{:S(2)}, u32[]{:S(2)}) collective-permute-start(bf16[512,2048]{1,0:T(8,128)(2,1)S(1)} %bitcast.72), channel_id=1, source_target_pairs={{0,2},{1,3},{2,0},{3,1},{4,6},{5,7},{6,4},{7,5},{8,10},{9,11},{10,... | collective-permute-start | bytes 6291464 | tf_op jit(solution)/shard_map/ppermute | solution.py:1419
  261.8 46.3 %collective-permute-start = (bf16[512,256]{1,0:T(8,128)(2,1)}, bf16[512,256]{1,0:T(8,128)(2,1)S(1)}, u32[]{:S(2)}, u32[]{:S(2)}) collective-permute-start(bf16[512,256]{1,0:T(8,128)(2,1)} %get-tuple-element.136.refs_17_), channel_id=1, source_target_pairs={{0,1},{1,0},{2,3},{3,2},{4,5},{5,4},{6,7},{7,6},{8,9},{9,8},{10,11... | collective-permute-start | bytes 786440 | tf_op jit(solution)/shard_map/ppermute | solution.py:1419
  261.9 53.4 %collective-permute-start.1 = (bf16[512,256]{1,0:T(8,128)(2,1)}, bf16[512,256]{1,0:T(8,128)(2,1)}, u32[]{:S(2)}, u32[]{:S(2)}) collective-permute-start(bf16[512,256]{1,0:T(8,128)(2,1)} %get-tuple-element.137.refs_18_), channel_id=1, source_target_pairs={{0,2},{1,3},{2,0},{3,1},{4,6},{5,7},{6,4},{7,5},{8,10},{9,11},{10,... | collective-permute-start | bytes 786440 | tf_op jit(solution)/shard_map/ppermute | solution.py:1419
  263.8 55.3 %collective-permute-start.2 = (bf16[512,256]{1,0:T(8,128)(2,1)}, bf16[512,256]{1,0:T(8,128)(2,1)}, u32[]{:S(2)}, u32[]{:S(2)}) collective-permute-start(bf16[512,256]{1,0:T(8,128)(2,1)} %get-tuple-element.138.refs_19_), channel_id=1, source_target_pairs={{0,3},{1,2},{2,1},{3,0},{4,7},{5,6},{6,5},{7,4},{8,11},{9,10},{10,... | collective-permute-start | bytes 786440 | tf_op jit(solution)/shard_map/ppermute | solution.py:1419
  263.9 66.5 %collective-permute-start.7 = (bf16[1024,512]{1,0:T(8,128)(2,1)S(1)}, bf16[1024,512]{1,0:T(8,128)(2,1)}, u32[]{:S(2)}, u32[]{:S(2)}) collective-permute-start(bf16[1024,512]{1,0:T(8,128)(2,1)S(1)} %copy-done.14), channel_id=1, source_target_pairs={{0,4},{1,5},{2,6},{3,7},{4,0},{5,1},{6,2},{7,3},{8,12},{9,13},{10,... | collective-permute-start | bytes 3145736 | tf_op jit(solution)/shard_map/ppermute | solution.py:1419
  319.8 96.3 %collective-permute-start.8 = (bf16[512,2048]{1,0:T(8,128)(2,1)S(1)}, bf16[512,2048]{1,0:T(8,128)(2,1)}, u32[]{:S(2)}, u32[]{:S(2)}) collective-permute-start(bf16[512,2048]{1,0:T(8,128)(2,1)S(1)} %bitcast.73), channel_id=1, source_target_pairs={{0,1},{1,0},{2,3},{3,2},{4,5},{5,4},{6,7},{7,6},{8,9},{9,8},{10,11... | collective-permute-start | bytes 6291464 | tf_op jit(solution)/shard_map/ppermute | solution.py:1419
  344.3 333.9 %reduce-scatter.6.cloned.1.call-start = ((), (), s32[]{:S(2)}) async-start(), calls=%async_computation.10 | async-start | bytes 10485760 | tf_op jit(solution)/shard_map/reduce_scatter | solution.py:1806
  344.4 71.7 %collective-permute-start.10 = (bf16[512,2048]{1,0:T(8,128)(2,1)}, bf16[512,2048]{1,0:T(8,128)(2,1)}, u32[]{:S(2)}, u32[]{:S(2)}) collective-permute-start(bf16[512,2048]{1,0:T(8,128)(2,1)} %collective-permute-done.9.far.refs_7_), channel_id=1, source_target_pairs={{0,1},{1,0},{2,3},{3,2},{4,5},{5,4},{6,7},{7,6},{8,9},{9,8},{10,11... | collective-permute-start | bytes 6291464 | tf_op jit(solution)/shard_map/ppermute | solution.py:1419
  561.3 291.1 %reduce-scatter.8.cloned.1.call-start = ((), (), s32[]{:S(2)}) async-start(), calls=%async_computation.11 | async-start | bytes 10485760 | tf_op jit(solution)/shard_map/reduce_scatter | solution.py:1814
  586.1 269.4 %reduce-scatter.10.cloned.1.call-start = ((), (), s32[]{:S(2)}) async-start(), calls=%async_computation.12 | async-start | bytes 3932160 | tf_op jit(solution)/shard_map/reduce_scatter | solution.py:1845
  607.8 49.4 %collective-permute-start.14 = (bf16[512,2048]{1,0:T(8,128)(2,1)}, bf16[512,2048]{1,0:T(8,128)(2,1)S(1)}, u32[]{:S(2)}, u32[]{:S(2)}) collective-permute-start(bf16[512,2048]{1,0:T(8,128)(2,1)} %shard_map.380), channel_id=1, source_target_pairs={{0,1},{1,0},{2,3},{3,2},{4,5},{5,4},{6,7},{7,6},{8,9},{9,8},{10,11... | collective-permute-start | bytes 6291464 | tf_op jit(solution)/shard_map/ppermute | solution.py:1419
  623.0 48.8 %collective-permute-start.16 = (bf16[512,2048]{1,0:T(8,128)(2,1)}, bf16[512,2048]{1,0:T(8,128)(2,1)}, u32[]{:S(2)}, u32[]{:S(2)}) collective-permute-start(bf16[512,2048]{1,0:T(8,128)(2,1)} %add_convert_fusion.1), channel_id=1, source_target_pairs={{0,2},{1,3},{2,0},{3,1},{4,6},{5,7},{6,4},{7,5},{8,10},{9,11},{10,... | collective-permute-start | bytes 6291464 | tf_op jit(solution)/shard_map/ppermute | solution.py:1419
  643.8 37.4 %collective-permute-start.20 = (bf16[512,256]{1,0:T(8,128)(2,1)}, bf16[512,256]{1,0:T(8,128)(2,1)S(1)}, u32[]{:S(2)}, u32[]{:S(2)}) collective-permute-start(bf16[512,256]{1,0:T(8,128)(2,1)} %get-tuple-element.183), channel_id=1, source_target_pairs={{0,1},{1,0},{2,3},{3,2},{4,5},{5,4},{6,7},{7,6},{8,9},{9,8},{10,11... | collective-permute-start | bytes 786440 | tf_op jit(solution)/shard_map/ppermute | solution.py:1419
  643.9 37.3 %collective-permute-start.21 = (bf16[512,256]{1,0:T(8,128)(2,1)}, bf16[512,256]{1,0:T(8,128)(2,1)S(1)}, u32[]{:S(2)}, u32[]{:S(2)}) collective-permute-start(bf16[512,256]{1,0:T(8,128)(2,1)} %get-tuple-element.184), channel_id=1, source_target_pairs={{0,2},{1,3},{2,0},{3,1},{4,6},{5,7},{6,4},{7,5},{8,10},{9,11},{10,... | collective-permute-start | bytes 786440 | tf_op jit(solution)/shard_map/ppermute | solution.py:1419
  748.1 107.3 %reduce-scatter.12.cloned.1.call-start = ((), (), s32[]{:S(2)}) async-start(), calls=%async_computation.13 | async-start | bytes 5242880 | tf_op jit(solution)/shard_map/reduce_scatter | solution.py:1852
  953.6 90.6 %all-reduce.2.cloned.1.call-start = ((), (), s32[]{:S(2)}) async-start(), calls=%async_computation.15 | async-start | bytes 2097152 | tf_op jit(solution)/shard_map/psum | solution.py:1874
  954.2 136.6 %reduce-scatter.14.cloned.1.call-start = ((), (), s32[]{:S(2)}) async-start(), calls=%async_computation.14 | async-start | bytes 3932160 | tf_op jit(solution)/shard_map/reduce_scatter | solution.py:1845
  1044.2 52.2 %collective-permute-start.24 = (bf16[512,1024]{1,0:T(8,128)(2,1)}, bf16[512,1024]{1,0:T(8,128)(2,1)}, u32[]{:S(2)}, u32[]{:S(2)}) collective-permute-start(bf16[512,1024]{1,0:T(8,128)(2,1)} %shard_map.393), channel_id=1, source_target_pairs={{0,1},{1,0},{2,3},{3,2},{4,5},{5,4},{6,7},{7,6},{8,9},{9,8},{10,11... | collective-permute-start | bytes 3145736 | tf_op jit(solution)/shard_map/ppermute | solution.py:1419
  (68 other events, 843.2 us)
Sparse Core Ops, SparseCore 0:
  10.5 73.0 all-gather.5
  85.9 69.9 all-gather.11
  178.8 42.9 all-gather.7
  223.4 52.6 all-gather.9
  344.5 52.7 all-gather.13
  561.4 86.1 reduce-scatter.5
  651.0 86.4 reduce-scatter.7
  748.2 43.7 reduce-scatter.9
  795.6 52.6 reduce-scatter.11
  956.6 87.5 all-reduce.1
  1047.7 42.9 reduce-scatter.13

commit v5 on v4

--- a/solution.py
+++ b/solution.py
@@ -1852,6 +1852,7 @@
             outward_grad = lax.psum_scatter(outward_half, "dp", scatter_dimension=0, tiled=True)
     output_got, down_got = backs
     layer_output = both(pick(output_rows, side), output_got)
+    outward_grad = lax.psum(outward_grad, "mp", axis_index_groups=[[0, 2, 4, 6], [1, 3, 5, 7]])
     normed_kept, normed_got, up_got, head_got_grad = unproject(
         head_grads[0] + head_grads[1], head_weight, [up_grad[:, hidden_local:], head_sides[1]], [head_part, outward_grad]
     )
@@ -1871,7 +1872,6 @@
     moment_head, square_head, head_dir = adapt_step(
         head_sides[0].astype(WIDE) + head_got_grad.astype(WIDE), head_master, head_moment, head_square, DECAY_RATE
     )
-    outward_grad = lax.psum(outward_grad, "mp", axis_index_groups=[[0, 2, 4, 6], [1, 3, 5, 7]])
     outward_grad = hand_on(outward_grad, [input_got])
     outward_got = flip(outward_grad, "mp", 1)
     outward_grad = jnp.where(

time: 1180 us -> 1240 us (1.051)
  waiting for transfers between devices: 126 us -> 217 us
  Pallas kernels: 880 us -> 849 us
    psum x1, waiting for transfers between devices: 1.48 us -> 54.2 us  [on_device_paired(): lax.psum(outward_grad, 'mp', axis_index_groups=[[0, 2, 4, 6], [1, 3, 5, 7]])]
    pallas_call x1, Pallas kernels: 86.8 us -> 56.7 us  [close(): pl.pallas_call(partial(close_kernel, groups=[len(group) - 3 for group in...]
    reduce_scatter x1, waiting for transfers between devices: 0.01 us -> 24.2 us  [on_device_paired(): lax.psum_scatter(outward_half, 'dp', scatter_dimension=0, tiled=True)]
    reduce_scatter x1, waiting for transfers between devices: 0.01 us -> 23.1 us  [on_device_paired(): lax.psum_scatter(up_part, 'dp', scatter_dimension=1, tiled=True)[0]]
  transfers between devices with their start and end apart: 41 -> 41, of which waited for: 18 -> 19; matrix products, arithmetic and copies ran while one was open for 6% -> 5% of each run, Pallas kernels for 55% -> 52%
where the time goes in v5:
time: 1240 us; the launch traced here: 1230 us
  Pallas kernels  849 us (68%)
  waiting for transfers between devices  217 us (18%)
  other arithmetic  87.4 us (7%)
  local copies, waits for them, and re-layouts  39.3 us (3%)
  starting transfers between devices  20.4 us (2%)
  between operations  19.3 us (2%)
    pallas_call x21, Pallas kernels, kernel_call(): pl.pallas_call(whole, grid_spec=pltpu.PrefetchScalarGridSpec(num_scalar_p...  261 us
    pallas_call x2, Pallas kernels, attend_back(): pl.pallas_call(partial(attend_back_kernel, bq=block, bk=block), grid=(pai...  107 us
    pallas_call x1, Pallas kernels, unproject(): pl.pallas_call(unproject_kernel, grid=(4, 2), in_specs=[line] * 6 + [stil...  97.5 us
    pallas_call x1, Pallas kernels, normed_exchange(): pl.pallas_call(normed_kernel, in_specs=[ANYWHERE] * 5, out_specs=[ANYWHER...  94.2 us
    pallas_call x1, Pallas kernels, ffn_second(): pl.pallas_call(partial(ffn_second_kernel, hidden_width=hidden_width), gri...  71.7 us
    pallas_call x1, Pallas kernels, ffn_up(): pl.pallas_call(ffn_up_kernel, grid=(4, 2 * count), in_specs=[ANYWHERE] +...  70.8 us
    ppermute x30, waiting for transfers between devices, flip(): lax.ppermute(value, axis, [(i, i ^ mask) for i in range(lax.axis_size(axi...  69.6 us
    pallas_call x1, Pallas kernels, close(): pl.pallas_call(partial(close_kernel, groups=[len(group) - 3 for group in...  56.7 us
  transfers between devices with their start and end apart: 41, of which 19 were waited for; matrix products, arithmetic and copies ran while one was open for 5% of the time, Pallas kernels for 52%

profile of v5, /device:TPU:0, one launch (start us, length us, event | category | flops | bytes accessed | tf_op | source)
XLA Modules:
  0.0 1234.6 jit_solution(17107261699997286827)
XLA Ops:
  23.3 51.2 %shard_map.363 = (bf16[256,2048]{1,0:T(8,128)(2,1)}, bf16[3,512,256]{2,1,0:T(8,128)(2,1)}, bf16[3,512,256]{2,1,0:T(8,128)(2,1)}, bf16[3,512,256]{2,1,0:T(8,128)(2,1)}) custom-call(bf16[256,2048]{1,0:T(8,128)(2,1)} %get-tuple-element.292.text, bf16[3,512,256]{2,1,0:T(8,128)(2,1)} %convert_element_type.175.head.refs_2_.refs_6_), custom_call_target="tpu_custom_call" | custom-call | bytes 104857600 | tf_op jit(solution)/shard_map/pallas_call | solution.py:1487
  84.4 94.2 %shard_map.365 = (bf16[512,2048]{1,0:T(8,128)(2,1)}, bf16[512,2048]{1,0:T(8,128)(2,1)}, bf16[512,2048]{1,0:T(8,128)(2,1)}, bf16[3,512,256]{2,1,0:T(8,128)(2,1)},...) custom-call(bf16[512,2048]{1,0:T(8,128)(2,1)} %fusion.5.refs_1_.normed, ...), custom_call_target="tpu_custom_call" | custom-call | bytes 104857600 | tf_op jit(solution)/shard_map/pallas_call | solution.py:1532
  213.2 15.8 %collective-permute-done.3.refs_11_ = bf16[256,2048]{1,0:T(8,128)(2,1)S(1)} collective-permute-done((bf16[256,2048]{1,0:T(8,128)(2,1)}, bf16[256,2048]{1,0:T(8,128)(2,1)S(1)}, u32[]{:S(2)}, u32[]{:S(2)}) %collective-permute-start.3) | collective-permute-done | bytes 1048608 | tf_op jit(solution)/shard_map/ppermute | solution.py:1419
  238.7 23.1 %shard_map.369 = (bf16[512,256]{1,0:T(8,128)(2,1)}, bf16[512,256]{1,0:T(8,128)(2,1)}, bf16[512,256]{1,0:T(8,128)(2,1)}, bf16[512,256]{1,0:T(8,128)(2,1)}, f32[2,2,2048]{2,1,0:T(2,128)}) custom-call(s32[3]{0:T(128)} %pad_add_fusion.refs_0_, bf16[512,256]{1,0:T(8,128)(2,1)} %get-tuple-element.120.refs_10_.refs_1_.refs_0_, ...), custom_call_target="tpu_custom_call" | custom-call | flops 12000000000 | bytes 3000000 | tf_op jit(solution)/shard_map/pallas_call | solution.py:475
  285.3 22.8 %shard_map.374 = (bf16[512,256]{1,0:T(8,128)(2,1)}, bf16[512,256]{1,0:T(8,128)(2,1)}, bf16[512,256]{1,0:T(8,128)(2,1)}, bf16[512,256]{1,0:T(8,128)(2,1)}, f32[2,2,2048]{2,1,0:T(2,128)}) custom-call(s32[3]{0:T(128)} %pad_add_fusion.refs_0_, bf16[512,256]{1,0:T(8,128)(2,1)} %get-tuple-element.140.refs_10_.refs_1_.refs_0_, ...), custom_call_target="tpu_custom_call" | custom-call | flops 12000000000 | bytes 3000000 | tf_op jit(solution)/shard_map/pallas_call | solution.py:475
  330.3 13.9 %shard_map.375 = (bf16[512,2048]{1,0:T(8,128)(2,1)}, bf16[512,2048]{1,0:T(8,128)(2,1)}, f32[512,2048]{1,0:T(8,128)}, bf16[512,2048]{1,0:T(8,128)(2,1)}, bf16[1024,512]{1,0:T(8,128)(2,1)}) custom-call(s32[3]{0:T(128)} %pad_add_fusion.refs_0_, bf16[512,256]{1,0:T(8,128)(2,1)} %get-tuple-element.135.refs_1_.refs_16_, ...), custom_call_target="tpu_custom_call", output_to_operand_aliasing={{4}: (16, {})} | custom-call | flops 1288490240 | bytes 6920601 | tf_op jit(solution)/shard_map/pallas_call | solution.py:475
  345.2 70.8 %shard_map.376 = (bf16[4,512,2048]{2,1,0:T(8,128)(2,1)}, bf16[4,512,2048]{2,1,0:T(8,128)(2,1)}, f32[4,8,512]{2,1,0:T(8,128)}, bf16[3,512,2048]{2,1,0:T(8,128)(2,1)}) custom-call(bf16[512,2048]{1,0:T(8,128)(2,1)} %get-tuple-element.160.lifted.refs_1_, bf16[2048,1024]{1,0:T(8,128)(2,1)} %all-gather.6.cloned.1.call-done._.up_own, ...), custom_call_target="tpu_custom_call" | custom-call | flops 80000000000 | bytes 104857600 | tf_op jit(solution)/shard_map/pallas_call | solution.py:1023
  416.1 38.9 %shard_map.377 = (bf16[4,512,2048]{2,1,0:T(8,128)(2,1)}, f32[4,8,512]{2,1,0:T(8,128)}) custom-call(bf16[512,2048]{1,0:T(8,128)(2,1)} %bitcast.74, bf16[512,2048]{1,0:T(8,128)(2,1)} %collective-permute-done.8.near.refs_6_, bf16[512,2048]{1,0:T(8,128)(2,1)} %collective-permute-done.9.far.refs_7_, bf16[512,2048]{1,0:T(8,128)(2,1)} %collective-permute-done.10.last.refs_8_, ...), custom_call_target="tpu_custom_call" | custom-call | flops 60000002048 | bytes 104857600 | tf_op jit(solution)/shard_map/pallas_call | solution.py:1085
  462.0 71.7 %shard_map.378 = (bf16[4,512,2048]{2,1,0:T(8,128)(2,1)}, bf16[4,512,2048]{2,1,0:T(8,128)(2,1)}, bf16[512,2048]{1,0:T(8,128)(2,1)}, bf16[512,2048]{1,0:T(8,128)(2,1)}, f32[8,2048]{1,0:T(8,128)}) custom-call(bf16[4,512,2048]{2,1,0:T(8,128)(2,1)} %get-tuple-element.162.act, bf16[4,512,2048]{2,1,0:T(8,128)(2,1)} %get-tuple-element.163.slope, ...), custom_call_target="tpu_custom_call" | custom-call | flops 80000000000 | bytes 104857600 | tf_op jit(solution)/shard_map/pallas_call | solution.py:1195
  533.8 27.3 %shard_map.385 = bf16[1,2048,2048]{2,1,0:T(8,128)(2,1)} custom-call(s32[3]{0:T(128)} %pad_add_fusion.refs_0_, bf16[4,512,2048]{2,1,0:T(8,128)(2,1)} %get-tuple-element.169.refs_1_.refs_2_.refs_3_.refs_4_, bf16[4,512,2048]{2,1,0:T(8,128)(2,1)} %get-tuple-element.169.refs_1_.refs_2_.refs_3_.refs_4_, ...), custom_call_target="tpu_custom_call" | custom-call | flops 5153960960 | bytes 12582912 | tf_op jit(solution)/shard_map/pallas_call | solution.py:475
  561.1 11.0 shard_map.382
  599.5 21.0 %shard_map.383 = (f32[512,2048]{1,0:T(8,128)}, bf16[512,2048]{1,0:T(8,128)(2,1)}, bf16[512,256]{1,0:T(8,128)(2,1)}, bf16[512,256]{1,0:T(8,128)(2,1)}, bf16[512,2...) custom-call(s32[3]{0:T(128)} %pad_add_fusion.refs_0_, ...), custom_call_target="tpu_custom_call" | custom-call | flops 1288490240 | bytes 8178892 | tf_op jit(solution)/shard_map/pallas_call | solution.py:475
  634.8 12.2 collective-permute-done.16
  657.2 54.0 %shard_map.386 = (bf16[4,512,256]{2,1,0:T(8,128)(2,1)}, bf16[4,512,256]{2,1,0:T(8,128)(2,1)}, bf16[4,512,256]{2,1,0:T(8,128)(2,1)}, bf16[1024,512]{1,0:T(8,128)(2,1)}) custom-call(bf16[512,256]{1,0:T(8,128)(2,1)} %get-tuple-element.140.refs_10_.refs_1_.refs_0_, bf16[512,256]{1,0:T(8,128)(2,1)} %get-tuple-element.141.refs_2_.refs_1_, ...), custom_call_target="tpu_custom_call" | custom-call | flops 40000000000 | bytes 20971520 | tf_op jit(solution)/shard_map/pallas_call | solution.py:734
  711.2 11.8 shard_map.388.refs_3_
  746.4 24.6 %shard_map.387 = bf16[1,2048,2048]{2,1,0:T(8,128)(2,1)} custom-call(s32[3]{0:T(128)} %pad_add_fusion.refs_0_, bf16[512,2048]{1,0:T(8,128)(2,1)} %get-tuple-element.160.lifted.refs_1_, bf16[3,512,2048]{2,1,0:T(8,128)(2,1)} %get-tuple-element.190.refs_2_.refs_3_.refs_4_, bf16[3,512,2048]{2,1,0:T(8,128)(2,1)} %get-tuple-element.190.refs_2_.refs_3_.refs_4_, ...), custom_call_target="tpu_custom_call" | custom-call | flops 5153960960 | bytes 12582912 | tf_op jit(solution)/shard_map/pallas_call | solution.py:475
  774.9 24.2 %reduce-scatter.12.cloned.1.call-done = bf16[512,1024]{1,0:T(8,128)(2,1)} async-done(((bf16[2048,1024]{1,0:T(8,128)(2,1)}), bf16[512,1024]{1,0:T(8,128)(2,1)}) %reduce-scatter.12.cloned.1.call-update) | async-done | bytes 1048592 | tf_op jit(solution)/shard_map/reduce_scatter | solution.py:1852
  799.2 53.5 %shard_map.384 = (bf16[4,512,256]{2,1,0:T(8,128)(2,1)}, bf16[4,512,256]{2,1,0:T(8,128)(2,1)}, bf16[4,512,256]{2,1,0:T(8,128)(2,1)}, bf16[256,2048]{1,0:T(8,128)(2,1)}) custom-call(bf16[512,256]{1,0:T(8,128)(2,1)} %get-tuple-element.120.refs_10_.refs_1_.refs_0_, bf16[512,256]{1,0:T(8,128)(2,1)} %get-tuple-element.122.refs_2_.refs_1_, ...), custom_call_target="tpu_custom_call" | custom-call | flops 40000000000 | bytes 20971520 | tf_op jit(solution)/shard_map/pallas_call | solution.py:734
  852.7 11.9 shard_map.389.refs_13_
  865.5 23.1 %reduce-scatter.8.cloned.1.call-done = bf16[1,512,2048]{2,1,0:T(8,128)(2,1)} async-done(((bf16[1,2048,2048]{2,1,0:T(8,128)(2,1)}), bf16[1,512,2048]{2,1,0:T(8,128)(2,1)}) %reduce-scatter.8.cloned.1.call-update) | async-done | bytes 2097168 | tf_op jit(solution)/shard_map/reduce_scatter | solution.py:1814
  891.6 44.8 %reduce-scatter.10.cloned.1.call-done.refs_12_ = bf16[3,512,256]{2,1,0:T(8,128)(2,1)} async-done(((bf16[3,2048,256]{2,1,0:T(8,128)(2,1)}), bf16[3,512,256]{2,1,0:T(8,128)(2,1)}) %reduce-scatter.10.cloned.1.call-update) | async-done | bytes 786448 | tf_op jit(solution)/shard_map/reduce_scatter | solution.py:1845
  936.4 54.2 %all-reduce.2.cloned.1.call-done.refs_14_.refs_0_ = bf16[512,1024]{1,0:T(8,128)(2,1)} async-done(((bf16[512,1024]{1,0:T(8,128)(2,1)}), bf16[512,1024]{1,0:T(8,128)(2,1)}) %all-reduce.2.cloned.1.call-update) | async-done | bytes 1048592 | tf_op jit(solution)/shard_map/psum | solution.py:1855
  990.6 97.5 %shard_map.391 = (bf16[512,2048]{1,0:T(8,128)(2,1)}, bf16[512,2048]{1,0:T(8,128)(2,1)}, bf16[512,1024]{1,0:T(8,128)(2,1)}, bf16[3,512,256]{2,1,0:T(8,128)(2,1)}) custom-call(bf16[4,512,256]{2,1,0:T(8,128)(2,1)} %get-tuple-element.179.refs_5_.refs_6_.refs_7_.refs_8_.refs_0_, ...), custom_call_target="tpu_custom_call" | custom-call | flops 40000000000 | bytes 20971520 | tf_op jit(solution)/shard_map/pallas_call | solution.py:1325
  1088.1 56.7 %shard_map.392 = (f32[512,1024]{1,0:T(8,128)}, f32[512,1024]{1,0:T(8,128)}, f32[1024,512]{1,0:T(8,128)}, f32[1024,512]{1,0:T(8,128)}, f32[512,2048]{1,0:T(8,128)...) custom-call(bf16[512,2048]{1,0:T(8,128)(2,1)} %get-tuple-element.194.refs_0_, ...), custom_call_target="tpu_custom_call" | custom-call | flops 1000000000 | bytes 104857600 | tf_op jit(solution)/shard_map/pallas_call | solution.py:1631
  (292 shorter events, 285.1 us)
Async XLA Ops:
  7.2 77.2 %all-gather.6.cloned.1.call-start = ((), (), s32[]{:S(2)}) async-start(), calls=%async_computation.5 | async-start | bytes 5242880 | tf_op jit(solution)/shard_map/all_gather | solution.py:1706
  10.2 218.8 %all-gather.12.cloned.1.call-start = ((), (), s32[]{:S(2)}) async-start(), calls=%async_computation.8 | async-start | bytes 5242880 | tf_op jit(solution)/shard_map/all_gather | solution.py:1710
  12.9 216.1 %all-gather.8.cloned.1.call-start = ((), (), s32[]{:S(2)}) async-start(), calls=%async_computation.6 | async-start | bytes 3932160 | tf_op jit(solution)/shard_map/all_gather | solution.py:1760
  178.6 166.5 %all-gather.10.cloned.1.call-start = ((), (), s32[]{:S(2)}) async-start(), calls=%async_computation.7 | async-start | bytes 5242880 | tf_op jit(solution)/shard_map/all_gather | solution.py:1761
  179.2 236.8 %all-gather.14.cloned.1.call-start = ((), (), s32[]{:S(2)}) async-start(), calls=%async_computation.9 | async-start | bytes 5242880 | tf_op jit(solution)/shard_map/all_gather | solution.py:1786
  181.0 48.0 %collective-permute-start.3 = (bf16[256,2048]{1,0:T(8,128)(2,1)}, bf16[256,2048]{1,0:T(8,128)(2,1)S(1)}, u32[]{:S(2)}, u32[]{:S(2)}) collective-permute-start(bf16[256,2048]{1,0:T(8,128)(2,1)} %get-tuple-element.288), channel_id=1, source_target_pairs={{0,4},{1,5},{2,6},{3,7},{4,0},{5,1},{6,2},{7,3},{8,12},{9,13},{10,... | collective-permute-start | bytes 3145736 | tf_op jit(solution)/shard_map/ppermute | solution.py:1419
  238.6 105.7 %collective-permute-start.9 = (bf16[512,2048]{1,0:T(8,128)(2,1)S(1)}, bf16[512,2048]{1,0:T(8,128)(2,1)}, u32[]{:S(2)}, u32[]{:S(2)}) collective-permute-start(bf16[512,2048]{1,0:T(8,128)(2,1)S(1)} %bitcast.72), channel_id=1, source_target_pairs={{0,2},{1,3},{2,0},{3,1},{4,6},{5,7},{6,4},{7,5},{8,10},{9,11},{10,... | collective-permute-start | bytes 6291464 | tf_op jit(solution)/shard_map/ppermute | solution.py:1419
  261.8 46.3 %collective-permute-start = (bf16[512,256]{1,0:T(8,128)(2,1)}, bf16[512,256]{1,0:T(8,128)(2,1)S(1)}, u32[]{:S(2)}, u32[]{:S(2)}) collective-permute-start(bf16[512,256]{1,0:T(8,128)(2,1)} %get-tuple-element.136.refs_17_), channel_id=1, source_target_pairs={{0,1},{1,0},{2,3},{3,2},{4,5},{5,4},{6,7},{7,6},{8,9},{9,8},{10,11... | collective-permute-start | bytes 786440 | tf_op jit(solution)/shard_map/ppermute | solution.py:1419
  261.8 53.5 %collective-permute-start.1 = (bf16[512,256]{1,0:T(8,128)(2,1)}, bf16[512,256]{1,0:T(8,128)(2,1)}, u32[]{:S(2)}, u32[]{:S(2)}) collective-permute-start(bf16[512,256]{1,0:T(8,128)(2,1)} %get-tuple-element.137.refs_18_), channel_id=1, source_target_pairs={{0,2},{1,3},{2,0},{3,1},{4,6},{5,7},{6,4},{7,5},{8,10},{9,11},{10,... | collective-permute-start | bytes 786440 | tf_op jit(solution)/shard_map/ppermute | solution.py:1419
  263.7 55.3 %collective-permute-start.2 = (bf16[512,256]{1,0:T(8,128)(2,1)}, bf16[512,256]{1,0:T(8,128)(2,1)}, u32[]{:S(2)}, u32[]{:S(2)}) collective-permute-start(bf16[512,256]{1,0:T(8,128)(2,1)} %get-tuple-element.138.refs_19_), channel_id=1, source_target_pairs={{0,3},{1,2},{2,1},{3,0},{4,7},{5,6},{6,5},{7,4},{8,11},{9,10},{10,... | collective-permute-start | bytes 786440 | tf_op jit(solution)/shard_map/ppermute | solution.py:1419
  263.8 66.5 %collective-permute-start.7 = (bf16[1024,512]{1,0:T(8,128)(2,1)S(1)}, bf16[1024,512]{1,0:T(8,128)(2,1)}, u32[]{:S(2)}, u32[]{:S(2)}) collective-permute-start(bf16[1024,512]{1,0:T(8,128)(2,1)S(1)} %copy-done.14), channel_id=1, source_target_pairs={{0,4},{1,5},{2,6},{3,7},{4,0},{5,1},{6,2},{7,3},{8,12},{9,13},{10,... | collective-permute-start | bytes 3145736 | tf_op jit(solution)/shard_map/ppermute | solution.py:1419
  319.7 96.3 %collective-permute-start.8 = (bf16[512,2048]{1,0:T(8,128)(2,1)S(1)}, bf16[512,2048]{1,0:T(8,128)(2,1)}, u32[]{:S(2)}, u32[]{:S(2)}) collective-permute-start(bf16[512,2048]{1,0:T(8,128)(2,1)S(1)} %bitcast.73), channel_id=1, source_target_pairs={{0,1},{1,0},{2,3},{3,2},{4,5},{5,4},{6,7},{7,6},{8,9},{9,8},{10,11... | collective-permute-start | bytes 6291464 | tf_op jit(solution)/shard_map/ppermute | solution.py:1419
  344.3 308.9 %reduce-scatter.6.cloned.1.call-start = ((), (), s32[]{:S(2)}) async-start(), calls=%async_computation.10 | async-start | bytes 10485760 | tf_op jit(solution)/shard_map/reduce_scatter | solution.py:1806
  344.3 71.7 %collective-permute-start.10 = (bf16[512,2048]{1,0:T(8,128)(2,1)}, bf16[512,2048]{1,0:T(8,128)(2,1)}, u32[]{:S(2)}, u32[]{:S(2)}) collective-permute-start(bf16[512,2048]{1,0:T(8,128)(2,1)} %collective-permute-done.9.far.refs_7_), channel_id=1, source_target_pairs={{0,1},{1,0},{2,3},{3,2},{4,5},{5,4},{6,7},{7,6},{8,9},{9,8},{10,11... | collective-permute-start | bytes 6291464 | tf_op jit(solution)/shard_map/ppermute | solution.py:1419
  561.1 238.0 %reduce-scatter.12.cloned.1.call-start = ((), (), s32[]{:S(2)}) async-start(), calls=%async_computation.13 | async-start | bytes 5242880 | tf_op jit(solution)/shard_map/reduce_scatter | solution.py:1852
  583.1 50.4 %collective-permute-start.14 = (bf16[512,2048]{1,0:T(8,128)(2,1)}, bf16[512,2048]{1,0:T(8,128)(2,1)S(1)}, u32[]{:S(2)}, u32[]{:S(2)}) collective-permute-start(bf16[512,2048]{1,0:T(8,128)(2,1)} %shard_map.380), channel_id=1, source_target_pairs={{0,1},{1,0},{2,3},{3,2},{4,5},{5,4},{6,7},{7,6},{8,9},{9,8},{10,11... | collective-permute-start | bytes 6291464 | tf_op jit(solution)/shard_map/ppermute | solution.py:1419
  598.2 48.8 %collective-permute-start.16 = (bf16[512,2048]{1,0:T(8,128)(2,1)}, bf16[512,2048]{1,0:T(8,128)(2,1)}, u32[]{:S(2)}, u32[]{:S(2)}) collective-permute-start(bf16[512,2048]{1,0:T(8,128)(2,1)} %add_convert_fusion.1), channel_id=1, source_target_pairs={{0,2},{1,3},{2,0},{3,1},{4,6},{5,7},{6,4},{7,5},{8,10},{9,11},{10,... | collective-permute-start | bytes 6291464 | tf_op jit(solution)/shard_map/ppermute | solution.py:1419
  620.5 35.7 %collective-permute-start.20 = (bf16[512,256]{1,0:T(8,128)(2,1)}, bf16[512,256]{1,0:T(8,128)(2,1)S(1)}, u32[]{:S(2)}, u32[]{:S(2)}) collective-permute-start(bf16[512,256]{1,0:T(8,128)(2,1)} %get-tuple-element.183), channel_id=1, source_target_pairs={{0,1},{1,0},{2,3},{3,2},{4,5},{5,4},{6,7},{7,6},{8,9},{9,8},{10,11... | collective-permute-start | bytes 786440 | tf_op jit(solution)/shard_map/ppermute | solution.py:1419
  620.6 35.6 %collective-permute-start.21 = (bf16[512,256]{1,0:T(8,128)(2,1)}, bf16[512,256]{1,0:T(8,128)(2,1)S(1)}, u32[]{:S(2)}, u32[]{:S(2)}) collective-permute-start(bf16[512,256]{1,0:T(8,128)(2,1)} %get-tuple-element.184), channel_id=1, source_target_pairs={{0,2},{1,3},{2,0},{3,1},{4,6},{5,7},{6,4},{7,5},{8,10},{9,11},{10,... | collective-permute-start | bytes 786440 | tf_op jit(solution)/shard_map/ppermute | solution.py:1419
  621.4 35.1 %collective-permute-start.22 = (bf16[512,256]{1,0:T(8,128)(2,1)}, bf16[512,256]{1,0:T(8,128)(2,1)S(1)}, u32[]{:S(2)}, u32[]{:S(2)}) collective-permute-start(bf16[512,256]{1,0:T(8,128)(2,1)} %get-tuple-element.185), channel_id=1, source_target_pairs={{0,3},{1,2},{2,1},{3,0},{4,7},{5,6},{6,5},{7,4},{8,11},{9,10},{10,... | collective-permute-start | bytes 786440 | tf_op jit(solution)/shard_map/ppermute | solution.py:1419
  746.3 142.3 %reduce-scatter.8.cloned.1.call-start = ((), (), s32[]{:S(2)}) async-start(), calls=%async_computation.11 | async-start | bytes 10485760 | tf_op jit(solution)/shard_map/reduce_scatter | solution.py:1814
  771.0 165.4 %reduce-scatter.10.cloned.1.call-start = ((), (), s32[]{:S(2)}) async-start(), calls=%async_computation.12 | async-start | bytes 3932160 | tf_op jit(solution)/shard_map/reduce_scatter | solution.py:1845
  771.7 218.9 %all-reduce.2.cloned.1.call-start = ((), (), s32[]{:S(2)}) async-start(), calls=%async_computation.14 | async-start | bytes 2097152 | tf_op jit(solution)/shard_map/psum | solution.py:1855
  799.1 348.4 %reduce-scatter.14.cloned.1.call-start = ((), (), s32[]{:S(2)}) async-start(), calls=%async_computation.15 | async-start | bytes 3932160 | tf_op jit(solution)/shard_map/reduce_scatter | solution.py:1845
  (65 other events, 810.2 us)
Sparse Core Ops, SparseCore 0:
  10.5 73.0 all-gather.5
  85.9 69.9 all-gather.11
  178.8 42.9 all-gather.7
  223.4 52.7 all-gather.9
  344.4 52.7 all-gather.13
  561.2 86.1 reduce-scatter.5
  746.4 52.6 reduce-scatter.11
  802.2 86.3 reduce-scatter.7
  892.4 43.9 reduce-scatter.9
  938.7 51.8 all-reduce.1
  994.2 43.3 reduce-scatter.13
